TPU v7x, 32 devices: a whole 2x2x4 slice. The times are simulated.
32 devices in a mesh: dp: 8 (over z, core), mp: 4 (over y, x).
Axes of the slice: x: 2, y: 2, z: 4, core: 2. Of those that a mesh axis runs over, the one named last changes fastest.
Arguments:
- out_grad: bfloat16 [4096, 4096], P(('dp', 'mp')), may hold values from -6 to 6
- gate_pre: bfloat16 [4096, 14336], P('dp', 'mp'), may hold values from -6 to 6
- up_pre: bfloat16 [4096, 14336], P('dp', 'mp'), may hold values from -6 to 6
- down_weight: bfloat16 [14336, 4096], P('mp', 'dp'), may hold values from -0.046875 to 0.046875
Outputs:
- grad_gate_pre: bfloat16 [4096, 14336], P('dp', 'mp')
- grad_up_pre: bfloat16 [4096, 14336], P('dp', 'mp')
- grad_down: bfloat16 [14336, 4096], P('mp', 'dp')
All inputs are finite; a program needn't handle non-finite values.
Results may differ from a plain program's by a relative error of at most 0.022.
Values may be sent and summed in bfloat16 or wider, within the bound.
No kernel may reach another device: no remote copies, remote signals or barrier semaphores. Data moves between devices by JAX's collectives and lax.ppermute only.
A program may use at most 128 MiB of HBM per device.

v0:
```python
import math

import jax
import jax.numpy as jnp
from jax import lax
from jax.sharding import PartitionSpec as P


def shards(out_grad, gate_pre, up_pre, down_weight):
    token_count = out_grad.shape[0] * lax.axis_size("mp") * lax.axis_size("dp")
    norm_scale = 1.0 / math.sqrt(token_count)
    full_rows = lax.all_gather(out_grad, "mp", axis=0, tiled=True)
    gate_float = gate_pre.astype(jnp.float32)
    up_float = up_pre.astype(jnp.float32)
    sigmoid_gate = jax.nn.sigmoid(gate_float)
    silu_gate = gate_float * sigmoid_gate
    hidden = (silu_gate * up_float).astype(jnp.bfloat16)
    d_hidden = lax.dot_general(
        full_rows,
        lax.all_gather(down_weight, "dp", axis=1, tiled=True),
        (((1,), (1,)), ((), ())),
        preferred_element_type=jnp.float32,
    )
    term = lax.dot_general(
        full_rows, hidden, (((0,), (0,)), ((), ())), preferred_element_type=jnp.float32
    )
    summed = lax.psum_scatter(
        lax.optimization_barrier(term.astype(jnp.bfloat16))
        .astype(jnp.float32)
        .astype(jnp.bfloat16),
        "dp",
        scatter_dimension=0,
        tiled=True,
    ).astype(jnp.float32)
    grad_down = (summed * norm_scale).astype(jnp.bfloat16).T
    grad_gate = (
        d_hidden * up_float * sigmoid_gate * (1.0 + gate_float * (1.0 - sigmoid_gate))
    ).astype(jnp.bfloat16)
    grad_up = (d_hidden * silu_gate).astype(jnp.bfloat16)
    return (grad_gate, grad_up, grad_down)


def solution(mesh):
    return jax.shard_map(
        shards,
        mesh=mesh,
        in_specs=(P(("dp", "mp"), None), P("dp", "mp"), P("dp", "mp"), P("mp", "dp")),
        out_specs=(P("dp", "mp"), P("dp", "mp"), P("mp", "dp")),
        check_vma=False,
    )
```

profile of v0, /device:TPU:0, one launch (start us, length us, event | category | flops | bytes accessed | tf_op | source)
XLA Modules:
  0.0 619.5 jit_solution(17610544887287987585)
XLA Ops:
  7.2 0.0 all-gather.3.cloned.1.call-start
  7.2 0.7 all-gather.3.cloned.1.call-update
  7.9 0.0 all-gather.5.cloned.1.call-start
  7.9 0.7 all-gather.5.cloned.1.call-update
  8.6 0.0 reduce-scatter.2.cloned.1.call-start
  8.7 56.6 %all-gather.3.cloned.1.call-done = bf16[512,4096]{1,0:T(8,128)(2,1)} async-done(((bf16[128,4096]{1,0:T(8,128)(2,1)}), bf16[512,4096]{1,0:T(8,128)(2,1)}) %all-gather.3.cloned.1.call-update) | async-done | bytes 4194320 | tf_op jit(solution)/shard_map/all_gather | solution.py:12
  65.3 22.3 %fusion = bf16[4096,3584]{0,1:T(8,128)(2,1)} fusion(bf16[512,4096]{1,0:T(8,128)(2,1)} %all-gather.3.cloned.1.call-done, bf16[512,3584]{1,0:T(8,128)(2,1)} %param.6, bf16[512,3584]{1,0:T(8,128)(2,1)} %param.5), kind=kOutput, calls=%fused_computation.1 | convolution fusion | flops 15061745664 | bytes 40894464 | tf_op jit(solution)/shard_map/dot_general | solution.py:24
  87.6 0.0 reduce-scatter.2.cloned.1.call-update
  87.6 233.5 %all-gather.5.cloned.1.call-done = bf16[3584,4096]{1,0:T(8,128)(2,1)} async-done(((bf16[3584,512]{1,0:T(8,128)(2,1)}), bf16[3584,4096]{1,0:T(8,128)(2,1)}) %all-gather.5.cloned.1.call-update) | async-done | bytes 29360144 | tf_op jit(solution)/shard_map/all_gather | solution.py:20
  321.2 26.6 %multiply_convert_fusion.1 = (bf16[512,3584]{1,0:T(8,128)(2,1)}, bf16[512,3584]{1,0:T(8,128)(2,1)}) fusion(bf16[512,3584]{1,0:T(8,128)(2,1)} %param.5, bf16[512,3584]{1,0:T(8,128)(2,1)} %param.6, bf16[512,4096]{1,0:T(8,128)(2,1)} %all-gather.3.cloned.1.call-done, bf16[3584,4096]{1,0:T(8,128)(2,1)} %all-gather.5.cloned.1.call-done), kind=kOutput, calls=%fused_computation.16 | convolution fusion | flops 15059910656 | bytes 48234496 | tf_op jit(solution)/shard_map/dot_general | solution.py:18
  347.8 260.6 %reduce-scatter.2.cloned.1.call-done = bf16[512,3584]{0,1:T(8,128)(2,1)} async-done(((bf16[4096,3584]{0,1:T(8,128)(2,1)}), bf16[512,3584]{0,1:T(8,128)(2,1)}) %reduce-scatter.2.cloned.1.call-update) | async-done | bytes 3670032 | tf_op jit(solution)/shard_map/reduce_scatter | solution.py:27
  608.4 4.6 fusion.9
Async XLA Ops:
  7.2 58.1 %all-gather.3.cloned.1.call-start = ((), (), s32[]{:S(2)}) async-start(), calls=%async_computation.1 | async-start | bytes 5242880 | tf_op jit(solution)/shard_map/all_gather | solution.py:12
  7.9 313.3 %all-gather.5.cloned.1.call-start = ((), (), s32[]{:S(2)}) async-start(), calls=%async_computation.2 | async-start | bytes 33030144 | tf_op jit(solution)/shard_map/all_gather | solution.py:20
  8.6 599.7 %reduce-scatter.2.cloned.1.call-start = ((), (), s32[]{:S(2)}) async-start(), calls=%async_computation.3 | async-start | bytes 33030144 | tf_op jit(solution)/shard_map/reduce_scatter | solution.py:27
Sparse Core Ops, SparseCore 0:
  9.8 55.3 all-gather.2
  66.9 254.2 all-gather.4
  323.5 284.8 reduce-scatter.1
where the time goes:
time: 620 us
  waiting for transfers between devices  552 us (89%)
  matrix products  48.9 us (8%)
  between operations  13.7 us (2%)
    reduce_scatter x1, waiting for transfers between devices, shards(): lax.psum_scatter(lax.optimization_barrier(term.astype(jnp.bfloat16)).asty...  261 us
    all_gather x1, waiting for transfers between devices, shards(): lax.all_gather(down_weight, 'dp', axis=1, tiled=True)  234 us
    all_gather x1, waiting for transfers between devices, shards(): full_rows = lax.all_gather(out_grad, 'mp', axis=0, tiled=True)  56.6 us
    dot_general x1, matrix products, shards(): lax.dot_general(full_rows, lax.all_gather(down_weight, 'dp', axis=1, tile...  26.6 us
    dot_general x1, matrix products, shards(): lax.dot_general(full_rows, hidden, (((0,), (0,)), ((), ())), preferred_el...  22.3 us
  transfers between devices with their start and end apart: 3, of which 3 were waited for; matrix products, arithmetic and copies ran while one was open for 8% of the time, Pallas kernels for 0%

commit v1 on v0

v1 whole, which is shorter than its diff:
```python
import functools
import math

import jax
import jax.numpy as jnp
from jax import lax
from jax.experimental import pallas as pl
from jax.experimental.pallas import tpu as pltpu
from jax.sharding import PartitionSpec as P

VMEM = 60 * 1024 * 1024
COPIES = 4
STEP_FLOPS = 2e9
F32, BF16 = jnp.float32, jnp.bfloat16
ANY = pl.BlockSpec(memory_space=pl.ANY)


def call(kernel, grid, in_specs, out_specs, out_shape, name, aliases=None, flops=0, scratch=()):
    return pl.pallas_call(
        kernel,
        grid_spec=pltpu.PrefetchScalarGridSpec(
            num_scalar_prefetch=1,
            grid=grid,
            in_specs=in_specs,
            out_specs=out_specs,
            scratch_shapes=scratch,
        ),
        out_shape=out_shape,
        input_output_aliases=aliases or {},
        compiler_params=pltpu.CompilerParams(
            vmem_limit_bytes=VMEM, dimension_semantics=("arbitrary",) * len(grid)
        ),
        cost_estimate=pl.CostEstimate(flops=int(flops), bytes_accessed=0, transcendentals=0),
        name=name,
    )


def column_tile(chunk, most=896):
    return max(t for t in range(128, most + 1, 128) if chunk % t == 0)


def dot(a, b, contract):
    return lax.dot_general(a, b, (contract, ((), ())), preferred_element_type=F32)


def half_kernel(flip, place, weight_ref, *rest):
    out_ref, held, load_sem, store_sem = rest[-4:]
    half = out_ref.shape[0]
    part = half // COPIES
    start = (place[1] ^ flip) * half

    def load(i):
        source = pl.multiple_of(start + i * part, part)
        here = pl.ds(i * part, part)
        return pltpu.make_async_copy(
            weight_ref.at[pl.ds(source, part), :], held.at[here, :], load_sem.at[i]
        )

    def store(i):
        here = pl.ds(i * part, part)
        return pltpu.make_async_copy(held.at[here, :], out_ref.at[here, :], store_sem.at[i])

    for i in range(COPIES):
        load(i).start()
    for i in range(COPIES):
        load(i).wait()
        store(i).start()
    for i in range(COPIES):
        store(i).wait()


def half_call(place, weight, flip, after):
    units, block = weight.shape
    half = units // 2
    return call(
        functools.partial(half_kernel, flip),
        (1,),
        [ANY] * (1 + len(after)),
        ANY,
        jax.ShapeDtypeStruct((half, block), BF16),
        "half",
        scratch=[
            pltpu.VMEM((half, block), BF16),
            pltpu.SemaphoreType.DMA((COPIES,)),
            pltpu.SemaphoreType.DMA((COPIES,)),
        ],
    )(place, weight, *after)


def hidden_kernel(place, gate_own, up_own, gate_sib, up_sib, out_ref):
    tokens = gate_own.shape[0]
    core = place[1]
    for at, gate_ref, up_ref in ((core, gate_own, up_own), (1 - core, gate_sib, up_sib)):
        gate = gate_ref[...].astype(F32)
        up = up_ref[...].astype(F32)
        hidden = gate * jax.nn.sigmoid(gate) * up
        start = pl.multiple_of(at * tokens, tokens)
        out_ref[:, pl.ds(start, tokens)] = hidden.T.astype(BF16)


def hidden_call(place, *arrays):
    tokens, units = arrays[0].shape
    tile = column_tile(units, 256)
    return call(
        hidden_kernel,
        (units // tile,),
        [pl.BlockSpec((tokens, tile), lambda i, s: (0, i))] * 4,
        pl.BlockSpec((tile, 2 * tokens), lambda i, s: (i, 0)),
        jax.ShapeDtypeStruct((units, 2 * tokens), BF16),
        "hidden",
    )(place, *arrays)


def along(place, flow, line):
    return jnp.where(place[1] == flow, place[0], line - 1 - place[0])


def term_specs(tile, tokens, block, first, ahead, line):
    def column(i, s):
        return 0, 2 * lax.rem(s[0] + ahead(s), line) + s[1]

    return [
        pl.BlockSpec((tile, tokens), lambda i, s: (first + i, 0)),
        pl.BlockSpec((tokens, block), column),
    ]


def step_kernel(flow, j, line, place, got_ref, hidden_ref, grad_ref, out_ref):
    at = along(place, flow, line)
    adds = at + j < line

    @pl.when(adds)
    def _():
        term = dot(hidden_ref[...], grad_ref[...], ((1,), (0,)))
        before = jnp.where(at > 0, got_ref[...].astype(F32), 0.0)
        out_ref[...] = (before + term).astype(BF16)

    @pl.when(jnp.logical_not(adds))
    def _():
        out_ref[...] = got_ref[...]


def step_call(place, got, hidden, grads, k, j, flow, line):
    chunk, block = got.shape
    tokens = hidden.shape[1]
    steps = 4
    tile = chunk // steps

    def ahead(s):
        return jnp.where(s[1] == flow, j, line - j)

    return call(
        functools.partial(step_kernel, flow, j, line),
        (steps,),
        [pl.BlockSpec((tile, block), lambda i, s: (i, 0))]
        + term_specs(tile, tokens, block, k * steps, ahead, line),
        pl.BlockSpec((tile, block), lambda i, s: (i, 0)),
        jax.ShapeDtypeStruct((chunk, block), BF16),
        "step",
        flops=STEP_FLOPS,
    )(place, got, hidden, grads)


def own_kernel(place, hidden_ref, grad_ref, *rest):
    rest[-1][...] = dot(hidden_ref[...], grad_ref[...], ((1,), (0,))).astype(BF16)


def own_call(place, hidden, grads, block, line, after):
    units, tokens = hidden.shape
    steps = 8
    tile = units // steps
    return call(
        own_kernel,
        (steps,),
        term_specs(tile, tokens, block, 0, lambda s: 0, line) + [ANY] * len(after),
        pl.BlockSpec((tile, block), lambda i, s: (i, 0)),
        jax.ShapeDtypeStruct((units, block), BF16),
        "own",
    )(place, hidden, grads, *after)


def final_kernel(scale, line, place, one_ref, two_ref, own_ref, *rest):
    at = along(place, 0, line)
    one = jnp.where(at > 0, one_ref[...].astype(F32), 0.0)
    two = jnp.where(at < line - 1, two_ref[...].astype(F32), 0.0)
    out_ref, token = rest[-2:]
    out_ref[...] = ((one + two + own_ref[...].astype(F32)) * scale).astype(BF16)
    token[...] = jnp.zeros_like(token)


def final_call(place, one, two, own, k, line, scale, before, after):
    chunk, block = one.shape
    steps = 4
    tile = chunk // steps
    got = pl.BlockSpec((tile, block), lambda i, s: (i, 0))
    here = pl.BlockSpec((tile, block), lambda i, s: (k * steps + i, 0))
    return call(
        functools.partial(final_kernel, scale, line),
        (steps,),
        [got, got, here] + [ANY] * len(before + after),
        [here, pl.BlockSpec((8, 128), lambda i, s: (0, 0))],
        [jax.ShapeDtypeStruct(own.shape, BF16), jax.ShapeDtypeStruct((8, 128), F32)],
        "final",
        {4: 0} if before else None,
    )(place, one, two, own, *before, *after)


def half_product(line, place, grads, weights):
    count = len(weights) // 2
    at = along(place, 0, line)
    d_hidden = None
    for chain in range(2):
        for slot in range(line):
            weight = weights[chain * count + max(0, 2 * slot - 1)][...]
            if slot:
                weight = jnp.where(at >= slot, weight, weights[chain * count + 2 * slot][...])
            part = dot(grads[chain * line + slot][...], weight, ((1,), (1,)))
            d_hidden = part if d_hidden is None else d_hidden + part
    return d_hidden


def store_grads(d_hidden, gate_ref, up_ref, gate_out, up_out):
    gate = gate_ref[...].astype(F32)
    up = up_ref[...].astype(F32)
    sig = jax.nn.sigmoid(gate)
    gate_out[...] = (d_hidden * up * sig * (1.0 + gate * (1.0 - sig))).astype(BF16)
    up_out[...] = (d_hidden * (gate * sig)).astype(BF16)


def product_kernel(line, count, place, *refs):
    d_hidden = half_product(line, place, refs[: 2 * line], refs[2 * line : 2 * line + count])
    out_ref, token = refs[-2:]
    out_ref[...] = d_hidden.astype(BF16)
    token[...] = jnp.zeros_like(token)


def grads_kernel(line, count, place, *refs):
    d_hidden = half_product(line, place, refs[: 2 * line], refs[2 * line : 2 * line + count])
    gate_ref, up_ref = refs[2 * line + count : 2 * line + count + 2]
    gate_out, up_out, token = refs[-3:]
    store_grads(d_hidden, gate_ref, up_ref, gate_out, up_out)
    token[...] = jnp.zeros_like(token)


def product_call(place, grads, weights, gate_up, flip, line, after):
    half, block = weights[0].shape
    tokens = grads.shape[0] // 2
    tile = column_tile(half, 512)
    steps = half // tile
    here = pl.BlockSpec((tokens, tile), lambda i, s: (0, s[1] * steps + i))

    def row_spec(chain, slot):
        def block_of(i, s):
            source = lax.rem(s[0] + jnp.where(s[1] == 0, line - slot, slot), line)
            return s[1] ^ flip, 2 * source + (s[1] ^ chain)

        return pl.BlockSpec((tokens, block), block_of)

    def weight_spec(index):
        index = index % (2 * line - 1)
        slot, flow = (index + 1) // 2, (index + 1) % 2

        def block_of(i, s):
            if index == 0:
                return i, 0
            return jnp.where((along(s, 0, line) >= slot) == (flow == 0), i, 0), 0

        return pl.BlockSpec((tile, block), block_of)

    if gate_up:
        kernel, outs = grads_kernel, [here, here]
        shapes = [jax.ShapeDtypeStruct(gate_up[0].shape, BF16)] * 2
    else:
        kernel, outs = product_kernel, [pl.BlockSpec((tokens, tile), lambda i, s: (0, i))]
        shapes = [jax.ShapeDtypeStruct((tokens, half), BF16)]
    return call(
        functools.partial(kernel, line, len(weights)),
        (steps,),
        [row_spec(chain, slot) for chain in range(2) for slot in range(line)]
        + [weight_spec(index) for index in range(len(weights))]
        + [here] * len(gate_up)
        + [ANY] * len(after),
        outs + [pl.BlockSpec((8, 128), lambda i, s: (0, 0))],
        shapes + [jax.ShapeDtypeStruct((8, 128), F32)],
        "grads" if gate_up else "product",
    )(place, *[grads] * (2 * line), *weights, *gate_up, *after)


def join_kernel(place, product_ref, gate_ref, up_ref, *rest):
    gate_out, up_out = rest[-2:]
    store_grads(product_ref[...].astype(F32), gate_ref, up_ref, gate_out, up_out)


def join_call(place, product, gate, up, gate_all, up_all, after):
    tokens, half = product.shape
    tile = column_tile(half, 512)
    steps = half // tile
    there = pl.BlockSpec((tokens, tile), lambda i, s: (0, (1 - s[1]) * steps + i))
    return call(
        join_kernel,
        (steps,),
        [pl.BlockSpec((tokens, tile), lambda i, s: (0, i)), there, there, ANY, ANY]
        + [ANY] * len(after),
        [there, there],
        [jax.ShapeDtypeStruct(gate_all.shape, BF16)] * 2,
        "join",
        {4: 0, 5: 1},
    )(place, product, gate, up, gate_all, up_all, *after)


def shards(out_grad, gate_pre, up_pre, down_weight):
    n_dp, n_mp = lax.axis_size("dp"), lax.axis_size("mp")
    line = n_dp // 2
    rows, width = out_grad.shape
    tokens, units = gate_pre.shape
    block = down_weight.shape[1]
    scale = 1.0 / math.sqrt(rows * n_mp * n_dp)

    index = lax.axis_index("dp")
    place = jnp.stack([index // 2, index % 2]).astype(jnp.int32)
    swap_pairs = [(i, i ^ 1) for i in range(n_dp)]

    rings = []
    for flow in range(2):
        ring = [2 * z + flow for z in range(line)] + [2 * z + 1 - flow for z in reversed(range(line))]
        rings.append([(ring[i], ring[(i + 1) % n_dp]) for i in range(n_dp)])

    def swap(x):
        return lax.ppermute(x, "dp", swap_pairs)

    def send(x, flow):
        return lax.ppermute(x, "dp", rings[flow])

    half_own = half_call(place, down_weight, 0, ())
    first = [half_own, swap(half_call(place, down_weight, 1, (half_own,)))]
    got = [[[send(x, flow) for x in first]] for flow in range(2)]

    groups = [
        [(2 * z + c) * n_mp + m for c in range(2) for m in range(n_mp)] for z in range(line)
    ]
    out_grads = lax.all_gather(
        out_grad, ("dp", "mp"), axis=0, tiled=True, axis_index_groups=groups
    )
    gate_sib, up_sib = swap(gate_pre), swap(up_pre)
    hidden = hidden_call(place, gate_pre, up_pre, gate_sib, up_sib)

    sent = []
    for slot in range(2, line + 1):
        sent = [
            [
                step_call(place, got[flow][-1][k], hidden, out_grads, k, line + 1 - slot, flow, line)
                for k in range(2)
            ]
            for flow in range(2)
        ]
        for flow in range(2):
            got[flow].append([send(x, flow) for x in sent[flow]])
    sent = sent[0] + sent[1]
    own = own_call(place, hidden, out_grads, block, line, sent)

    weights = []
    for k in range(2):
        weights.append(first[k])
        for slot in range(1, line):
            weights += [got[0][slot - 1][k], got[1][line - slot - 1][k]]
    product, token = product_call(place, out_grads, weights, (), 1, line, sent)
    from_sib = swap(product)
    own_half = (gate_pre, up_pre)
    *grads, token = product_call(place, out_grads, weights, own_half, 0, line, [token])

    last = [got[flow][-1] for flow in range(2)]
    grad_down, token = final_call(place, last[0][0], last[1][0], own, 0, line, scale, (), (token,))
    grads = join_call(place, from_sib, gate_pre, up_pre, *grads, [token])
    grad_down, _ = final_call(
        place, last[0][1], last[1][1], own, 1, line, scale, (grad_down,), tuple(grads)
    )
    return (*grads, grad_down)


def solution(mesh):
    return jax.shard_map(
        shards,
        mesh=mesh,
        in_specs=(P(("dp", "mp"), None), P("dp", "mp"), P("dp", "mp"), P("mp", "dp")),
        out_specs=(P("dp", "mp"), P("dp", "mp"), P("mp", "dp")),
        check_vma=False,
    )
```

time: 620 us -> 349 us (0.56)
  waiting for transfers between devices: 552 us -> 153 us
  Pallas kernels: 0 us -> 155 us
  matrix products: 48.9 us -> 0 us
  starting transfers between devices: 0.11 us -> 18.5 us
    all_gather x2 -> x1, waiting for transfers between devices: 290 us -> 8.32 us  [shards(): lax.all_gather(out_grad, ('dp', 'mp'), axis=0, tiled=True, axis_index_gro...]
    reduce_scatter x1 -> x0, waiting for transfers between devices: 261 us -> none  [shards(): lax.psum_scatter(lax.optimization_barrier(term.astype(jnp.bfloat16)).asty...]
    pallas_call x0 -> x21, Pallas kernels: none -> 155 us  [the longest x12 72.1 us: step_call(): call(functools.partial(step_kernel, flow, j, line), (steps,), [pl.BlockSp...]
    ppermute x0 -> x20, waiting for transfers between devices: none -> 144 us  [the longest x16 137 us: send(): return lax.ppermute(x, 'dp', rings[flow])]
    dot_general x2 -> x0, matrix products: 48.9 us -> none  [the longest x1 26.6 us: shards(): lax.dot_general(full_rows, lax.all_gather(down_weight, 'dp', axis=1, tile...]
    ppermute x0 -> x20, starting transfers between devices: none -> 18.4 us  [the longest x16 17.3 us: send(): return lax.ppermute(x, 'dp', rings[flow])]
  transfers between devices with their start and end apart: 3 -> 21, of which waited for: 3 -> 9; matrix products, arithmetic and copies ran while one was open for 8% -> 0% of each run, Pallas kernels for 0% -> 43%
where the time goes in v1:
time: 349 us; the launch traced here: 347 us
  Pallas kernels  155 us (44%)
  waiting for transfers between devices  153 us (44%)
  starting transfers between devices  18.5 us (5%)
  between operations  14.1 us (4%)
  local copies, waits for them, and re-layouts  4.92 us (1%)
    ppermute x16, waiting for transfers between devices, send(): return lax.ppermute(x, 'dp', rings[flow])  137 us
    pallas_call x12, Pallas kernels, step_call(): call(functools.partial(step_kernel, flow, j, line), (steps,), [pl.BlockSp...  72.1 us
    pallas_call x2, Pallas kernels, product_call(): call(functools.partial(kernel, line, len(weights)), (steps,), [row_spec(c...  33.6 us
    ppermute x16, starting transfers between devices, send(): return lax.ppermute(x, 'dp', rings[flow])  17.3 us
    pallas_call x1, Pallas kernels, hidden_call(): call(hidden_kernel, (units // tile,), [pl.BlockSpec((tokens, tile), lambd...  14.6 us
    pallas_call x2, Pallas kernels, final_call(): call(functools.partial(final_kernel, scale, line), (steps,), [got, got, h...  10.8 us
    pallas_call x1, Pallas kernels, own_call(): call(own_kernel, (steps,), term_specs(tile, tokens, block, 0, lambda s: 0...  10.5 us
    all_gather x1, waiting for transfers between devices, shards(): lax.all_gather(out_grad, ('dp', 'mp'), axis=0, tiled=True, axis_index_gro...  8.32 us
  transfers between devices with their start and end apart: 21, of which 9 were waited for; matrix products, arithmetic and copies ran while one was open for 0% of the time, Pallas kernels for 43%

profile of v1, /device:TPU:0, one launch (start us, length us, event | category | flops | bytes accessed | tf_op | source)
XLA Modules:
  0.0 346.6 jit_solution(11274271254122970331)
XLA Ops:
  7.2 0.0 all-gather.2.cloned.1.call-start
  7.2 0.7 all-gather.2.cloned.1.call-update
  7.9 0.5 collective-permute-start.2
  8.4 0.1 collective-permute-start.3
  8.5 0.6 pad_add_fusion.place
  9.1 3.0 half.2.rest_0_.refs_8_
  12.1 0.0 copy-start
  12.1 3.1 half.3
  15.2 0.5 collective-permute-start.8
  15.7 2.7 collective-permute-start
  18.4 0.0 collective-permute-start.1
  18.4 6.9 %collective-permute-done.8.refs_15_ = bf16[1792,512]{1,0:T(8,128)(2,1)} collective-permute-done((bf16[1792,512]{1,0:T(8,128)(2,1)}, bf16[1792,512]{1,0:T(8,128)(2,1)}, u32[]{:S(2)}, u32[]{:S(2)}) %collective-permute-start.8) | collective-permute-done | bytes 1835040 | tf_op jit(solution)/shard_map/ppermute | solution.py:329
  25.3 0.4 collective-permute-start.10
  25.7 0.0 collective-permute-done.2.gate_sib
  25.7 1.7 collective-permute-start.9
  27.3 0.0 collective-permute-done.3.up_sib
  27.3 14.6 %hidden.1.hidden_ref = bf16[3584,1024]{1,0:T(8,128)(2,1)} custom-call(s32[2]{0:T(128)} %pad_add_fusion.place, bf16[512,3584]{1,0:T(8,128)(2,1)} %gate_ref.1, bf16[512,3584]{1,0:T(8,128)(2,1)} %up_ref.1, bf16[512,3584]{1,0:T(8,128)(2,1)} %collective-permute-done.2.gate_sib, bf16[512,3584]{1,0:T(8,128)(2,1)} %collective-permute-done.3.up_sib), custom_call_target="tpu_custom_call" | custom-call | tf_op jit(solution)/shard_map/hidden/pallas_call | solution.py:104
  41.9 16.7 %collective-permute-done.got_ref.refs_9_ = bf16[1792,512]{1,0:T(8,128)(2,1)} collective-permute-done((bf16[1792,512]{1,0:T(8,128)(2,1)S(1)}, bf16[1792,512]{1,0:T(8,128)(2,1)}, u32[]{:S(2)}, u32[]{:S(2)}) %collective-permute-start) | collective-permute-done | bytes 1835040 | tf_op jit(solution)/shard_map/ppermute | solution.py:332
  58.7 8.3 %all-gather.2.cloned.1.call-done.grad_ref.refs_0_.refs_1_.refs_2_.refs_3_.refs_4_.refs_5_.refs_6_.refs_7_ = bf16[1024,4096]{1,0:T(8,128)(2,1)} async-done(((bf16[128,4096]{1,0:T(8,128)(2,1)}), bf16[1024,4096]{1,0:T(8,128)(2,1)}) %all-gather.2.cloned.1.call-update) | async-done | bytes 8388624 | tf_op jit(solution)/shard_map/all_gather | solution.py:341
  67.0 6.7 %step.14 = bf16[1792,512]{1,0:T(8,128)(2,1)} custom-call(s32[2]{0:T(128)} %pad_add_fusion.place, bf16[1792,512]{1,0:T(8,128)(2,1)} %collective-permute-done.got_ref.refs_9_, bf16[3584,1024]{1,0:T(8,128)(2,1)} %hidden.1.hidden_ref, bf16[1024,4096]{1,0:T(8,128)(2,1)} %all-gather.2.cloned.1.call-done.grad_ref.refs_0_.refs_1_.refs_2_.refs_3_.refs_4_.refs_5_.refs_6_.refs_7_), custom_call_target="tpu_custom_call" | custom-call | flops 2000000000 | tf_op jit(solution)/shard_map/step/pallas_call | solution.py:152
  73.7 0.1 collective-permute-start.6
  73.8 0.0 collective-permute-done.1.got_ref.refs_14_
  73.8 5.3 %step.12 = bf16[1792,512]{1,0:T(8,128)(2,1)} custom-call(s32[2]{0:T(128)} %pad_add_fusion.place, bf16[1792,512]{1,0:T(8,128)(2,1)} %collective-permute-done.1.got_ref.refs_14_, bf16[3584,1024]{1,0:T(8,128)(2,1)} %hidden.1.hidden_ref, bf16[1024,4096]{1,0:T(8,128)(2,1)} %all-gather.2.cloned.1.call-done.grad_ref.refs_0_.refs_1_.refs_2_.refs_3_.refs_4_.refs_5_.refs_6_.refs_7_), custom_call_target="tpu_custom_call" | custom-call | flops 2000000000 | tf_op jit(solution)/shard_map/step/pallas_call | solution.py:152
  79.1 1.7 collective-permute-start.4
  80.9 19.9 %collective-permute-done.10.got_ref.refs_21_ = bf16[1792,512]{1,0:T(8,128)(2,1)} collective-permute-done((bf16[1792,512]{1,0:T(8,128)(2,1)}, bf16[1792,512]{1,0:T(8,128)(2,1)}, u32[]{:S(2)}, u32[]{:S(2)}) %collective-permute-start.10) | collective-permute-done | bytes 1835040 | tf_op jit(solution)/shard_map/ppermute | solution.py:332
  100.7 5.4 %step.16 = bf16[1792,512]{1,0:T(8,128)(2,1)} custom-call(s32[2]{0:T(128)} %pad_add_fusion.place, bf16[1792,512]{1,0:T(8,128)(2,1)} %collective-permute-done.10.got_ref.refs_21_, bf16[3584,1024]{1,0:T(8,128)(2,1)} %hidden.1.hidden_ref, bf16[1024,4096]{1,0:T(8,128)(2,1)} %all-gather.2.cloned.1.call-done.grad_ref.refs_0_.refs_1_.refs_2_.refs_3_.refs_4_.refs_5_.refs_6_.refs_7_), custom_call_target="tpu_custom_call" | custom-call | flops 2000000000 | tf_op jit(solution)/shard_map/step/pallas_call | solution.py:152
  106.1 0.0 collective-permute-start.11
  106.1 0.0 collective-permute-done.9.got_ref.refs_16_
  106.1 6.7 %step.18 = bf16[1792,512]{1,0:T(8,128)(2,1)} custom-call(s32[2]{0:T(128)} %pad_add_fusion.place, bf16[1792,512]{1,0:T(8,128)(2,1)} %collective-permute-done.9.got_ref.refs_16_, bf16[3584,1024]{1,0:T(8,128)(2,1)} %hidden.1.hidden_ref, bf16[1024,4096]{1,0:T(8,128)(2,1)} %all-gather.2.cloned.1.call-done.grad_ref.refs_0_.refs_1_.refs_2_.refs_3_.refs_4_.refs_5_.refs_6_.refs_7_), custom_call_target="tpu_custom_call" | custom-call | flops 2000000000 | tf_op jit(solution)/shard_map/step/pallas_call | solution.py:152
  112.8 0.7 collective-permute-start.13
  113.5 23.9 %collective-permute-done.6.got_ref.refs_11_ = bf16[1792,512]{1,0:T(8,128)(2,1)} collective-permute-done((bf16[1792,512]{1,0:T(8,128)(2,1)}, bf16[1792,512]{1,0:T(8,128)(2,1)}, u32[]{:S(2)}, u32[]{:S(2)}) %collective-permute-start.6) | collective-permute-done | bytes 1835040 | tf_op jit(solution)/shard_map/ppermute | solution.py:332
  137.4 6.7 %step.15 = bf16[1792,512]{1,0:T(8,128)(2,1)} custom-call(s32[2]{0:T(128)} %pad_add_fusion.place, bf16[1792,512]{1,0:T(8,128)(2,1)} %collective-permute-done.6.got_ref.refs_11_, bf16[3584,1024]{1,0:T(8,128)(2,1)} %hidden.1.hidden_ref, bf16[1024,4096]{1,0:T(8,128)(2,1)} %all-gather.2.cloned.1.call-done.grad_ref.refs_0_.refs_1_.refs_2_.refs_3_.refs_4_.refs_5_.refs_6_.refs_7_), custom_call_target="tpu_custom_call" | custom-call | flops 2000000000 | tf_op jit(solution)/shard_map/step/pallas_call | solution.py:152
  144.1 2.5 collective-permute-start.7
  146.6 0.0 collective-permute-done.4.got_ref.refs_12_
  146.6 1.2 copy-done.3
  147.8 5.3 %step.13 = bf16[1792,512]{1,0:T(8,128)(2,1)} custom-call(s32[2]{0:T(128)} %pad_add_fusion.place, bf16[1792,512]{1,0:T(8,128)(2,1)} %copy-done.3, bf16[3584,1024]{1,0:T(8,128)(2,1)} %hidden.1.hidden_ref, bf16[1024,4096]{1,0:T(8,128)(2,1)} %all-gather.2.cloned.1.call-done.grad_ref.refs_0_.refs_1_.refs_2_.refs_3_.refs_4_.refs_5_.refs_6_.refs_7_), custom_call_target="tpu_custom_call" | custom-call | flops 2000000000 | tf_op jit(solution)/shard_map/step/pallas_call | solution.py:152
  153.1 0.0 collective-permute-start.5
  153.1 26.1 %collective-permute-done.11.got_ref.refs_19_ = bf16[1792,512]{1,0:T(8,128)(2,1)S(1)} collective-permute-done((bf16[1792,512]{1,0:T(8,128)(2,1)}, bf16[1792,512]{1,0:T(8,128)(2,1)S(1)}, u32[]{:S(2)}, u32[]{:S(2)}) %collective-permute-start.11) | collective-permute-done | bytes 1835040 | tf_op jit(solution)/shard_map/ppermute | solution.py:332
  179.3 1.2 copy-done.4
  180.5 5.4 %step.17 = bf16[1792,512]{1,0:T(8,128)(2,1)} custom-call(s32[2]{0:T(128)} %pad_add_fusion.place, bf16[1792,512]{1,0:T(8,128)(2,1)} %copy-done.4, bf16[3584,1024]{1,0:T(8,128)(2,1)} %hidden.1.hidden_ref, bf16[1024,4096]{1,0:T(8,128)(2,1)} %all-gather.2.cloned.1.call-done.grad_ref.refs_0_.refs_1_.refs_2_.refs_3_.refs_4_.refs_5_.refs_6_.refs_7_), custom_call_target="tpu_custom_call" | custom-call | flops 2000000000 | tf_op jit(solution)/shard_map/step/pallas_call | solution.py:152
  185.9 0.0 collective-permute-start.12
  185.9 0.0 collective-permute-done.13.got_ref.refs_18_
  185.9 6.7 %step.19 = bf16[1792,512]{1,0:T(8,128)(2,1)} custom-call(s32[2]{0:T(128)} %pad_add_fusion.place, bf16[1792,512]{1,0:T(8,128)(2,1)} %collective-permute-done.13.got_ref.refs_18_, bf16[3584,1024]{1,0:T(8,128)(2,1)} %hidden.1.hidden_ref, bf16[1024,4096]{1,0:T(8,128)(2,1)} %all-gather.2.cloned.1.call-done.grad_ref.refs_0_.refs_1_.refs_2_.refs_3_.refs_4_.refs_5_.refs_6_.refs_7_), custom_call_target="tpu_custom_call" | custom-call | flops 2000000000 | tf_op jit(solution)/shard_map/step/pallas_call | solution.py:152
  192.6 2.0 collective-permute-start.14
  194.6 21.5 %collective-permute-done.7.got_ref.refs_13_ = bf16[1792,512]{1,0:T(8,128)(2,1)} collective-permute-done((bf16[1792,512]{1,0:T(8,128)(2,1)}, bf16[1792,512]{1,0:T(8,128)(2,1)}, u32[]{:S(2)}, u32[]{:S(2)}) %collective-permute-start.7) | collective-permute-done | bytes 1835040 | tf_op jit(solution)/shard_map/ppermute | solution.py:332
  216.1 6.7 %step.20.refs_22_.rest_0_ = bf16[1792,512]{1,0:T(8,128)(2,1)} custom-call(s32[2]{0:T(128)} %pad_add_fusion.place, bf16[1792,512]{1,0:T(8,128)(2,1)} %collective-permute-done.7.got_ref.refs_13_, bf16[3584,1024]{1,0:T(8,128)(2,1)} %hidden.1.hidden_ref, ...), custom_call_target="tpu_custom_call" | custom-call | flops 2000000000 | tf_op jit(solution)/shard_map/step/pallas_call | solution.py:152
  222.8 2.5 collective-permute-start.16
  225.2 1.2 copy-done.5
  226.5 5.4 %step.22.refs_24_.rest_2_ = bf16[1792,512]{1,0:T(8,128)(2,1)} custom-call(s32[2]{0:T(128)} %pad_add_fusion.place, bf16[1792,512]{1,0:T(8,128)(2,1)} %copy-done.5, bf16[3584,1024]{1,0:T(8,128)(2,1)} %hidden.1.hidden_ref, bf16[1024,4096]{1,0:T(8,128)(2,1)} %all-gather.2.cloned.1.call-done.grad_ref.refs_0_.refs_1_.refs_2_.refs_3_.refs_4_.refs_5_.refs_6_.refs_7_), custom_call_target="tpu_custom_call" | custom-call | flops 2000000000 | tf_op jit(solution)/shard_map/step/pallas_call | solution.py:152
  231.9 0.0 collective-permute-start.17
  231.9 26.0 %collective-permute-done.12.got_ref.refs_17_ = bf16[1792,512]{1,0:T(8,128)(2,1)S(1)} collective-permute-done((bf16[1792,512]{1,0:T(8,128)(2,1)}, bf16[1792,512]{1,0:T(8,128)(2,1)S(1)}, u32[]{:S(2)}, u32[]{:S(2)}) %collective-permute-start.12) | collective-permute-done | bytes 1835040 | tf_op jit(solution)/shard_map/ppermute | solution.py:332
  257.9 1.2 copy-done.6
  259.1 5.3 %step.23.refs_25_.rest_3_ = bf16[1792,512]{1,0:T(8,128)(2,1)} custom-call(s32[2]{0:T(128)} %pad_add_fusion.place, bf16[1792,512]{1,0:T(8,128)(2,1)} %copy-done.6, bf16[3584,1024]{1,0:T(8,128)(2,1)} %hidden.1.hidden_ref, bf16[1024,4096]{1,0:T(8,128)(2,1)} %all-gather.2.cloned.1.call-done.grad_ref.refs_0_.refs_1_.refs_2_.refs_3_.refs_4_.refs_5_.refs_6_.refs_7_), custom_call_target="tpu_custom_call" | custom-call | flops 2000000000 | tf_op jit(solution)/shard_map/step/pallas_call | solution.py:152
  264.5 6.7 %step.21.refs_23_.rest_1_ = bf16[1792,512]{1,0:T(8,128)(2,1)} custom-call(s32[2]{0:T(128)} %pad_add_fusion.place, bf16[1792,512]{1,0:T(8,128)(2,1)} %collective-permute-done.14.got_ref.refs_20_, bf16[3584,1024]{1,0:T(8,128)(2,1)} %hidden.1.hidden_ref, ...), custom_call_target="tpu_custom_call" | custom-call | flops 2000000000 | tf_op jit(solution)/shard_map/step/pallas_call | solution.py:152
  271.2 16.4 %product.1 = (bf16[512,1792]{1,0:T(8,128)(2,1)}, f32[8,128]{1,0:T(8,128)}) custom-call(s32[2]{0:T(128)} %pad_add_fusion.place, bf16[1024,4096]{1,0:T(8,128)(2,1)} %all-gather.2.cloned.1.call-done.grad_ref.refs_0_.refs_1_.refs_2_.refs_3_.refs_4_.refs_5_.refs_6_.refs_7_, ...), custom_call_target="tpu_custom_call" | custom-call | tf_op jit(solution)/shard_map/product/pallas_call | solution.py:276
  287.6 0.1 collective-permute-start.15
  287.7 0.5 collective-permute-start.19
  288.2 2.5 collective-permute-start.18
  290.6 10.5 %own.1.own_ref = bf16[3584,512]{1,0:T(8,128)(2,1)} custom-call(s32[2]{0:T(128)} %pad_add_fusion.place, bf16[3584,1024]{1,0:T(8,128)(2,1)} %hidden.1.hidden_ref, bf16[1024,4096]{1,0:T(8,128)(2,1)} %all-gather.2.cloned.1.call-done.grad_ref.refs_0_.refs_1_.refs_2_.refs_3_.refs_4_.refs_5_.refs_6_.refs_7_, bf16[1792,512]{1,0:T(8,128)(2,1)} %step.20.refs_22_.rest_0_, ...), custom_call_target="tpu_custom_call" | custom-call | tf_op jit(solution)/shard_map/own/pallas_call | solution.py:172
  301.1 17.2 %grads.1 = (bf16[512,3584]{1,0:T(8,128)(2,1)}, bf16[512,3584]{1,0:T(8,128)(2,1)}, f32[8,128]{1,0:T(8,128)}) custom-call(s32[2]{0:T(128)} %pad_add_fusion.place, bf16[1024,4096]{1,0:T(8,128)(2,1)} %all-gather.2.cloned.1.call-done.grad_ref.refs_0_.refs_1_.refs_2_.refs_3_.refs_4_.refs_5_.refs_6_.refs_7_, ...), custom_call_target="tpu_custom_call" | custom-call | tf_op jit(solution)/shard_map/grads/pallas_call | solution.py:276
  318.4 5.4 %final.2 = (bf16[3584,512]{1,0:T(8,128)(2,1)}, f32[8,128]{1,0:T(8,128)}) custom-call(s32[2]{0:T(128)} %pad_add_fusion.place, bf16[1792,512]{1,0:T(8,128)(2,1)} %collective-permute-done.16.one_ref, bf16[1792,512]{1,0:T(8,128)(2,1)} %collective-permute-done.17.two_ref, bf16[3584,512]{1,0:T(8,128)(2,1)} %own.1.own_ref, f32[8,128]{1,0:T(8,128)} %get-tuple-element.17.rest_0_), custom_call_target="tpu_custom_call" | custom-call | tf_op jit(solution)/shard_map/final/pallas_call | solution.py:197
  323.8 7.7 %join.1 = (bf16[512,3584]{1,0:T(8,128)(2,1)}, bf16[512,3584]{1,0:T(8,128)(2,1)}) custom-call(s32[2]{0:T(128)} %pad_add_fusion.place, bf16[512,1792]{1,0:T(8,128)(2,1)} %collective-permute-done.15.product_ref, bf16[512,3584]{1,0:T(8,128)(2,1)} %gate_ref.1, bf16[512,3584]{1,0:T(8,128)(2,1)} %up_ref.1, ...), custom_call_target="tpu_custom_call", output_to_operand_aliasing={{0}: (4, {}), {1}: (5, {})} | custom-call | tf_op jit(solution)/shard_map/join/pallas_call | solution.py:299
  331.4 2.9 collective-permute-done.19.two_ref
  334.3 5.4 %final.3 = (bf16[3584,512]{1,0:T(8,128)(2,1)}, f32[8,128]{1,0:T(8,128)}) custom-call(s32[2]{0:T(128)} %pad_add_fusion.place, bf16[1792,512]{1,0:T(8,128)(2,1)} %collective-permute-done.18.one_ref, bf16[1792,512]{1,0:T(8,128)(2,1)} %collective-permute-done.19.two_ref, bf16[3584,512]{1,0:T(8,128)(2,1)} %own.1.own_ref, ...), custom_call_target="tpu_custom_call", output_to_operand_aliasing={{0}: (4, {})} | custom-call | tf_op jit(solution)/shard_map/final/pallas_call | solution.py:197
  (15 shorter events, 0.0 us)
Async XLA Ops:
  7.2 59.8 %all-gather.2.cloned.1.call-start = ((), (), s32[]{:S(2)}) async-start(), calls=%async_computation | async-start | bytes 9437184 | tf_op jit(solution)/shard_map/all_gather | solution.py:341
  7.9 17.8 %collective-permute-start.2 = (bf16[512,3584]{1,0:T(8,128)(2,1)}, bf16[512,3584]{1,0:T(8,128)(2,1)}, u32[]{:S(2)}, u32[]{:S(2)}) collective-permute-start(bf16[512,3584]{1,0:T(8,128)(2,1)} %gate_ref.1), channel_id=1, source_target_pairs={{0,4},{4,0},{8,12},{12,8},{16,20},{20,16},{24,28},{28,24},{1,5},{5... | collective-permute-start | bytes 11010056 | tf_op jit(solution)/shard_map/ppermute | solution.py:329
  8.4 18.9 %collective-permute-start.3 = (bf16[512,3584]{1,0:T(8,128)(2,1)}, bf16[512,3584]{1,0:T(8,128)(2,1)}, u32[]{:S(2)}, u32[]{:S(2)}) collective-permute-start(bf16[512,3584]{1,0:T(8,128)(2,1)} %up_ref.1), channel_id=1, source_target_pairs={{0,4},{4,0},{8,12},{12,8},{16,20},{20,16},{24,28},{28,24},{1,5},{5... | collective-permute-start | bytes 11010056 | tf_op jit(solution)/shard_map/ppermute | solution.py:329
  12.1 3.6 %copy-start = (bf16[1792,512]{1,0:T(8,128)(2,1)S(1)}, bf16[1792,512]{1,0:T(8,128)(2,1)}, u32[]{:S(2)}) copy-start(bf16[1792,512]{1,0:T(8,128)(2,1)} %half.2.rest_0_.refs_8_) | copy-start | bytes 5505028
  15.2 10.1 %collective-permute-start.8 = (bf16[1792,512]{1,0:T(8,128)(2,1)}, bf16[1792,512]{1,0:T(8,128)(2,1)}, u32[]{:S(2)}, u32[]{:S(2)}) collective-permute-start(bf16[1792,512]{1,0:T(8,128)(2,1)} %half.3), channel_id=1, source_target_pairs={{0,4},{4,0},{8,12},{12,8},{16,20},{20,16},{24,28},{28,24},{1,5},{5... | collective-permute-start | bytes 5505032 | tf_op jit(solution)/shard_map/ppermute | solution.py:329
  15.7 43.0 %collective-permute-start = (bf16[1792,512]{1,0:T(8,128)(2,1)S(1)}, bf16[1792,512]{1,0:T(8,128)(2,1)}, u32[]{:S(2)}, u32[]{:S(2)}) collective-permute-start(bf16[1792,512]{1,0:T(8,128)(2,1)S(1)} %copy-done), channel_id=1, source_target_pairs={{0,8},{8,16},{16,24},{24,28},{28,20},{20,12},{12,4},{4,0},{1,9},{9... | collective-permute-start | bytes 5505032 | tf_op jit(solution)/shard_map/ppermute | solution.py:332
  18.4 55.5 %collective-permute-start.1 = (bf16[1792,512]{1,0:T(8,128)(2,1)S(1)}, bf16[1792,512]{1,0:T(8,128)(2,1)}, u32[]{:S(2)}, u32[]{:S(2)}) collective-permute-start(bf16[1792,512]{1,0:T(8,128)(2,1)S(1)} %copy-done), channel_id=1, source_target_pairs={{4,12},{12,20},{20,28},{28,24},{24,16},{16,8},{8,0},{0,4},{5,13},{... | collective-permute-start | bytes 5505032 | tf_op jit(solution)/shard_map/ppermute | solution.py:332
  25.3 75.4 %collective-permute-start.10 = (bf16[1792,512]{1,0:T(8,128)(2,1)}, bf16[1792,512]{1,0:T(8,128)(2,1)}, u32[]{:S(2)}, u32[]{:S(2)}) collective-permute-start(bf16[1792,512]{1,0:T(8,128)(2,1)} %collective-permute-done.8.refs_15_), channel_id=1, source_target_pairs={{4,12},{12,20},{20,28},{28,24},{24,16},{16,8},{8,0},{0,4},{5,13},{... | collective-permute-start | bytes 5505032 | tf_op jit(solution)/shard_map/ppermute | solution.py:332
  25.7 80.4 %collective-permute-start.9 = (bf16[1792,512]{1,0:T(8,128)(2,1)}, bf16[1792,512]{1,0:T(8,128)(2,1)}, u32[]{:S(2)}, u32[]{:S(2)}) collective-permute-start(bf16[1792,512]{1,0:T(8,128)(2,1)} %collective-permute-done.8.refs_15_), channel_id=1, source_target_pairs={{0,8},{8,16},{16,24},{24,28},{28,20},{20,12},{12,4},{4,0},{1,9},{9... | collective-permute-start | bytes 5505032 | tf_op jit(solution)/shard_map/ppermute | solution.py:332
  73.7 63.8 %collective-permute-start.6 = (bf16[1792,512]{1,0:T(8,128)(2,1)}, bf16[1792,512]{1,0:T(8,128)(2,1)}, u32[]{:S(2)}, u32[]{:S(2)}) collective-permute-start(bf16[1792,512]{1,0:T(8,128)(2,1)} %step.14), channel_id=1, source_target_pairs={{0,8},{8,16},{16,24},{24,28},{28,20},{20,12},{12,4},{4,0},{1,9},{9... | collective-permute-start | bytes 5505032 | tf_op jit(solution)/shard_map/ppermute | solution.py:332
  79.1 67.4 %collective-permute-start.4 = (bf16[1792,512]{1,0:T(8,128)(2,1)}, bf16[1792,512]{1,0:T(8,128)(2,1)S(1)}, u32[]{:S(2)}, u32[]{:S(2)}) collective-permute-start(bf16[1792,512]{1,0:T(8,128)(2,1)} %step.12), channel_id=1, source_target_pairs={{4,12},{12,20},{20,28},{28,24},{24,16},{16,8},{8,0},{0,4},{5,13},{... | collective-permute-start | bytes 5505032 | tf_op jit(solution)/shard_map/ppermute | solution.py:332
  106.1 73.2 %collective-permute-start.11 = (bf16[1792,512]{1,0:T(8,128)(2,1)}, bf16[1792,512]{1,0:T(8,128)(2,1)S(1)}, u32[]{:S(2)}, u32[]{:S(2)}) collective-permute-start(bf16[1792,512]{1,0:T(8,128)(2,1)} %step.16), channel_id=1, source_target_pairs={{4,12},{12,20},{20,28},{28,24},{24,16},{16,8},{8,0},{0,4},{5,13},{... | collective-permute-start | bytes 5505032 | tf_op jit(solution)/shard_map/ppermute | solution.py:332
  112.8 73.1 %collective-permute-start.13 = (bf16[1792,512]{1,0:T(8,128)(2,1)}, bf16[1792,512]{1,0:T(8,128)(2,1)}, u32[]{:S(2)}, u32[]{:S(2)}) collective-permute-start(bf16[1792,512]{1,0:T(8,128)(2,1)} %step.18), channel_id=1, source_target_pairs={{0,8},{8,16},{16,24},{24,28},{28,20},{20,12},{12,4},{4,0},{1,9},{9... | collective-permute-start | bytes 5505032 | tf_op jit(solution)/shard_map/ppermute | solution.py:332
  144.1 72.0 %collective-permute-start.7 = (bf16[1792,512]{1,0:T(8,128)(2,1)}, bf16[1792,512]{1,0:T(8,128)(2,1)}, u32[]{:S(2)}, u32[]{:S(2)}) collective-permute-start(bf16[1792,512]{1,0:T(8,128)(2,1)} %step.15), channel_id=1, source_target_pairs={{0,8},{8,16},{16,24},{24,28},{28,20},{20,12},{12,4},{4,0},{1,9},{9... | collective-permute-start | bytes 5505032 | tf_op jit(solution)/shard_map/ppermute | solution.py:332
  146.6 1.2 copy-start.3
  153.1 72.1 %collective-permute-start.5 = (bf16[1792,512]{1,0:T(8,128)(2,1)}, bf16[1792,512]{1,0:T(8,128)(2,1)S(1)}, u32[]{:S(2)}, u32[]{:S(2)}) collective-permute-start(bf16[1792,512]{1,0:T(8,128)(2,1)} %step.13), channel_id=1, source_target_pairs={{4,12},{12,20},{20,28},{28,24},{24,16},{16,8},{8,0},{0,4},{5,13},{... | collective-permute-start | bytes 5505032 | tf_op jit(solution)/shard_map/ppermute | solution.py:332
  179.3 1.2 copy-start.4
  185.9 72.1 %collective-permute-start.12 = (bf16[1792,512]{1,0:T(8,128)(2,1)}, bf16[1792,512]{1,0:T(8,128)(2,1)S(1)}, u32[]{:S(2)}, u32[]{:S(2)}) collective-permute-start(bf16[1792,512]{1,0:T(8,128)(2,1)} %step.17), channel_id=1, source_target_pairs={{4,12},{12,20},{20,28},{28,24},{24,16},{16,8},{8,0},{0,4},{5,13},{... | collective-permute-start | bytes 5505032 | tf_op jit(solution)/shard_map/ppermute | solution.py:332
  192.6 71.9 %collective-permute-start.14 = (bf16[1792,512]{1,0:T(8,128)(2,1)}, bf16[1792,512]{1,0:T(8,128)(2,1)}, u32[]{:S(2)}, u32[]{:S(2)}) collective-permute-start(bf16[1792,512]{1,0:T(8,128)(2,1)} %step.19), channel_id=1, source_target_pairs={{0,8},{8,16},{16,24},{24,28},{28,20},{20,12},{12,4},{4,0},{1,9},{9... | collective-permute-start | bytes 5505032 | tf_op jit(solution)/shard_map/ppermute | solution.py:332
  222.8 95.6 %collective-permute-start.16 = (bf16[1792,512]{1,0:T(8,128)(2,1)}, bf16[1792,512]{1,0:T(8,128)(2,1)}, u32[]{:S(2)}, u32[]{:S(2)}) collective-permute-start(bf16[1792,512]{1,0:T(8,128)(2,1)} %step.20.refs_22_.rest_0_), channel_id=1, source_target_pairs={{0,8},{8,16},{16,24},{24,28},{28,20},{20,12},{12,4},{4,0},{1,9},{9... | collective-permute-start | bytes 5505032 | tf_op jit(solution)/shard_map/ppermute | solution.py:332
  225.2 1.2 copy-start.5
  231.9 86.5 %collective-permute-start.17 = (bf16[1792,512]{1,0:T(8,128)(2,1)}, bf16[1792,512]{1,0:T(8,128)(2,1)}, u32[]{:S(2)}, u32[]{:S(2)}) collective-permute-start(bf16[1792,512]{1,0:T(8,128)(2,1)} %step.22.refs_24_.rest_2_), channel_id=1, source_target_pairs={{4,12},{12,20},{20,28},{28,24},{24,16},{16,8},{8,0},{0,4},{5,13},{... | collective-permute-start | bytes 5505032 | tf_op jit(solution)/shard_map/ppermute | solution.py:332
  257.9 1.2 copy-start.6
  271.2 16.5 %copy-start.1 = (bf16[1792,512]{1,0:T(8,128)(2,1)S(1)}, bf16[1792,512]{1,0:T(8,128)(2,1)}, u32[]{:S(2)}) copy-start(bf16[1792,512]{1,0:T(8,128)(2,1)} %step.23.refs_25_.rest_3_) | copy-start | bytes 5505028
  271.2 17.0 %copy-start.2 = (bf16[1792,512]{1,0:T(8,128)(2,1)S(1)}, bf16[1792,512]{1,0:T(8,128)(2,1)}, u32[]{:S(2)}) copy-start(bf16[1792,512]{1,0:T(8,128)(2,1)} %step.21.refs_23_.rest_1_) | copy-start | bytes 5505028
  287.6 36.2 %collective-permute-start.15 = (bf16[512,1792]{1,0:T(8,128)(2,1)}, bf16[512,1792]{1,0:T(8,128)(2,1)}, u32[]{:S(2)}, u32[]{:S(2)}) collective-permute-start(bf16[512,1792]{1,0:T(8,128)(2,1)} %get-tuple-element.13), channel_id=1, source_target_pairs={{0,4},{4,0},{8,12},{12,8},{16,20},{20,16},{24,28},{28,24},{1,5},{5... | collective-permute-start | bytes 5505032 | tf_op jit(solution)/shard_map/ppermute | solution.py:329
  287.7 46.7 %collective-permute-start.19 = (bf16[1792,512]{1,0:T(8,128)(2,1)S(1)}, bf16[1792,512]{1,0:T(8,128)(2,1)}, u32[]{:S(2)}, u32[]{:S(2)}) collective-permute-start(bf16[1792,512]{1,0:T(8,128)(2,1)S(1)} %copy-done.1), channel_id=1, source_target_pairs={{4,12},{12,20},{20,28},{28,24},{24,16},{16,8},{8,0},{0,4},{5,13},{... | collective-permute-start | bytes 5505032 | tf_op jit(solution)/shard_map/ppermute | solution.py:332
  288.2 46.2 %collective-permute-start.18 = (bf16[1792,512]{1,0:T(8,128)(2,1)S(1)}, bf16[1792,512]{1,0:T(8,128)(2,1)}, u32[]{:S(2)}, u32[]{:S(2)}) collective-permute-start(bf16[1792,512]{1,0:T(8,128)(2,1)S(1)} %copy-done.2), channel_id=1, source_target_pairs={{0,8},{8,16},{16,24},{24,28},{28,20},{20,12},{12,4},{4,0},{1,9},{9... | collective-permute-start | bytes 5505032 | tf_op jit(solution)/shard_map/ppermute | solution.py:332
Sparse Core Ops, SparseCore 0:
  9.9 57.0 all-gather.1

commit v2 on v1

--- a/solution.py
+++ b/solution.py
@@ -43,11 +43,10 @@
     return lax.dot_general(a, b, (contract, ((), ())), preferred_element_type=F32)
 
 
-def half_kernel(flip, place, weight_ref, *rest):
-    out_ref, held, load_sem, store_sem = rest[-4:]
+def half_kernel(place, weight_ref, out_ref, held, load_sem, store_sem):
     half = out_ref.shape[0]
     part = half // COPIES
-    start = (place[1] ^ flip) * half
+    start = place[1] * half
 
     def load(i):
         source = pl.multiple_of(start + i * part, part)
@@ -69,13 +68,13 @@
         store(i).wait()
 
 
-def half_call(place, weight, flip, after):
+def half_call(place, weight):
     units, block = weight.shape
     half = units // 2
     return call(
-        functools.partial(half_kernel, flip),
+        half_kernel,
         (1,),
-        [ANY] * (1 + len(after)),
+        [ANY],
         ANY,
         jax.ShapeDtypeStruct((half, block), BF16),
         "half",
@@ -84,7 +83,7 @@
             pltpu.SemaphoreType.DMA((COPIES,)),
             pltpu.SemaphoreType.DMA((COPIES,)),
         ],
-    )(place, weight, *after)
+    )(place, weight)
 
 
 def hidden_kernel(place, gate_own, up_own, gate_sib, up_sib, out_ref):
@@ -125,7 +124,8 @@
     ]
 
 
-def step_kernel(flow, j, line, place, got_ref, hidden_ref, grad_ref, out_ref):
+def step_kernel(flow, j, line, place, got_ref, hidden_ref, grad_ref, *rest):
+    out_ref = rest[-1]
     at = along(place, flow, line)
     adds = at + j < line
 
@@ -140,63 +140,78 @@
         out_ref[...] = got_ref[...]
 
 
-def step_call(place, got, hidden, grads, k, j, flow, line):
+def step_call(place, got, hidden, grads, k, quarters, j, flow, line, after=()):
     chunk, block = got.shape
     tokens = hidden.shape[1]
-    steps = 4
-    tile = chunk // steps
+    tile = chunk // 4
+    low, high = quarters
 
     def ahead(s):
         return jnp.where(s[1] == flow, j, line - j)
 
     return call(
         functools.partial(step_kernel, flow, j, line),
-        (steps,),
-        [pl.BlockSpec((tile, block), lambda i, s: (i, 0))]
-        + term_specs(tile, tokens, block, k * steps, ahead, line),
+        (high - low,),
+        [pl.BlockSpec((tile, block), lambda i, s: (low + i, 0))]
+        + term_specs(tile, tokens, block, k * 4 + low, ahead, line)
+        + [ANY] * len(after),
         pl.BlockSpec((tile, block), lambda i, s: (i, 0)),
-        jax.ShapeDtypeStruct((chunk, block), BF16),
+        jax.ShapeDtypeStruct(((high - low) * tile, block), BF16),
         "step",
-        flops=STEP_FLOPS,
-    )(place, got, hidden, grads)
-
-
-def own_kernel(place, hidden_ref, grad_ref, *rest):
-    rest[-1][...] = dot(hidden_ref[...], grad_ref[...], ((1,), (0,))).astype(BF16)
-
-
-def own_call(place, hidden, grads, block, line, after):
+        flops=STEP_FLOPS * (high - low) / 4,
+    )(place, got, hidden, grads, *after)
+
+
+def own_kernel(place, hidden_ref, grad_ref, out_ref):
+    out_ref[...] = dot(hidden_ref[...], grad_ref[...], ((1,), (0,))).astype(BF16)
+
+
+def own_call(place, hidden, grads, block, line):
     units, tokens = hidden.shape
     steps = 8
     tile = units // steps
     return call(
         own_kernel,
         (steps,),
-        term_specs(tile, tokens, block, 0, lambda s: 0, line) + [ANY] * len(after),
+        term_specs(tile, tokens, block, 0, lambda s: 0, line),
         pl.BlockSpec((tile, block), lambda i, s: (i, 0)),
         jax.ShapeDtypeStruct((units, block), BF16),
         "own",
-    )(place, hidden, grads, *after)
+    )(place, hidden, grads)
 
 
 def final_kernel(scale, line, place, one_ref, two_ref, own_ref, *rest):
     at = along(place, 0, line)
-    one = jnp.where(at > 0, one_ref[...].astype(F32), 0.0)
-    two = jnp.where(at < line - 1, two_ref[...].astype(F32), 0.0)
     out_ref, token = rest[-2:]
-    out_ref[...] = ((one + two + own_ref[...].astype(F32)) * scale).astype(BF16)
     token[...] = jnp.zeros_like(token)
 
-
-def final_call(place, one, two, own, k, line, scale, before, after):
-    chunk, block = one.shape
-    steps = 4
-    tile = chunk // steps
+    def store(*refs):
+        total = own_ref[...].astype(F32)
+        for ref in refs:
+            total += ref[...].astype(F32)
+        out_ref[...] = (total * scale).astype(BF16)
+
+    @pl.when(at == 0)
+    def _():
+        store(two_ref)
+
+    @pl.when(at == line - 1)
+    def _():
+        store(one_ref)
+
+    @pl.when(jnp.logical_and(at > 0, at < line - 1))
+    def _():
+        store(one_ref, two_ref)
+
+
+def final_call(place, one, two, own, quarter, line, scale, before, after):
+    rows, block = one.shape
+    tile = own.shape[0] // 16
     got = pl.BlockSpec((tile, block), lambda i, s: (i, 0))
-    here = pl.BlockSpec((tile, block), lambda i, s: (k * steps + i, 0))
+    here = pl.BlockSpec((tile, block), lambda i, s: (2 * quarter + i, 0))
     return call(
         functools.partial(final_kernel, scale, line),
-        (steps,),
+        (rows // tile,),
         [got, got, here] + [ANY] * len(before + after),
         [here, pl.BlockSpec((8, 128), lambda i, s: (0, 0))],
         [jax.ShapeDtypeStruct(own.shape, BF16), jax.ShapeDtypeStruct((8, 128), F32)],
@@ -331,8 +346,7 @@
     def send(x, flow):
         return lax.ppermute(x, "dp", rings[flow])
 
-    half_own = half_call(place, down_weight, 0, ())
-    first = [half_own, swap(half_call(place, down_weight, 1, (half_own,)))]
+    first = [half_call(place, down_weight), half_call(place, swap(down_weight))]
     got = [[[send(x, flow) for x in first]] for flow in range(2)]
 
     groups = [
@@ -344,19 +358,22 @@
     gate_sib, up_sib = swap(gate_pre), swap(up_pre)
     hidden = hidden_call(place, gate_pre, up_pre, gate_sib, up_sib)
 
-    sent = []
-    for slot in range(2, line + 1):
-        sent = [
-            [
-                step_call(place, got[flow][-1][k], hidden, out_grads, k, line + 1 - slot, flow, line)
-                for k in range(2)
-            ]
-            for flow in range(2)
-        ]
+    def step(slot, flow, k, quarters, after=()):
+        before = got[flow][slot - 2][k]
+        j = line + 1 - slot
+        return step_call(place, before, hidden, out_grads, k, quarters, j, flow, line, after)
+
+    for slot in range(2, line):
+        sent = [[step(slot, flow, k, (0, 4)) for k in range(2)] for flow in range(2)]
         for flow in range(2):
             got[flow].append([send(x, flow) for x in sent[flow]])
+
+    own = own_call(place, hidden, out_grads, block, line)
+    sent = [
+        [step(line, flow, 0, (0, 4), (own,)), step(line, flow, 1, (0, 3))] for flow in range(2)
+    ]
+    last = [[send(x, flow) for x in sent[flow]] for flow in range(2)]
     sent = sent[0] + sent[1]
-    own = own_call(place, hidden, out_grads, block, line, sent)
 
     weights = []
     for k in range(2):
@@ -368,12 +385,15 @@
     own_half = (gate_pre, up_pre)
     *grads, token = product_call(place, out_grads, weights, own_half, 0, line, [token])
 
-    last = [got[flow][-1] for flow in range(2)]
-    grad_down, token = final_call(place, last[0][0], last[1][0], own, 0, line, scale, (), (token,))
+    for flow in range(2):
+        last[flow].append(send(step(line, flow, 1, (3, 4), (token,)), flow))
+    one, two = last
+    grad_down, token = final_call(place, one[0], two[0], own, 0, line, scale, (), (token,))
     grads = join_call(place, from_sib, gate_pre, up_pre, *grads, [token])
-    grad_down, _ = final_call(
-        place, last[0][1], last[1][1], own, 1, line, scale, (grad_down,), tuple(grads)
-    )
+    for piece, quarter in ((1, 4), (2, 7)):
+        grad_down, _ = final_call(
+            place, one[piece], two[piece], own, quarter, line, scale, (grad_down,), tuple(grads)
+        )
     return (*grads, grad_down)
 
 

time: 349 us -> 346 us (level)
  waiting for transfers between devices: 153 us -> 133 us
  Pallas kernels: 155 us -> 166 us
  starting transfers between devices: 18.5 us -> 23.5 us
    ppermute x16 -> x18, waiting for transfers between devices: 137 us -> 114 us  [send(): return lax.ppermute(x, 'dp', rings[flow])]
    pallas_call x16 -> x19, Pallas kernels: 89 us -> 99.7 us  [the longest x14 77.8 us: step_call(): call(functools.partial(step_kernel, flow, j, line), (high - low,), [pl.Bl...]
    ppermute x16 -> x18, starting transfers between devices: 17.3 us -> 22.4 us  [send(): return lax.ppermute(x, 'dp', rings[flow])]
  transfers between devices with their start and end apart: 21 -> 23, of which waited for: 9 -> 9; matrix products, arithmetic and copies ran while one was open for 0% -> 0% of each run, Pallas kernels for 43% -> 48%
where the time goes in v2:
time: 346 us; the launch traced here: 344 us
  Pallas kernels  166 us (48%)
  waiting for transfers between devices  133 us (38%)
  starting transfers between devices  23.5 us (7%)
  between operations  14.1 us (4%)
  local copies, waits for them, and re-layouts  6.14 us (2%)
    ppermute x18, waiting for transfers between devices, send(): return lax.ppermute(x, 'dp', rings[flow])  114 us
    pallas_call x14, Pallas kernels, step_call(): call(functools.partial(step_kernel, flow, j, line), (high - low,), [pl.Bl...  77.8 us
    pallas_call x2, Pallas kernels, product_call(): call(functools.partial(kernel, line, len(weights)), (steps,), [row_spec(c...  33.6 us
    ppermute x18, starting transfers between devices, send(): return lax.ppermute(x, 'dp', rings[flow])  22.4 us
    pallas_call x3, Pallas kernels, final_call(): call(functools.partial(final_kernel, scale, line), (rows // tile,), [got,...  15.9 us
    pallas_call x1, Pallas kernels, hidden_call(): call(hidden_kernel, (units // tile,), [pl.BlockSpec((tokens, tile), lambd...  14.8 us
    all_gather x1, waiting for transfers between devices, shards(): lax.all_gather(out_grad, ('dp', 'mp'), axis=0, tiled=True, axis_index_gro...  11.1 us
    pallas_call x1, Pallas kernels, own_call(): call(own_kernel, (steps,), term_specs(tile, tokens, block, 0, lambda s: 0...  10.5 us
  transfers between devices with their start and end apart: 23, of which 9 were waited for; matrix products, arithmetic and copies ran while one was open for 0% of the time, Pallas kernels for 48%

profile of v2, /device:TPU:0, one launch (start us, length us, event | category | flops | bytes accessed | tf_op | source)
XLA Modules:
  0.0 343.9 jit_solution(14227290375236020746)
XLA Ops:
  7.2 0.0 all-gather.2.cloned.1.call-start
  7.2 0.7 all-gather.2.cloned.1.call-update
  7.9 0.5 collective-permute-start.8
  8.4 0.1 collective-permute-start.2
  8.5 0.4 collective-permute-start.3
  8.9 0.6 pad_add_fusion.place
  9.6 3.0 half.2.refs_8_
  12.6 2.7 collective-permute-start
  15.2 3.0 half.3.refs_15_
  18.3 2.5 collective-permute-start.9
  20.8 1.8 collective-permute-done.2.gate_sib
  22.6 0.1 collective-permute-start.10
  22.7 5.1 %collective-permute-done.3.up_sib = bf16[512,3584]{1,0:T(8,128)(2,1)} collective-permute-done((bf16[512,3584]{1,0:T(8,128)(2,1)}, bf16[512,3584]{1,0:T(8,128)(2,1)}, u32[]{:S(2)}, u32[]{:S(2)}) %collective-permute-start.3) | collective-permute-done | bytes 3670048 | tf_op jit(solution)/shard_map/ppermute | solution.py:344
  27.8 14.8 %hidden.1.hidden_ref = bf16[3584,1024]{1,0:T(8,128)(2,1)} custom-call(s32[2]{0:T(128)} %pad_add_fusion.place, bf16[512,3584]{1,0:T(8,128)(2,1)} %gate_ref.1, bf16[512,3584]{1,0:T(8,128)(2,1)} %up_ref.1, bf16[512,3584]{1,0:T(8,128)(2,1)} %collective-permute-done.2.gate_sib, bf16[512,3584]{1,0:T(8,128)(2,1)} %collective-permute-done.3.up_sib), custom_call_target="tpu_custom_call" | custom-call | tf_op jit(solution)/shard_map/hidden/pallas_call | solution.py:103
  42.7 13.2 %collective-permute-done.got_ref.refs_9_ = bf16[1792,512]{1,0:T(8,128)(2,1)S(1)} collective-permute-done((bf16[1792,512]{1,0:T(8,128)(2,1)}, bf16[1792,512]{1,0:T(8,128)(2,1)S(1)}, u32[]{:S(2)}, u32[]{:S(2)}) %collective-permute-start) | collective-permute-done | bytes 1835040 | tf_op jit(solution)/shard_map/ppermute | solution.py:347
  55.9 11.1 %all-gather.2.cloned.1.call-done.grad_ref.refs_0_.refs_1_.refs_2_.refs_3_.refs_4_.refs_5_.refs_6_.refs_7_ = bf16[1024,4096]{1,0:T(8,128)(2,1)} async-done(((bf16[128,4096]{1,0:T(8,128)(2,1)}), bf16[1024,4096]{1,0:T(8,128)(2,1)}) %all-gather.2.cloned.1.call-update) | async-done | bytes 8388624 | tf_op jit(solution)/shard_map/all_gather | solution.py:355
  67.0 6.7 %step.16 = bf16[1792,512]{1,0:T(8,128)(2,1)} custom-call(s32[2]{0:T(128)} %pad_add_fusion.place, bf16[1792,512]{1,0:T(8,128)(2,1)} %copy-done.2, bf16[3584,1024]{1,0:T(8,128)(2,1)} %hidden.1.hidden_ref, bf16[1024,4096]{1,0:T(8,128)(2,1)} %all-gather.2.cloned.1.call-done.grad_ref.refs_0_.refs_1_.refs_2_.refs_3_.refs_4_.refs_5_.refs_6_.refs_7_), custom_call_target="tpu_custom_call" | custom-call | flops 2000000000 | tf_op jit(solution)/shard_map/step/pallas_call | solution.py:152
  73.7 0.1 collective-permute-start.6
  73.8 5.3 %step.14 = bf16[1792,512]{1,0:T(8,128)(2,1)} custom-call(s32[2]{0:T(128)} %pad_add_fusion.place, bf16[1792,512]{1,0:T(8,128)(2,1)} %collective-permute-done.1.got_ref.refs_14_, bf16[3584,1024]{1,0:T(8,128)(2,1)} %hidden.1.hidden_ref, bf16[1024,4096]{1,0:T(8,128)(2,1)} %all-gather.2.cloned.1.call-done.grad_ref.refs_0_.refs_1_.refs_2_.refs_3_.refs_4_.refs_5_.refs_6_.refs_7_), custom_call_target="tpu_custom_call" | custom-call | flops 2000000000 | tf_op jit(solution)/shard_map/step/pallas_call | solution.py:152
  79.1 1.7 collective-permute-start.4
  80.9 14.3 %collective-permute-done.9.got_ref.refs_16_ = bf16[1792,512]{1,0:T(8,128)(2,1)} collective-permute-done((bf16[1792,512]{1,0:T(8,128)(2,1)}, bf16[1792,512]{1,0:T(8,128)(2,1)}, u32[]{:S(2)}, u32[]{:S(2)}) %collective-permute-start.9) | collective-permute-done | bytes 1835040 | tf_op jit(solution)/shard_map/ppermute | solution.py:347
  95.2 6.7 %step.20 = bf16[1792,512]{1,0:T(8,128)(2,1)} custom-call(s32[2]{0:T(128)} %pad_add_fusion.place, bf16[1792,512]{1,0:T(8,128)(2,1)} %collective-permute-done.9.got_ref.refs_16_, bf16[3584,1024]{1,0:T(8,128)(2,1)} %hidden.1.hidden_ref, bf16[1024,4096]{1,0:T(8,128)(2,1)} %all-gather.2.cloned.1.call-done.grad_ref.refs_0_.refs_1_.refs_2_.refs_3_.refs_4_.refs_5_.refs_6_.refs_7_), custom_call_target="tpu_custom_call" | custom-call | flops 2000000000 | tf_op jit(solution)/shard_map/step/pallas_call | solution.py:152
  101.9 1.2 collective-permute-start.13
  103.0 0.0 collective-permute-done.10.got_ref.refs_21_
  103.1 5.4 %step.18 = bf16[1792,512]{1,0:T(8,128)(2,1)} custom-call(s32[2]{0:T(128)} %pad_add_fusion.place, bf16[1792,512]{1,0:T(8,128)(2,1)} %collective-permute-done.10.got_ref.refs_21_, bf16[3584,1024]{1,0:T(8,128)(2,1)} %hidden.1.hidden_ref, bf16[1024,4096]{1,0:T(8,128)(2,1)} %all-gather.2.cloned.1.call-done.grad_ref.refs_0_.refs_1_.refs_2_.refs_3_.refs_4_.refs_5_.refs_6_.refs_7_), custom_call_target="tpu_custom_call" | custom-call | flops 2000000000 | tf_op jit(solution)/shard_map/step/pallas_call | solution.py:152
  108.4 0.7 collective-permute-start.11
  109.1 25.4 %collective-permute-done.6.got_ref.refs_11_ = bf16[1792,512]{1,0:T(8,128)(2,1)S(1)} collective-permute-done((bf16[1792,512]{1,0:T(8,128)(2,1)}, bf16[1792,512]{1,0:T(8,128)(2,1)S(1)}, u32[]{:S(2)}, u32[]{:S(2)}) %collective-permute-start.6) | collective-permute-done | bytes 1835040 | tf_op jit(solution)/shard_map/ppermute | solution.py:347
  134.5 1.3 copy-done.3
  135.8 6.7 %step.17 = bf16[1792,512]{1,0:T(8,128)(2,1)} custom-call(s32[2]{0:T(128)} %pad_add_fusion.place, bf16[1792,512]{1,0:T(8,128)(2,1)} %copy-done.3, bf16[3584,1024]{1,0:T(8,128)(2,1)} %hidden.1.hidden_ref, bf16[1024,4096]{1,0:T(8,128)(2,1)} %all-gather.2.cloned.1.call-done.grad_ref.refs_0_.refs_1_.refs_2_.refs_3_.refs_4_.refs_5_.refs_6_.refs_7_), custom_call_target="tpu_custom_call" | custom-call | flops 2000000000 | tf_op jit(solution)/shard_map/step/pallas_call | solution.py:152
  142.5 2.4 collective-permute-start.7
  144.9 0.0 collective-permute-done.4.got_ref.refs_12_
  144.9 1.2 copy-done.4
  146.1 5.3 %step.15 = bf16[1792,512]{1,0:T(8,128)(2,1)} custom-call(s32[2]{0:T(128)} %pad_add_fusion.place, bf16[1792,512]{1,0:T(8,128)(2,1)} %copy-done.4, bf16[3584,1024]{1,0:T(8,128)(2,1)} %hidden.1.hidden_ref, bf16[1024,4096]{1,0:T(8,128)(2,1)} %all-gather.2.cloned.1.call-done.grad_ref.refs_0_.refs_1_.refs_2_.refs_3_.refs_4_.refs_5_.refs_6_.refs_7_), custom_call_target="tpu_custom_call" | custom-call | flops 2000000000 | tf_op jit(solution)/shard_map/step/pallas_call | solution.py:152
  151.4 22.4 %collective-permute-done.13.got_ref.refs_18_ = bf16[1792,512]{1,0:T(8,128)(2,1)} collective-permute-done((bf16[1792,512]{1,0:T(8,128)(2,1)}, bf16[1792,512]{1,0:T(8,128)(2,1)}, u32[]{:S(2)}, u32[]{:S(2)}) %collective-permute-start.13) | collective-permute-done | bytes 1835040 | tf_op jit(solution)/shard_map/ppermute | solution.py:347
  173.8 6.7 %step.21 = bf16[1792,512]{1,0:T(8,128)(2,1)} custom-call(s32[2]{0:T(128)} %pad_add_fusion.place, bf16[1792,512]{1,0:T(8,128)(2,1)} %collective-permute-done.13.got_ref.refs_18_, bf16[3584,1024]{1,0:T(8,128)(2,1)} %hidden.1.hidden_ref, bf16[1024,4096]{1,0:T(8,128)(2,1)} %all-gather.2.cloned.1.call-done.grad_ref.refs_0_.refs_1_.refs_2_.refs_3_.refs_4_.refs_5_.refs_6_.refs_7_), custom_call_target="tpu_custom_call" | custom-call | flops 2000000000 | tf_op jit(solution)/shard_map/step/pallas_call | solution.py:152
  180.5 2.5 collective-permute-start.14
  183.0 5.4 %step.19 = bf16[1792,512]{1,0:T(8,128)(2,1)} custom-call(s32[2]{0:T(128)} %pad_add_fusion.place, bf16[1792,512]{1,0:T(8,128)(2,1)} %collective-permute-done.11.got_ref.refs_19_, bf16[3584,1024]{1,0:T(8,128)(2,1)} %hidden.1.hidden_ref, bf16[1024,4096]{1,0:T(8,128)(2,1)} %all-gather.2.cloned.1.call-done.grad_ref.refs_0_.refs_1_.refs_2_.refs_3_.refs_4_.refs_5_.refs_6_.refs_7_), custom_call_target="tpu_custom_call" | custom-call | flops 2000000000 | tf_op jit(solution)/shard_map/step/pallas_call | solution.py:152
  188.4 0.0 collective-permute-start.12
  188.4 10.5 %own.1.rest_0_.own_ref = bf16[3584,512]{1,0:T(8,128)(2,1)} custom-call(s32[2]{0:T(128)} %pad_add_fusion.place, bf16[3584,1024]{1,0:T(8,128)(2,1)} %hidden.1.hidden_ref, bf16[1024,4096]{1,0:T(8,128)(2,1)} %all-gather.2.cloned.1.call-done.grad_ref.refs_0_.refs_1_.refs_2_.refs_3_.refs_4_.refs_5_.refs_6_.refs_7_), custom_call_target="tpu_custom_call" | custom-call | tf_op jit(solution)/shard_map/own/pallas_call | solution.py:173
  198.9 14.3 %collective-permute-done.7.got_ref.refs_13_ = bf16[1792,512]{1,0:T(8,128)(2,1)} collective-permute-done((bf16[1792,512]{1,0:T(8,128)(2,1)}, bf16[1792,512]{1,0:T(8,128)(2,1)}, u32[]{:S(2)}, u32[]{:S(2)}) %collective-permute-start.7) | collective-permute-done | bytes 1835040 | tf_op jit(solution)/shard_map/ppermute | solution.py:347
  213.2 6.7 %step.22.refs_22_ = bf16[1792,512]{1,0:T(8,128)(2,1)} custom-call(s32[2]{0:T(128)} %pad_add_fusion.place, bf16[1792,512]{1,0:T(8,128)(2,1)} %collective-permute-done.7.got_ref.refs_13_, bf16[3584,1024]{1,0:T(8,128)(2,1)} %hidden.1.hidden_ref, ...), custom_call_target="tpu_custom_call" | custom-call | flops 2000000000 | tf_op jit(solution)/shard_map/step/pallas_call | solution.py:152
  219.9 2.5 collective-permute-start.16
  222.4 5.4 %step.24.refs_24_ = bf16[1792,512]{1,0:T(8,128)(2,1)} custom-call(s32[2]{0:T(128)} %pad_add_fusion.place, bf16[1792,512]{1,0:T(8,128)(2,1)} %collective-permute-done.5.got_ref.refs_10_, bf16[3584,1024]{1,0:T(8,128)(2,1)} %hidden.1.hidden_ref, ...), custom_call_target="tpu_custom_call" | custom-call | flops 2000000000 | tf_op jit(solution)/shard_map/step/pallas_call | solution.py:152
  227.7 24.8 %collective-permute-done.14.got_ref.refs_20_ = bf16[1792,512]{1,0:T(8,128)(2,1)S(1)} collective-permute-done((bf16[1792,512]{1,0:T(8,128)(2,1)}, bf16[1792,512]{1,0:T(8,128)(2,1)S(1)}, u32[]{:S(2)}, u32[]{:S(2)}) %collective-permute-start.14) | collective-permute-done | bytes 1835040 | tf_op jit(solution)/shard_map/ppermute | solution.py:347
  252.5 1.3 copy-done
  253.8 5.9 %step.23.refs_23_ = bf16[1344,512]{1,0:T(8,128)(2,1)} custom-call(s32[2]{0:T(128)} %pad_add_fusion.place, bf16[1792,512]{1,0:T(8,128)(2,1)} %copy-done, bf16[3584,1024]{1,0:T(8,128)(2,1)} %hidden.1.hidden_ref, bf16[1024,4096]{1,0:T(8,128)(2,1)} %all-gather.2.cloned.1.call-done.grad_ref.refs_0_.refs_1_.refs_2_.refs_3_.refs_4_.refs_5_.refs_6_.refs_7_), custom_call_target="tpu_custom_call" | custom-call | flops 1500000000 | tf_op jit(solution)/shard_map/step/pallas_call | solution.py:152
  259.7 0.0 collective-permute-done.12.got_ref.refs_17_
  259.7 1.2 copy-done.1
  260.9 4.9 %step.25.refs_25_ = bf16[1344,512]{1,0:T(8,128)(2,1)} custom-call(s32[2]{0:T(128)} %pad_add_fusion.place, bf16[1792,512]{1,0:T(8,128)(2,1)} %copy-done.1, bf16[3584,1024]{1,0:T(8,128)(2,1)} %hidden.1.hidden_ref, bf16[1024,4096]{1,0:T(8,128)(2,1)} %all-gather.2.cloned.1.call-done.grad_ref.refs_0_.refs_1_.refs_2_.refs_3_.refs_4_.refs_5_.refs_6_.refs_7_), custom_call_target="tpu_custom_call" | custom-call | flops 1500000000 | tf_op jit(solution)/shard_map/step/pallas_call | solution.py:152
  265.8 16.4 %product.1 = (bf16[512,1792]{1,0:T(8,128)(2,1)}, f32[8,128]{1,0:T(8,128)}) custom-call(s32[2]{0:T(128)} %pad_add_fusion.place, bf16[1024,4096]{1,0:T(8,128)(2,1)} %all-gather.2.cloned.1.call-done.grad_ref.refs_0_.refs_1_.refs_2_.refs_3_.refs_4_.refs_5_.refs_6_.refs_7_, ...), custom_call_target="tpu_custom_call" | custom-call | tf_op jit(solution)/shard_map/product/pallas_call | solution.py:291
  282.2 0.1 collective-permute-start.15
  282.3 3.4 collective-permute-start.20
  285.6 0.0 collective-permute-start.21
  285.7 17.2 %grads.1 = (bf16[512,3584]{1,0:T(8,128)(2,1)}, bf16[512,3584]{1,0:T(8,128)(2,1)}, f32[8,128]{1,0:T(8,128)}) custom-call(s32[2]{0:T(128)} %pad_add_fusion.place, bf16[1024,4096]{1,0:T(8,128)(2,1)} %all-gather.2.cloned.1.call-done.grad_ref.refs_0_.refs_1_.refs_2_.refs_3_.refs_4_.refs_5_.refs_6_.refs_7_, ...), custom_call_target="tpu_custom_call" | custom-call | tf_op jit(solution)/shard_map/grads/pallas_call | solution.py:291
  302.9 3.7 %step.26 = bf16[448,512]{1,0:T(8,128)(2,1)} custom-call(s32[2]{0:T(128)} %pad_add_fusion.place, bf16[1792,512]{1,0:T(8,128)(2,1)} %copy-done, bf16[3584,1024]{1,0:T(8,128)(2,1)} %hidden.1.hidden_ref, bf16[1024,4096]{1,0:T(8,128)(2,1)} %all-gather.2.cloned.1.call-done.grad_ref.refs_0_.refs_1_.refs_2_.refs_3_.refs_4_.refs_5_.refs_6_.refs_7_, ...), custom_call_target="tpu_custom_call" | custom-call | flops 500000000 | tf_op jit(solution)/shard_map/step/pallas_call | solution.py:152
  306.6 3.1 step.27
  309.7 0.0 collective-permute-done.16.one_ref
  309.8 2.6 collective-permute-start.18
  312.4 0.0 collective-permute-done.17.two_ref
  312.4 7.2 %final.3 = (bf16[3584,512]{1,0:T(8,128)(2,1)}, f32[8,128]{1,0:T(8,128)}) custom-call(s32[2]{0:T(128)} %pad_add_fusion.place, bf16[1792,512]{1,0:T(8,128)(2,1)} %collective-permute-done.16.one_ref, bf16[1792,512]{1,0:T(8,128)(2,1)} %collective-permute-done.17.two_ref, bf16[3584,512]{1,0:T(8,128)(2,1)} %own.1.rest_0_.own_ref, f32[8,128]{1,0:T(8,128)} %get-tuple-element.18.rest_0_), custom_call_target="tpu_custom_call" | custom-call | tf_op jit(solution)/shard_map/final/pallas_call | solution.py:212
  319.6 7.7 %join.1 = (bf16[512,3584]{1,0:T(8,128)(2,1)}, bf16[512,3584]{1,0:T(8,128)(2,1)}) custom-call(s32[2]{0:T(128)} %pad_add_fusion.place, bf16[512,1792]{1,0:T(8,128)(2,1)} %collective-permute-done.15.product_ref, bf16[512,3584]{1,0:T(8,128)(2,1)} %gate_ref.1, bf16[512,3584]{1,0:T(8,128)(2,1)} %up_ref.1, ...), custom_call_target="tpu_custom_call", output_to_operand_aliasing={{0}: (4, {}), {1}: (5, {})} | custom-call | tf_op jit(solution)/shard_map/join/pallas_call | solution.py:314
  327.2 1.1 copy-done.7
  328.4 5.9 %final.4 = (bf16[3584,512]{1,0:T(8,128)(2,1)}, f32[8,128]{1,0:T(8,128)}) custom-call(s32[2]{0:T(128)} %pad_add_fusion.place, bf16[1344,512]{1,0:T(8,128)(2,1)} %copy-done.7, bf16[1344,512]{1,0:T(8,128)(2,1)} %collective-permute-done.21.two_ref, bf16[3584,512]{1,0:T(8,128)(2,1)} %own.1.rest_0_.own_ref, ...), custom_call_target="tpu_custom_call", output_to_operand_aliasing={{0}: (4, {})} | custom-call | tf_op jit(solution)/shard_map/final/pallas_call | solution.py:212
  334.2 2.9 final.5
  (24 shorter events, 0.1 us)
Async XLA Ops:
  7.2 59.8 %all-gather.2.cloned.1.call-start = ((), (), s32[]{:S(2)}) async-start(), calls=%async_computation | async-start | bytes 9437184 | tf_op jit(solution)/shard_map/all_gather | solution.py:355
  7.9 7.3 %collective-permute-start.8 = (bf16[3584,512]{1,0:T(8,128)(2,1)}, bf16[3584,512]{1,0:T(8,128)(2,1)}, u32[]{:S(2)}, u32[]{:S(2)}) collective-permute-start(bf16[3584,512]{1,0:T(8,128)(2,1)} %weight_ref.1), channel_id=1, source_target_pairs={{0,4},{4,0},{8,12},{12,8},{16,20},{20,16},{24,28},{28,24},{1,5},{5... | collective-permute-start | bytes 11010056 | tf_op jit(solution)/shard_map/ppermute | solution.py:344
  8.4 14.2 %collective-permute-start.2 = (bf16[512,3584]{1,0:T(8,128)(2,1)}, bf16[512,3584]{1,0:T(8,128)(2,1)}, u32[]{:S(2)}, u32[]{:S(2)}) collective-permute-start(bf16[512,3584]{1,0:T(8,128)(2,1)} %gate_ref.1), channel_id=1, source_target_pairs={{0,4},{4,0},{8,12},{12,8},{16,20},{20,16},{24,28},{28,24},{1,5},{5... | collective-permute-start | bytes 11010056 | tf_op jit(solution)/shard_map/ppermute | solution.py:344
  8.5 19.3 %collective-permute-start.3 = (bf16[512,3584]{1,0:T(8,128)(2,1)}, bf16[512,3584]{1,0:T(8,128)(2,1)}, u32[]{:S(2)}, u32[]{:S(2)}) collective-permute-start(bf16[512,3584]{1,0:T(8,128)(2,1)} %up_ref.1), channel_id=1, source_target_pairs={{0,4},{4,0},{8,12},{12,8},{16,20},{20,16},{24,28},{28,24},{1,5},{5... | collective-permute-start | bytes 11010056 | tf_op jit(solution)/shard_map/ppermute | solution.py:344
  12.6 43.3 %collective-permute-start = (bf16[1792,512]{1,0:T(8,128)(2,1)}, bf16[1792,512]{1,0:T(8,128)(2,1)S(1)}, u32[]{:S(2)}, u32[]{:S(2)}) collective-permute-start(bf16[1792,512]{1,0:T(8,128)(2,1)} %half.2.refs_8_), channel_id=1, source_target_pairs={{0,8},{8,16},{16,24},{24,28},{28,20},{20,12},{12,4},{4,0},{1,9},{9... | collective-permute-start | bytes 5505032 | tf_op jit(solution)/shard_map/ppermute | solution.py:347
  15.2 58.6 %collective-permute-start.1 = (bf16[1792,512]{1,0:T(8,128)(2,1)}, bf16[1792,512]{1,0:T(8,128)(2,1)}, u32[]{:S(2)}, u32[]{:S(2)}) collective-permute-start(bf16[1792,512]{1,0:T(8,128)(2,1)} %half.2.refs_8_), channel_id=1, source_target_pairs={{4,12},{12,20},{20,28},{28,24},{24,16},{16,8},{8,0},{0,4},{5,13},{... | collective-permute-start | bytes 5505032 | tf_op jit(solution)/shard_map/ppermute | solution.py:347
  18.3 76.9 %collective-permute-start.9 = (bf16[1792,512]{1,0:T(8,128)(2,1)}, bf16[1792,512]{1,0:T(8,128)(2,1)}, u32[]{:S(2)}, u32[]{:S(2)}) collective-permute-start(bf16[1792,512]{1,0:T(8,128)(2,1)} %half.3.refs_15_), channel_id=1, source_target_pairs={{0,8},{8,16},{16,24},{24,28},{28,20},{20,12},{12,4},{4,0},{1,9},{9... | collective-permute-start | bytes 5505032 | tf_op jit(solution)/shard_map/ppermute | solution.py:347
  22.6 80.5 %collective-permute-start.10 = (bf16[1792,512]{1,0:T(8,128)(2,1)}, bf16[1792,512]{1,0:T(8,128)(2,1)}, u32[]{:S(2)}, u32[]{:S(2)}) collective-permute-start(bf16[1792,512]{1,0:T(8,128)(2,1)} %half.3.refs_15_), channel_id=1, source_target_pairs={{4,12},{12,20},{20,28},{28,24},{24,16},{16,8},{8,0},{0,4},{5,13},{... | collective-permute-start | bytes 5505032 | tf_op jit(solution)/shard_map/ppermute | solution.py:347
  55.9 11.1 %copy-start.2 = (bf16[1792,512]{1,0:T(8,128)(2,1)}, bf16[1792,512]{1,0:T(8,128)(2,1)S(1)}, u32[]{:S(2)}) copy-start(bf16[1792,512]{1,0:T(8,128)(2,1)S(1)} %collective-permute-done.got_ref.refs_9_) | copy-start | bytes 5505028
  73.7 60.8 %collective-permute-start.6 = (bf16[1792,512]{1,0:T(8,128)(2,1)}, bf16[1792,512]{1,0:T(8,128)(2,1)S(1)}, u32[]{:S(2)}, u32[]{:S(2)}) collective-permute-start(bf16[1792,512]{1,0:T(8,128)(2,1)} %step.16), channel_id=1, source_target_pairs={{0,8},{8,16},{16,24},{24,28},{28,20},{20,12},{12,4},{4,0},{1,9},{9... | collective-permute-start | bytes 5505032 | tf_op jit(solution)/shard_map/ppermute | solution.py:347
  79.1 65.7 %collective-permute-start.4 = (bf16[1792,512]{1,0:T(8,128)(2,1)}, bf16[1792,512]{1,0:T(8,128)(2,1)S(1)}, u32[]{:S(2)}, u32[]{:S(2)}) collective-permute-start(bf16[1792,512]{1,0:T(8,128)(2,1)} %step.14), channel_id=1, source_target_pairs={{4,12},{12,20},{20,28},{28,24},{24,16},{16,8},{8,0},{0,4},{5,13},{... | collective-permute-start | bytes 5505032 | tf_op jit(solution)/shard_map/ppermute | solution.py:347
  101.9 72.0 %collective-permute-start.13 = (bf16[1792,512]{1,0:T(8,128)(2,1)}, bf16[1792,512]{1,0:T(8,128)(2,1)}, u32[]{:S(2)}, u32[]{:S(2)}) collective-permute-start(bf16[1792,512]{1,0:T(8,128)(2,1)} %step.20), channel_id=1, source_target_pairs={{0,8},{8,16},{16,24},{24,28},{28,20},{20,12},{12,4},{4,0},{1,9},{9... | collective-permute-start | bytes 5505032 | tf_op jit(solution)/shard_map/ppermute | solution.py:347
  108.4 74.6 %collective-permute-start.11 = (bf16[1792,512]{1,0:T(8,128)(2,1)}, bf16[1792,512]{1,0:T(8,128)(2,1)}, u32[]{:S(2)}, u32[]{:S(2)}) collective-permute-start(bf16[1792,512]{1,0:T(8,128)(2,1)} %step.18), channel_id=1, source_target_pairs={{4,12},{12,20},{20,28},{28,24},{24,16},{16,8},{8,0},{0,4},{5,13},{... | collective-permute-start | bytes 5505032 | tf_op jit(solution)/shard_map/ppermute | solution.py:347
  134.5 1.3 copy-start.3
  142.5 70.7 %collective-permute-start.7 = (bf16[1792,512]{1,0:T(8,128)(2,1)}, bf16[1792,512]{1,0:T(8,128)(2,1)}, u32[]{:S(2)}, u32[]{:S(2)}) collective-permute-start(bf16[1792,512]{1,0:T(8,128)(2,1)} %step.17), channel_id=1, source_target_pairs={{0,8},{8,16},{16,24},{24,28},{28,20},{20,12},{12,4},{4,0},{1,9},{9... | collective-permute-start | bytes 5505032 | tf_op jit(solution)/shard_map/ppermute | solution.py:347
  144.9 1.2 copy-start.4
  151.4 70.9 %collective-permute-start.5 = (bf16[1792,512]{1,0:T(8,128)(2,1)}, bf16[1792,512]{1,0:T(8,128)(2,1)}, u32[]{:S(2)}, u32[]{:S(2)}) collective-permute-start(bf16[1792,512]{1,0:T(8,128)(2,1)} %step.15), channel_id=1, source_target_pairs={{4,12},{12,20},{20,28},{28,24},{24,16},{16,8},{8,0},{0,4},{5,13},{... | collective-permute-start | bytes 5505032 | tf_op jit(solution)/shard_map/ppermute | solution.py:347
  180.5 72.0 %collective-permute-start.14 = (bf16[1792,512]{1,0:T(8,128)(2,1)}, bf16[1792,512]{1,0:T(8,128)(2,1)S(1)}, u32[]{:S(2)}, u32[]{:S(2)}) collective-permute-start(bf16[1792,512]{1,0:T(8,128)(2,1)} %step.21), channel_id=1, source_target_pairs={{0,8},{8,16},{16,24},{24,28},{28,20},{20,12},{12,4},{4,0},{1,9},{9... | collective-permute-start | bytes 5505032 | tf_op jit(solution)/shard_map/ppermute | solution.py:347
  188.4 71.3 %collective-permute-start.12 = (bf16[1792,512]{1,0:T(8,128)(2,1)}, bf16[1792,512]{1,0:T(8,128)(2,1)S(1)}, u32[]{:S(2)}, u32[]{:S(2)}) collective-permute-start(bf16[1792,512]{1,0:T(8,128)(2,1)} %step.19), channel_id=1, source_target_pairs={{4,12},{12,20},{20,28},{28,24},{24,16},{16,8},{8,0},{0,4},{5,13},{... | collective-permute-start | bytes 5505032 | tf_op jit(solution)/shard_map/ppermute | solution.py:347
  219.9 89.9 %collective-permute-start.16 = (bf16[1792,512]{1,0:T(8,128)(2,1)}, bf16[1792,512]{1,0:T(8,128)(2,1)}, u32[]{:S(2)}, u32[]{:S(2)}) collective-permute-start(bf16[1792,512]{1,0:T(8,128)(2,1)} %step.22.refs_22_), channel_id=1, source_target_pairs={{0,8},{8,16},{16,24},{24,28},{28,20},{20,12},{12,4},{4,0},{1,9},{9... | collective-permute-start | bytes 5505032 | tf_op jit(solution)/shard_map/ppermute | solution.py:347
  227.7 84.7 %collective-permute-start.17 = (bf16[1792,512]{1,0:T(8,128)(2,1)}, bf16[1792,512]{1,0:T(8,128)(2,1)}, u32[]{:S(2)}, u32[]{:S(2)}) collective-permute-start(bf16[1792,512]{1,0:T(8,128)(2,1)} %step.24.refs_24_), channel_id=1, source_target_pairs={{4,12},{12,20},{20,28},{28,24},{24,16},{16,8},{8,0},{0,4},{5,13},{... | collective-permute-start | bytes 5505032 | tf_op jit(solution)/shard_map/ppermute | solution.py:347
  252.5 1.3 copy-start
  259.7 1.2 copy-start.1
  265.8 16.5 %copy-start.5 = (bf16[1344,512]{1,0:T(8,128)(2,1)S(1)}, bf16[1344,512]{1,0:T(8,128)(2,1)}, u32[]{:S(2)}) copy-start(bf16[1344,512]{1,0:T(8,128)(2,1)} %step.23.refs_23_) | copy-start | bytes 4128772
  265.8 19.9 %copy-start.6 = (bf16[1344,512]{1,0:T(8,128)(2,1)S(1)}, bf16[1344,512]{1,0:T(8,128)(2,1)}, u32[]{:S(2)}) copy-start(bf16[1344,512]{1,0:T(8,128)(2,1)} %step.25.refs_25_) | copy-start | bytes 4128772
  282.2 37.4 %collective-permute-start.15 = (bf16[512,1792]{1,0:T(8,128)(2,1)}, bf16[512,1792]{1,0:T(8,128)(2,1)}, u32[]{:S(2)}, u32[]{:S(2)}) collective-permute-start(bf16[512,1792]{1,0:T(8,128)(2,1)} %get-tuple-element.14), channel_id=1, source_target_pairs={{0,4},{4,0},{8,12},{12,8},{16,20},{20,16},{24,28},{28,24},{1,5},{5... | collective-permute-start | bytes 5505032 | tf_op jit(solution)/shard_map/ppermute | solution.py:344
  282.3 45.0 %collective-permute-start.20 = (bf16[1344,512]{1,0:T(8,128)(2,1)S(1)}, bf16[1344,512]{1,0:T(8,128)(2,1)S(1)}, u32[]{:S(2)}, u32[]{:S(2)}) collective-permute-start(bf16[1344,512]{1,0:T(8,128)(2,1)S(1)} %copy-done.5), channel_id=1, source_target_pairs={{0,8},{8,16},{16,24},{24,28},{28,20},{20,12},{12,4},{4,0},{1,9},{9... | collective-permute-start | bytes 4128776 | tf_op jit(solution)/shard_map/ppermute | solution.py:347
  285.6 41.6 %collective-permute-start.21 = (bf16[1344,512]{1,0:T(8,128)(2,1)S(1)}, bf16[1344,512]{1,0:T(8,128)(2,1)}, u32[]{:S(2)}, u32[]{:S(2)}) collective-permute-start(bf16[1344,512]{1,0:T(8,128)(2,1)S(1)} %copy-done.6), channel_id=1, source_target_pairs={{4,12},{12,20},{20,28},{28,24},{24,16},{16,8},{8,0},{0,4},{5,13},{... | collective-permute-start | bytes 4128776 | tf_op jit(solution)/shard_map/ppermute | solution.py:347
  309.8 24.5 %collective-permute-start.18 = (bf16[448,512]{1,0:T(8,128)(2,1)}, bf16[448,512]{1,0:T(8,128)(2,1)}, u32[]{:S(2)}, u32[]{:S(2)}) collective-permute-start(bf16[448,512]{1,0:T(8,128)(2,1)} %step.26), channel_id=1, source_target_pairs={{0,8},{8,16},{16,24},{24,28},{28,20},{20,12},{12,4},{4,0},{1,9},{9... | collective-permute-start | bytes 1376264 | tf_op jit(solution)/shard_map/ppermute | solution.py:347
  312.4 21.8 %collective-permute-start.19 = (bf16[448,512]{1,0:T(8,128)(2,1)}, bf16[448,512]{1,0:T(8,128)(2,1)}, u32[]{:S(2)}, u32[]{:S(2)}) collective-permute-start(bf16[448,512]{1,0:T(8,128)(2,1)} %step.27), channel_id=1, source_target_pairs={{4,12},{12,20},{20,28},{28,24},{24,16},{16,8},{8,0},{0,4},{5,13},{... | collective-permute-start | bytes 1376264 | tf_op jit(solution)/shard_map/ppermute | solution.py:347
  327.2 1.1 copy-start.7
Sparse Core Ops, SparseCore 0:
  9.9 57.0 all-gather.1

commit v3 on v2

--- a/solution.py
+++ b/solution.py
@@ -9,13 +9,12 @@
 from jax.sharding import PartitionSpec as P
 
 VMEM = 60 * 1024 * 1024
-COPIES = 4
 STEP_FLOPS = 2e9
 F32, BF16 = jnp.float32, jnp.bfloat16
 ANY = pl.BlockSpec(memory_space=pl.ANY)
 
 
-def call(kernel, grid, in_specs, out_specs, out_shape, name, aliases=None, flops=0, scratch=()):
+def call(kernel, grid, in_specs, out_specs, out_shape, name, aliases=None, flops=0):
     return pl.pallas_call(
         kernel,
         grid_spec=pltpu.PrefetchScalarGridSpec(
@@ -23,7 +22,6 @@
             grid=grid,
             in_specs=in_specs,
             out_specs=out_specs,
-            scratch_shapes=scratch,
         ),
         out_shape=out_shape,
         input_output_aliases=aliases or {},
@@ -43,47 +41,26 @@
     return lax.dot_general(a, b, (contract, ((), ())), preferred_element_type=F32)
 
 
-def half_kernel(place, weight_ref, out_ref, held, load_sem, store_sem):
-    half = out_ref.shape[0]
-    part = half // COPIES
-    start = place[1] * half
-
-    def load(i):
-        source = pl.multiple_of(start + i * part, part)
-        here = pl.ds(i * part, part)
-        return pltpu.make_async_copy(
-            weight_ref.at[pl.ds(source, part), :], held.at[here, :], load_sem.at[i]
-        )
-
-    def store(i):
-        here = pl.ds(i * part, part)
-        return pltpu.make_async_copy(held.at[here, :], out_ref.at[here, :], store_sem.at[i])
-
-    for i in range(COPIES):
-        load(i).start()
-    for i in range(COPIES):
-        load(i).wait()
-        store(i).start()
-    for i in range(COPIES):
-        store(i).wait()
-
-
-def half_call(place, weight):
-    units, block = weight.shape
-    half = units // 2
-    return call(
-        half_kernel,
-        (1,),
-        [ANY],
-        ANY,
-        jax.ShapeDtypeStruct((half, block), BF16),
-        "half",
-        scratch=[
-            pltpu.VMEM((half, block), BF16),
-            pltpu.SemaphoreType.DMA((COPIES,)),
-            pltpu.SemaphoreType.DMA((COPIES,)),
+def spread_kernel(place, even_ref, odd_ref, out_ref):
+    peers = out_ref.shape[0] // 2
+    for core, ref in enumerate((even_ref, odd_ref)):
+        for peer in range(peers):
+            out_ref[core * peers + peer] = ref[...]
+
+
+def spread_call(place, out_grad, peers, line, block):
+    rows = out_grad.shape[0]
+    return call(
+        spread_kernel,
+        (line,),
+        [
+            pl.BlockSpec((rows, block), lambda b, s: (0, 2 * b)),
+            pl.BlockSpec((rows, block), lambda b, s: (0, 2 * b + 1)),
         ],
-    )(place, weight)
+        pl.BlockSpec((peers, rows, block), lambda b, s: (0, 0, b)),
+        jax.ShapeDtypeStruct((peers, rows, line * block), BF16),
+        "spread",
+    )(place, out_grad, out_grad)
 
 
 def hidden_kernel(place, gate_own, up_own, gate_sib, up_sib, out_ref):
@@ -116,7 +93,7 @@
 
 def term_specs(tile, tokens, block, first, ahead, line):
     def column(i, s):
-        return 0, 2 * lax.rem(s[0] + ahead(s), line) + s[1]
+        return 0, lax.rem(s[0] + ahead(s), line)
 
     return [
         pl.BlockSpec((tile, tokens), lambda i, s: (first + i, 0)),
@@ -206,9 +183,12 @@
 
 def final_call(place, one, two, own, quarter, line, scale, before, after):
     rows, block = one.shape
-    tile = own.shape[0] // 16
+    tile = own.shape[0] // 8
+    if rows == tile:
+        tile //= 2
+    first = quarter * (own.shape[0] // 8) // tile
     got = pl.BlockSpec((tile, block), lambda i, s: (i, 0))
-    here = pl.BlockSpec((tile, block), lambda i, s: (2 * quarter + i, 0))
+    here = pl.BlockSpec((tile, block), lambda i, s: (first + i, 0))
     return call(
         functools.partial(final_kernel, scale, line),
         (rows // tile,),
@@ -220,16 +200,17 @@
     )(place, one, two, own, *before, *after)
 
 
-def half_product(line, place, grads, weights):
-    count = len(weights) // 2
+def half_product(line, slots, place, grads, weights, before):
     at = along(place, 0, line)
-    d_hidden = None
-    for chain in range(2):
-        for slot in range(line):
-            weight = weights[chain * count + max(0, 2 * slot - 1)][...]
+    d_hidden = before[...] if before is not None else None
+    weights, grads = iter(weights), iter(grads)
+    for _ in range(2):
+        for slot in slots:
+            weight = next(weights)[...]
             if slot:
-                weight = jnp.where(at >= slot, weight, weights[chain * count + 2 * slot][...])
-            part = dot(grads[chain * line + slot][...], weight, ((1,), (1,)))
+                other = next(weights)
+                weight = jnp.where(at >= slot, weight, other[...])
+            part = dot(next(grads)[...], weight, ((1,), (1,)))
             d_hidden = part if d_hidden is None else d_hidden + part
     return d_hidden
 
@@ -242,63 +223,64 @@
     up_out[...] = (d_hidden * (gate * sig)).astype(BF16)
 
 
-def product_kernel(line, count, place, *refs):
-    d_hidden = half_product(line, place, refs[: 2 * line], refs[2 * line : 2 * line + count])
-    out_ref, token = refs[-2:]
-    out_ref[...] = d_hidden.astype(BF16)
+def product_kernel(line, slots, counts, place, *refs):
+    n_grads, n_weights, n_before, n_gate = counts
+    grads, refs = refs[:n_grads], refs[n_grads:]
+    weights, refs = refs[:n_weights], refs[n_weights:]
+    before = refs[0] if n_before else None
+    d_hidden = half_product(line, slots, place, grads, weights, before)
+    gate_up = refs[n_before : n_before + n_gate]
+    *outs, token = refs[-2 - (n_gate > 0) :]
+    if gate_up:
+        store_grads(d_hidden, *gate_up, *outs)
+    else:
+        outs[0][...] = d_hidden.astype(outs[0].dtype)
     token[...] = jnp.zeros_like(token)
 
 
-def grads_kernel(line, count, place, *refs):
-    d_hidden = half_product(line, place, refs[: 2 * line], refs[2 * line : 2 * line + count])
-    gate_ref, up_ref = refs[2 * line + count : 2 * line + count + 2]
-    gate_out, up_out, token = refs[-3:]
-    store_grads(d_hidden, gate_ref, up_ref, gate_out, up_out)
-    token[...] = jnp.zeros_like(token)
-
-
-def product_call(place, grads, weights, gate_up, flip, line, after):
+def product_call(place, grads, weights, slots, before, gate_up, dtype, flip, line, name, after):
     half, block = weights[0].shape
-    tokens = grads.shape[0] // 2
+    tokens = grads[0].shape[0] // 2
     tile = column_tile(half, 512)
     steps = half // tile
     here = pl.BlockSpec((tokens, tile), lambda i, s: (0, s[1] * steps + i))
-
-    def row_spec(chain, slot):
+    short = pl.BlockSpec((tokens, tile), lambda i, s: (0, i))
+
+    def row_spec(slot):
         def block_of(i, s):
             source = lax.rem(s[0] + jnp.where(s[1] == 0, line - slot, slot), line)
-            return s[1] ^ flip, 2 * source + (s[1] ^ chain)
+            return s[1] ^ flip, source
 
         return pl.BlockSpec((tokens, block), block_of)
 
-    def weight_spec(index):
-        index = index % (2 * line - 1)
-        slot, flow = (index + 1) // 2, (index + 1) % 2
-
+    def weight_spec(slot, flow):
         def block_of(i, s):
-            if index == 0:
-                return i, 0
             return jnp.where((along(s, 0, line) >= slot) == (flow == 0), i, 0), 0
 
-        return pl.BlockSpec((tile, block), block_of)
-
+        return pl.BlockSpec((tile, block), block_of if slot else lambda i, s: (i, 0))
+
+    weight_specs = []
+    for _ in range(2):
+        for slot in slots:
+            weight_specs += [weight_spec(slot, flow) for flow in range(2 if slot else 1)]
     if gate_up:
-        kernel, outs = grads_kernel, [here, here]
-        shapes = [jax.ShapeDtypeStruct(gate_up[0].shape, BF16)] * 2
+        outs, shapes = [here, here], [jax.ShapeDtypeStruct(gate_up[0].shape, BF16)] * 2
     else:
-        kernel, outs = product_kernel, [pl.BlockSpec((tokens, tile), lambda i, s: (0, i))]
-        shapes = [jax.ShapeDtypeStruct((tokens, half), BF16)]
-    return call(
-        functools.partial(kernel, line, len(weights)),
+        outs, shapes = [short], [jax.ShapeDtypeStruct((tokens, half), dtype)]
+    row_specs = [row_spec(slot) for _ in range(2) for slot in slots]
+    counts = (len(row_specs), len(weights), len(before), len(gate_up))
+    return call(
+        functools.partial(product_kernel, line, slots, counts),
         (steps,),
-        [row_spec(chain, slot) for chain in range(2) for slot in range(line)]
-        + [weight_spec(index) for index in range(len(weights))]
+        row_specs
+        + weight_specs
+        + [short] * len(before)
         + [here] * len(gate_up)
         + [ANY] * len(after),
         outs + [pl.BlockSpec((8, 128), lambda i, s: (0, 0))],
         shapes + [jax.ShapeDtypeStruct((8, 128), F32)],
-        "grads" if gate_up else "product",
-    )(place, *[grads] * (2 * line), *weights, *gate_up, *after)
+        name,
+    )(place, *[grads[0]] * len(slots), *[grads[1]] * len(slots), *weights, *before, *gate_up, *after)
 
 
 def join_kernel(place, product_ref, gate_ref, up_ref, *rest):
@@ -308,7 +290,7 @@
 
 def join_call(place, product, gate, up, gate_all, up_all, after):
     tokens, half = product.shape
-    tile = column_tile(half, 512)
+    tile = column_tile(half, 896)
     steps = half // tile
     there = pl.BlockSpec((tokens, tile), lambda i, s: (0, (1 - s[1]) * steps + i))
     return call(
@@ -346,15 +328,22 @@
     def send(x, flow):
         return lax.ppermute(x, "dp", rings[flow])
 
-    first = [half_call(place, down_weight), half_call(place, swap(down_weight))]
+    half = units // 2
+
+    def own_half(weight):
+        return lax.dynamic_slice_in_dim(weight, index % 2 * half, half, axis=0)
+
+    first = [own_half(down_weight), own_half(swap(down_weight))]
     got = [[[send(x, flow) for x in first]] for flow in range(2)]
 
     groups = [
         [(2 * z + c) * n_mp + m for c in range(2) for m in range(n_mp)] for z in range(line)
     ]
-    out_grads = lax.all_gather(
-        out_grad, ("dp", "mp"), axis=0, tiled=True, axis_index_groups=groups
-    )
+    spread = spread_call(place, out_grad, 2 * n_mp, line, block)
+    out_grads = lax.all_to_all(
+        spread, ("dp", "mp"), split_axis=0, concat_axis=0, tiled=True, axis_index_groups=groups
+    ).reshape(2 * tokens, line * block)
+    both_grads = (out_grads, swap(out_grads))
     gate_sib, up_sib = swap(gate_pre), swap(up_pre)
     hidden = hidden_call(place, gate_pre, up_pre, gate_sib, up_sib)
 
@@ -368,32 +357,60 @@
         for flow in range(2):
             got[flow].append([send(x, flow) for x in sent[flow]])
 
+    def weights_of(slots):
+        weights = []
+        for k in range(2):
+            for slot in slots:
+                if slot:
+                    weights += [got[0][slot - 1][k], got[1][line - slot - 1][k]]
+                else:
+                    weights.append(first[k])
+        return weights
+
+    early_slots = [slot for slot in range(line) if slot not in (1, line - 1)]
+    late_slots = [slot for slot in range(line) if slot not in early_slots]
+    early = [
+        product_call(
+            place, both_grads, weights_of(early_slots), early_slots, (), (), F32, flip, line, "early", ()
+        )
+        for flip in (1, 0)
+    ]
+
     own = own_call(place, hidden, out_grads, block, line)
     sent = [
-        [step(line, flow, 0, (0, 4), (own,)), step(line, flow, 1, (0, 3))] for flow in range(2)
+        [
+            step(line, flow, 0, (0, 4), (own,)),
+            step(line, flow, 1, (0, 3), (early[0][1], early[1][1])),
+        ]
+        for flow in range(2)
     ]
     last = [[send(x, flow) for x in sent[flow]] for flow in range(2)]
     sent = sent[0] + sent[1]
 
-    weights = []
-    for k in range(2):
-        weights.append(first[k])
-        for slot in range(1, line):
-            weights += [got[0][slot - 1][k], got[1][line - slot - 1][k]]
-    product, token = product_call(place, out_grads, weights, (), 1, line, sent)
+    late = weights_of(late_slots)
+    product, token = product_call(
+        place, both_grads, late, late_slots, (early[0][0],), (), BF16, 1, line, "product", sent
+    )
     from_sib = swap(product)
-    own_half = (gate_pre, up_pre)
-    *grads, token = product_call(place, out_grads, weights, own_half, 0, line, [token])
+    *grads, token = product_call(
+        place, both_grads, late, late_slots, (early[1][0],), (gate_pre, up_pre), None, 0, line, "grads", [token]
+    )
 
     for flow in range(2):
         last[flow].append(send(step(line, flow, 1, (3, 4), (token,)), flow))
     one, two = last
     grad_down, token = final_call(place, one[0], two[0], own, 0, line, scale, (), (token,))
     grads = join_call(place, from_sib, gate_pre, up_pre, *grads, [token])
-    for piece, quarter in ((1, 4), (2, 7)):
-        grad_down, _ = final_call(
-            place, one[piece], two[piece], own, quarter, line, scale, (grad_down,), tuple(grads)
-        )
+    grad_down, _ = final_call(
+        place, one[1], two[1], own, 4, line, scale, (grad_down,), tuple(grads)
+    )
+    at = along(place, 0, line)
+    start = units - units // 8
+    total = own[start:].astype(F32)
+    total += jnp.where(at > 0, one[2].astype(F32), 0.0)
+    total += jnp.where(at < line - 1, two[2].astype(F32), 0.0)
+    piece = (total * scale).astype(BF16)
+    grad_down = lax.dynamic_update_slice_in_dim(grad_down, piece, start, axis=0)
     return (*grads, grad_down)
 
 

time: 346 us -> 336 us (0.971)
  between operations: 14.1 us -> 0.71 us
  waiting for transfers between devices: 133 us -> 123 us
  starting transfers between devices: 23.5 us -> 28.7 us
    pallas_call x4 -> x5, Pallas kernels: 39.6 us -> 50.8 us  [the longest x4 46 us: product_call(): call(functools.partial(product_kernel, line, slots, counts), (steps,), ro...]
    all_gather x1 -> x0, waiting for transfers between devices: 11.1 us -> none  [shards(): lax.all_gather(out_grad, ('dp', 'mp'), axis=0, tiled=True, axis_index_gro...]
    ppermute x4 -> x5, waiting for transfers between devices: 6.91 us -> 0.01 us  [swap(): return lax.ppermute(x, 'dp', swap_pairs)]
    pallas_call x3 -> x2, Pallas kernels: 15.9 us -> 9.9 us  [final_call(): call(functools.partial(final_kernel, scale, line), (rows // tile,), [got,...]
    all_to_all x0 -> x1, waiting for transfers between devices: none -> 5.46 us  [shards(): lax.all_to_all(spread, ('dp', 'mp'), split_axis=0, concat_axis=0, tiled=T...]
    all_to_all x0 -> x1, starting transfers between devices: none -> 4.85 us  [shards(): lax.all_to_all(spread, ('dp', 'mp'), split_axis=0, concat_axis=0, tiled=T...]
    dynamic_slice x0 -> x2, local copies, waits for them, and re-layouts: none -> 4.43 us  [own_half(): return lax.dynamic_slice_in_dim(weight, index % 2 * half, half, axis=0)]
  transfers between devices with their start and end apart: 23 -> 24, of which waited for: 9 -> 10; matrix products, arithmetic and copies ran while one was open for 0% -> 2% of each run, Pallas kernels for 48% -> 51%
where the time goes in v3:
time: 336 us; the launch traced here: 333 us
  Pallas kernels  169 us (50%)
  waiting for transfers between devices  123 us (37%)
  starting transfers between devices  28.7 us (9%)
  local copies, waits for them, and re-layouts  9.43 us (3%)
    ppermute x18, waiting for transfers between devices, send(): return lax.ppermute(x, 'dp', rings[flow])  117 us
    pallas_call x14, Pallas kernels, step_call(): call(functools.partial(step_kernel, flow, j, line), (high - low,), [pl.Bl...  77.9 us
    pallas_call x4, Pallas kernels, product_call(): call(functools.partial(product_kernel, line, slots, counts), (steps,), ro...  46 us
    ppermute x18, starting transfers between devices, send(): return lax.ppermute(x, 'dp', rings[flow])  22.2 us
    pallas_call x1, Pallas kernels, hidden_call(): call(hidden_kernel, (units // tile,), [pl.BlockSpec((tokens, tile), lambd...  14.5 us
    pallas_call x1, Pallas kernels, own_call(): call(own_kernel, (steps,), term_specs(tile, tokens, block, 0, lambda s: 0...  10.5 us
    pallas_call x2, Pallas kernels, final_call(): call(functools.partial(final_kernel, scale, line), (rows // tile,), [got,...  9.9 us
  transfers between devices with their start and end apart: 24, of which 10 were waited for; matrix products, arithmetic and copies ran while one was open for 2% of the time, Pallas kernels for 51%

profile of v3, /device:TPU:0, one launch (start us, length us, event | category | flops | bytes accessed | tf_op | source)
XLA Modules:
  0.0 333.4 jit_solution(300204624406500784)
XLA Ops:
  0.6 0.5 collective-permute-start.9
  1.1 0.1 collective-permute-start.3
  1.2 0.4 collective-permute-start.4
  1.7 0.6 pad_add_fusion.place
  2.3 4.8 %spread.1 = bf16[8,128,2048]{2,1,0:T(8,128)(2,1)} custom-call(s32[2]{0:T(128)} %pad_add_fusion.place, bf16[128,4096]{1,0:T(8,128)(2,1)} %odd_ref.1, bf16[128,4096]{1,0:T(8,128)(2,1)} %odd_ref.1), custom_call_target="tpu_custom_call" | custom-call | tf_op jit(solution)/shard_map/spread/pallas_call | solution.py:53
  7.1 4.8 %all-to-all-start = ((bf16[8,128,2048]{2,1,0:T(8,128)(2,1)}), bf16[8,128,2048]{2,1,0:T(8,128)(2,1)}, u32[]{:S(2)}, u32[]{:S(2)}) async-start(bf16[8,128,2048]{2,1,0:T(8,128)(2,1)} %spread.1), calls=%async_computation | async-start | bytes 8388608 | tf_op jit(solution)/shard_map/all_to_all | solution.py:343
  12.0 1.6 constant_dynamic-slice_fusion.1.refs_4_
  13.6 0.5 collective-permute-start.2
  14.1 1.9 collective-permute-start.1
  16.1 2.8 constant_dynamic-slice_fusion.refs_7_
  18.9 0.1 collective-permute-start.11
  19.0 2.0 collective-permute-start.10
  20.9 14.5 %hidden.1.hidden_ref = bf16[3584,1024]{1,0:T(8,128)(2,1)} custom-call(s32[2]{0:T(128)} %pad_add_fusion.place, bf16[512,3584]{1,0:T(8,128)(2,1)} %gate_ref.1, bf16[512,3584]{1,0:T(8,128)(2,1)} %up_ref.1, bf16[512,3584]{1,0:T(8,128)(2,1)} %collective-permute-done.3.gate_sib, bf16[512,3584]{1,0:T(8,128)(2,1)} %collective-permute-done.4.up_sib), custom_call_target="tpu_custom_call" | custom-call | tf_op jit(solution)/shard_map/hidden/pallas_call | solution.py:80
  35.5 20.4 %collective-permute-done.2.got_ref.refs_7_ = bf16[1792,512]{1,0:T(8,128)(2,1)} collective-permute-done((bf16[1792,512]{1,0:T(8,128)(2,1)S(1)}, bf16[1792,512]{1,0:T(8,128)(2,1)}, u32[]{:S(2)}, u32[]{:S(2)}) %collective-permute-start.2) | collective-permute-done | bytes 1835040 | tf_op jit(solution)/shard_map/ppermute | solution.py:329
  55.8 5.5 %all-to-all-done = bf16[8,128,2048]{2,1,0:T(8,128)(2,1)} async-done(((bf16[8,128,2048]{2,1,0:T(8,128)(2,1)}), bf16[8,128,2048]{2,1,0:T(8,128)(2,1)}, u32[]{:S(2)}, u32[]{:S(2)}) %all-to-all-start) | async-done | bytes 4194336 | tf_op jit(solution)/shard_map/all_to_all | solution.py:343
  61.3 5.3 %step.14 = bf16[1792,512]{1,0:T(8,128)(2,1)} custom-call(s32[2]{0:T(128)} %pad_add_fusion.place, bf16[1792,512]{1,0:T(8,128)(2,1)} %collective-permute-done.2.got_ref.refs_7_, bf16[3584,1024]{1,0:T(8,128)(2,1)} %hidden.1.hidden_ref, bf16[1024,2048]{1,0:T(8,128)(2,1)} %bitcast.2.grad_ref.refs_0_.refs_1_), custom_call_target="tpu_custom_call" | custom-call | flops 2000000000 | tf_op jit(solution)/shard_map/step/pallas_call | solution.py:129
  66.6 1.5 collective-permute-start.5
  68.1 6.7 %step.16 = bf16[1792,512]{1,0:T(8,128)(2,1)} custom-call(s32[2]{0:T(128)} %pad_add_fusion.place, bf16[1792,512]{1,0:T(8,128)(2,1)} %collective-permute-done.1.got_ref.refs_4_, bf16[3584,1024]{1,0:T(8,128)(2,1)} %hidden.1.hidden_ref, bf16[1024,2048]{1,0:T(8,128)(2,1)} %bitcast.2.grad_ref.refs_0_.refs_1_), custom_call_target="tpu_custom_call" | custom-call | flops 2000000000 | tf_op jit(solution)/shard_map/step/pallas_call | solution.py:129
  74.8 0.5 collective-permute-start
  75.3 19.9 %collective-permute-done.11.got_ref.refs_11_ = bf16[1792,512]{1,0:T(8,128)(2,1)} collective-permute-done((bf16[1792,512]{1,0:T(8,128)(2,1)}, bf16[1792,512]{1,0:T(8,128)(2,1)}, u32[]{:S(2)}, u32[]{:S(2)}) %collective-permute-start.11) | collective-permute-done | bytes 1835040 | tf_op jit(solution)/shard_map/ppermute | solution.py:329
  95.2 5.4 %step.18 = bf16[1792,512]{1,0:T(8,128)(2,1)} custom-call(s32[2]{0:T(128)} %pad_add_fusion.place, bf16[1792,512]{1,0:T(8,128)(2,1)} %collective-permute-done.11.got_ref.refs_11_, bf16[3584,1024]{1,0:T(8,128)(2,1)} %hidden.1.hidden_ref, bf16[1024,2048]{1,0:T(8,128)(2,1)} %bitcast.2.grad_ref.refs_0_.refs_1_), custom_call_target="tpu_custom_call" | custom-call | flops 2000000000 | tf_op jit(solution)/shard_map/step/pallas_call | solution.py:129
  100.5 1.0 collective-permute-start.12
  101.5 6.7 %step.20 = bf16[1792,512]{1,0:T(8,128)(2,1)} custom-call(s32[2]{0:T(128)} %pad_add_fusion.place, bf16[1792,512]{1,0:T(8,128)(2,1)} %collective-permute-done.10.got_ref.refs_8_, bf16[3584,1024]{1,0:T(8,128)(2,1)} %hidden.1.hidden_ref, bf16[1024,2048]{1,0:T(8,128)(2,1)} %bitcast.2.grad_ref.refs_0_.refs_1_), custom_call_target="tpu_custom_call" | custom-call | flops 2000000000 | tf_op jit(solution)/shard_map/step/pallas_call | solution.py:129
  108.2 0.2 collective-permute-start.14
  108.4 26.0 %collective-permute-done.5.got_ref.refs_6_ = bf16[1792,512]{1,0:T(8,128)(2,1)S(1)} collective-permute-done((bf16[1792,512]{1,0:T(8,128)(2,1)}, bf16[1792,512]{1,0:T(8,128)(2,1)S(1)}, u32[]{:S(2)}, u32[]{:S(2)}) %collective-permute-start.5) | collective-permute-done | bytes 1835040 | tf_op jit(solution)/shard_map/ppermute | solution.py:329
  134.4 1.2 copy-done.2
  135.6 5.3 %step.15 = bf16[1792,512]{1,0:T(8,128)(2,1)} custom-call(s32[2]{0:T(128)} %pad_add_fusion.place, bf16[1792,512]{1,0:T(8,128)(2,1)} %copy-done.2, bf16[3584,1024]{1,0:T(8,128)(2,1)} %hidden.1.hidden_ref, bf16[1024,2048]{1,0:T(8,128)(2,1)} %bitcast.2.grad_ref.refs_0_.refs_1_), custom_call_target="tpu_custom_call" | custom-call | flops 2000000000 | tf_op jit(solution)/shard_map/step/pallas_call | solution.py:129
  140.9 1.1 collective-permute-start.6
  142.1 1.2 copy-done.3
  143.3 6.7 %step.17 = bf16[1792,512]{1,0:T(8,128)(2,1)} custom-call(s32[2]{0:T(128)} %pad_add_fusion.place, bf16[1792,512]{1,0:T(8,128)(2,1)} %copy-done.3, bf16[3584,1024]{1,0:T(8,128)(2,1)} %hidden.1.hidden_ref, bf16[1024,2048]{1,0:T(8,128)(2,1)} %bitcast.2.grad_ref.refs_0_.refs_1_), custom_call_target="tpu_custom_call" | custom-call | flops 2000000000 | tf_op jit(solution)/shard_map/step/pallas_call | solution.py:129
  150.0 1.4 collective-permute-start.8
  151.4 22.4 %collective-permute-done.12.got_ref.refs_9_ = bf16[1792,512]{1,0:T(8,128)(2,1)} collective-permute-done((bf16[1792,512]{1,0:T(8,128)(2,1)}, bf16[1792,512]{1,0:T(8,128)(2,1)}, u32[]{:S(2)}, u32[]{:S(2)}) %collective-permute-start.12) | collective-permute-done | bytes 1835040 | tf_op jit(solution)/shard_map/ppermute | solution.py:329
  173.8 5.3 %step.19 = bf16[1792,512]{1,0:T(8,128)(2,1)} custom-call(s32[2]{0:T(128)} %pad_add_fusion.place, bf16[1792,512]{1,0:T(8,128)(2,1)} %collective-permute-done.12.got_ref.refs_9_, bf16[3584,1024]{1,0:T(8,128)(2,1)} %hidden.1.hidden_ref, bf16[1024,2048]{1,0:T(8,128)(2,1)} %bitcast.2.grad_ref.refs_0_.refs_1_), custom_call_target="tpu_custom_call" | custom-call | flops 2000000000 | tf_op jit(solution)/shard_map/step/pallas_call | solution.py:129
  179.1 1.0 collective-permute-start.13
  180.2 6.7 %step.21 = bf16[1792,512]{1,0:T(8,128)(2,1)} custom-call(s32[2]{0:T(128)} %pad_add_fusion.place, bf16[1792,512]{1,0:T(8,128)(2,1)} %collective-permute-done.14.got_ref.refs_8_, bf16[3584,1024]{1,0:T(8,128)(2,1)} %hidden.1.hidden_ref, bf16[1024,2048]{1,0:T(8,128)(2,1)} %bitcast.2.grad_ref.refs_0_.refs_1_), custom_call_target="tpu_custom_call" | custom-call | flops 2000000000 | tf_op jit(solution)/shard_map/step/pallas_call | solution.py:129
  186.8 1.5 collective-permute-start.15
  188.4 10.5 %own.1.rest_0_.own_ref = bf16[3584,512]{1,0:T(8,128)(2,1)} custom-call(s32[2]{0:T(128)} %pad_add_fusion.place, bf16[3584,1024]{1,0:T(8,128)(2,1)} %hidden.1.hidden_ref, bf16[1024,2048]{1,0:T(8,128)(2,1)} %bitcast.2.grad_ref.refs_0_.refs_1_), custom_call_target="tpu_custom_call" | custom-call | tf_op jit(solution)/shard_map/own/pallas_call | solution.py:150
  198.8 14.3 %collective-permute-done.6.got_ref.refs_5_ = bf16[1792,512]{1,0:T(8,128)(2,1)} collective-permute-done((bf16[1792,512]{1,0:T(8,128)(2,1)}, bf16[1792,512]{1,0:T(8,128)(2,1)}, u32[]{:S(2)}, u32[]{:S(2)}) %collective-permute-start.6) | collective-permute-done | bytes 1835040 | tf_op jit(solution)/shard_map/ppermute | solution.py:329
  213.1 5.4 %step.24.refs_15_ = bf16[1792,512]{1,0:T(8,128)(2,1)} custom-call(s32[2]{0:T(128)} %pad_add_fusion.place, bf16[1792,512]{1,0:T(8,128)(2,1)} %collective-permute-done.6.got_ref.refs_5_, bf16[3584,1024]{1,0:T(8,128)(2,1)} %hidden.1.hidden_ref, bf16[1024,2048]{1,0:T(8,128)(2,1)} %bitcast.2.grad_ref.refs_0_.refs_1_, bf16[3584,512]{1,0:T(8,128)(2,1)} %own.1.rest_0_.own_ref), custom_call_target="tpu_custom_call" | custom-call | flops 2000000000 | tf_op jit(solution)/shard_map/step/pallas_call | solution.py:129
  218.5 1.0 collective-permute-start.18
  219.5 6.7 %step.22.refs_13_ = bf16[1792,512]{1,0:T(8,128)(2,1)} custom-call(s32[2]{0:T(128)} %pad_add_fusion.place, bf16[1792,512]{1,0:T(8,128)(2,1)} %collective-permute-done.8.got_ref.refs_6_, bf16[3584,1024]{1,0:T(8,128)(2,1)} %hidden.1.hidden_ref, bf16[1024,2048]{1,0:T(8,128)(2,1)} %bitcast.2.grad_ref.refs_0_.refs_1_, bf16[3584,512]{1,0:T(8,128)(2,1)} %own.1.rest_0_.own_ref), custom_call_target="tpu_custom_call" | custom-call | flops 2000000000 | tf_op jit(solution)/shard_map/step/pallas_call | solution.py:129
  226.2 2.9 collective-permute-start.17
  229.0 10.9 %early.3 = (f32[512,1792]{1,0:T(8,128)}, f32[8,128]{1,0:T(8,128)}) custom-call(s32[2]{0:T(128)} %pad_add_fusion.place, bf16[1024,2048]{1,0:T(8,128)(2,1)} %bitcast.2.grad_ref.refs_0_.refs_1_, bf16[1024,2048]{1,0:T(8,128)(2,1)} %bitcast.2.grad_ref.refs_0_.refs_1_, bf16[1024,2048]{1,0:T(8,128)(2,1)} %collective-permute-done.refs_2_.refs_3_, ...), custom_call_target="tpu_custom_call" | custom-call | tf_op jit(solution)/shard_map/early/pallas_call | solution.py:272
  239.9 10.9 %early.2 = (f32[512,1792]{1,0:T(8,128)}, f32[8,128]{1,0:T(8,128)}) custom-call(s32[2]{0:T(128)} %pad_add_fusion.place, bf16[1024,2048]{1,0:T(8,128)(2,1)} %bitcast.2.grad_ref.refs_0_.refs_1_, bf16[1024,2048]{1,0:T(8,128)(2,1)} %bitcast.2.grad_ref.refs_0_.refs_1_, bf16[1024,2048]{1,0:T(8,128)(2,1)} %collective-permute-done.refs_2_.refs_3_, ...), custom_call_target="tpu_custom_call" | custom-call | tf_op jit(solution)/shard_map/early/pallas_call | solution.py:272
  250.8 1.6 collective-permute-done.13.got_ref.refs_9_
  252.4 1.3 copy-done
  253.6 4.9 %step.25.refs_16_ = bf16[1344,512]{1,0:T(8,128)(2,1)} custom-call(s32[2]{0:T(128)} %pad_add_fusion.place, bf16[1792,512]{1,0:T(8,128)(2,1)} %copy-done, bf16[3584,1024]{1,0:T(8,128)(2,1)} %hidden.1.hidden_ref, bf16[1024,2048]{1,0:T(8,128)(2,1)} %bitcast.2.grad_ref.refs_0_.refs_1_, f32[8,128]{1,0:T(8,128)} %get-tuple-element.18.rest_0_, ...), custom_call_target="tpu_custom_call" | custom-call | flops 1500000000 | tf_op jit(solution)/shard_map/step/pallas_call | solution.py:129
  258.6 1.2 copy-done.1
  259.8 5.9 %step.23.refs_14_ = bf16[1344,512]{1,0:T(8,128)(2,1)} custom-call(s32[2]{0:T(128)} %pad_add_fusion.place, bf16[1792,512]{1,0:T(8,128)(2,1)} %copy-done.1, bf16[3584,1024]{1,0:T(8,128)(2,1)} %hidden.1.hidden_ref, bf16[1024,2048]{1,0:T(8,128)(2,1)} %bitcast.2.grad_ref.refs_0_.refs_1_, f32[8,128]{1,0:T(8,128)} %get-tuple-element.18.rest_0_, ...), custom_call_target="tpu_custom_call" | custom-call | flops 1500000000 | tf_op jit(solution)/shard_map/step/pallas_call | solution.py:129
  265.7 11.6 %product.1 = (bf16[512,1792]{1,0:T(8,128)(2,1)}, f32[8,128]{1,0:T(8,128)}) custom-call(s32[2]{0:T(128)} %pad_add_fusion.place, bf16[1024,2048]{1,0:T(8,128)(2,1)} %bitcast.2.grad_ref.refs_0_.refs_1_, bf16[1024,2048]{1,0:T(8,128)(2,1)} %bitcast.2.grad_ref.refs_0_.refs_1_, bf16[1024,2048]{1,0:T(8,128)(2,1)} %collective-permute-done.refs_2_.refs_3_, ...), custom_call_target="tpu_custom_call" | custom-call | tf_op jit(solution)/shard_map/product/pallas_call | solution.py:272
  277.2 0.1 collective-permute-start.16
  277.3 0.5 collective-permute-start.20
  277.8 3.1 collective-permute-start.19
  280.9 12.7 %grads.1 = (bf16[512,3584]{1,0:T(8,128)(2,1)}, bf16[512,3584]{1,0:T(8,128)(2,1)}, f32[8,128]{1,0:T(8,128)}) custom-call(s32[2]{0:T(128)} %pad_add_fusion.place, bf16[1024,2048]{1,0:T(8,128)(2,1)} %bitcast.2.grad_ref.refs_0_.refs_1_, bf16[1024,2048]{1,0:T(8,128)(2,1)} %bitcast.2.grad_ref.refs_0_.refs_1_, ...), custom_call_target="tpu_custom_call" | custom-call | tf_op jit(solution)/shard_map/grads/pallas_call | solution.py:272
  293.6 3.7 %step.26 = bf16[448,512]{1,0:T(8,128)(2,1)} custom-call(s32[2]{0:T(128)} %pad_add_fusion.place, bf16[1792,512]{1,0:T(8,128)(2,1)} %copy-done.1, bf16[3584,1024]{1,0:T(8,128)(2,1)} %hidden.1.hidden_ref, bf16[1024,2048]{1,0:T(8,128)(2,1)} %bitcast.2.grad_ref.refs_0_.refs_1_, f32[8,128]{1,0:T(8,128)} %get-tuple-element.25.rest_0_), custom_call_target="tpu_custom_call" | custom-call | flops 500000000 | tf_op jit(solution)/shard_map/step/pallas_call | solution.py:129
  297.3 3.3 step.27
  300.7 2.6 collective-permute-start.21
  303.3 5.2 %final.2 = (bf16[3584,512]{1,0:T(8,128)(2,1)}, f32[8,128]{1,0:T(8,128)}) custom-call(s32[2]{0:T(128)} %pad_add_fusion.place, bf16[1792,512]{1,0:T(8,128)(2,1)} %collective-permute-done.17.one_ref, bf16[1792,512]{1,0:T(8,128)(2,1)} %collective-permute-done.18.two_ref, bf16[3584,512]{1,0:T(8,128)(2,1)} %own.1.rest_0_.own_ref, f32[8,128]{1,0:T(8,128)} %get-tuple-element.25.rest_0_), custom_call_target="tpu_custom_call" | custom-call | tf_op jit(solution)/shard_map/final/pallas_call | solution.py:192
  308.4 5.4 %join.1 = (bf16[512,3584]{1,0:T(8,128)(2,1)}, bf16[512,3584]{1,0:T(8,128)(2,1)}) custom-call(s32[2]{0:T(128)} %pad_add_fusion.place, bf16[512,1792]{1,0:T(8,128)(2,1)} %collective-permute-done.16.product_ref, bf16[512,3584]{1,0:T(8,128)(2,1)} %gate_ref.1, bf16[512,3584]{1,0:T(8,128)(2,1)} %up_ref.1, ...), custom_call_target="tpu_custom_call", output_to_operand_aliasing={{0}: (4, {}), {1}: (5, {})} | custom-call | tf_op jit(solution)/shard_map/join/pallas_call | solution.py:296
  313.8 7.5 %collective-permute-done.20.two_ref = bf16[1344,512]{1,0:T(8,128)(2,1)} collective-permute-done((bf16[1344,512]{1,0:T(8,128)(2,1)S(1)}, bf16[1344,512]{1,0:T(8,128)(2,1)}, u32[]{:S(2)}, u32[]{:S(2)}) %collective-permute-start.20) | collective-permute-done | bytes 1376288 | tf_op jit(solution)/shard_map/ppermute | solution.py:329
  321.3 0.6 collective-permute-done.19.one_ref
  321.8 4.7 %final.3 = (bf16[3584,512]{1,0:T(8,128)(2,1)}, f32[8,128]{1,0:T(8,128)}) custom-call(s32[2]{0:T(128)} %pad_add_fusion.place, bf16[1344,512]{1,0:T(8,128)(2,1)} %collective-permute-done.19.one_ref, bf16[1344,512]{1,0:T(8,128)(2,1)} %collective-permute-done.20.two_ref, bf16[3584,512]{1,0:T(8,128)(2,1)} %own.1.rest_0_.own_ref, ...), custom_call_target="tpu_custom_call", output_to_operand_aliasing={{0}: (4, {})} | custom-call | tf_op jit(solution)/shard_map/final/pallas_call | solution.py:192
  326.6 4.6 %collective-permute-done.21 = bf16[448,512]{1,0:T(8,128)(2,1)S(1)} collective-permute-done((bf16[448,512]{1,0:T(8,128)(2,1)}, bf16[448,512]{1,0:T(8,128)(2,1)S(1)}, u32[]{:S(2)}, u32[]{:S(2)}) %collective-permute-start.21) | collective-permute-done | bytes 458784 | tf_op jit(solution)/shard_map/ppermute | solution.py:329
  331.2 2.2 fusion
  (26 shorter events, 0.1 us)
Async XLA Ops:
  0.6 15.4 %collective-permute-start.9 = (bf16[3584,512]{1,0:T(8,128)(2,1)}, bf16[3584,512]{1,0:T(8,128)(2,1)}, u32[]{:S(2)}, u32[]{:S(2)}) collective-permute-start(bf16[3584,512]{1,0:T(8,128)(2,1)} %param.7), channel_id=1, source_target_pairs={{0,4},{4,0},{8,12},{12,8},{16,20},{20,16},{24,28},{28,24},{1,5},{5... | collective-permute-start | bytes 11010056 | tf_op jit(solution)/shard_map/ppermute | solution.py:326
  1.1 17.8 %collective-permute-start.3 = (bf16[512,3584]{1,0:T(8,128)(2,1)}, bf16[512,3584]{1,0:T(8,128)(2,1)}, u32[]{:S(2)}, u32[]{:S(2)}) collective-permute-start(bf16[512,3584]{1,0:T(8,128)(2,1)} %gate_ref.1), channel_id=1, source_target_pairs={{0,4},{4,0},{8,12},{12,8},{16,20},{20,16},{24,28},{28,24},{1,5},{5... | collective-permute-start | bytes 11010056 | tf_op jit(solution)/shard_map/ppermute | solution.py:326
  1.2 19.7 %collective-permute-start.4 = (bf16[512,3584]{1,0:T(8,128)(2,1)}, bf16[512,3584]{1,0:T(8,128)(2,1)}, u32[]{:S(2)}, u32[]{:S(2)}) collective-permute-start(bf16[512,3584]{1,0:T(8,128)(2,1)} %up_ref.1), channel_id=1, source_target_pairs={{0,4},{4,0},{8,12},{12,8},{16,20},{20,16},{24,28},{28,24},{1,5},{5... | collective-permute-start | bytes 11010056 | tf_op jit(solution)/shard_map/ppermute | solution.py:326
  7.1 54.2 %all-to-all-start = ((bf16[8,128,2048]{2,1,0:T(8,128)(2,1)}), bf16[8,128,2048]{2,1,0:T(8,128)(2,1)}, u32[]{:S(2)}, u32[]{:S(2)}) async-start(bf16[8,128,2048]{2,1,0:T(8,128)(2,1)} %spread.1), calls=%async_computation | async-start | bytes 8388608 | tf_op jit(solution)/shard_map/all_to_all | solution.py:343
  13.6 5.3 %copy-start.4 = (bf16[1792,512]{1,0:T(8,128)(2,1)}, bf16[1792,512]{1,0:T(8,128)(2,1)S(1)}, u32[]{:S(2)}) copy-start(bf16[1792,512]{1,0:T(8,128)(2,1)S(1)} %constant_dynamic-slice_fusion.1.refs_4_) | copy-start | bytes 5505028
  13.6 42.2 %collective-permute-start.2 = (bf16[1792,512]{1,0:T(8,128)(2,1)S(1)}, bf16[1792,512]{1,0:T(8,128)(2,1)}, u32[]{:S(2)}, u32[]{:S(2)}) collective-permute-start(bf16[1792,512]{1,0:T(8,128)(2,1)S(1)} %constant_dynamic-slice_fusion.1.refs_4_), channel_id=1, source_target_pairs={{4,12},{12,20},{20,28},{28,24},{24,16},{16,8},{8,0},{0,4},{5,13},{... | collective-permute-start | bytes 5505032 | tf_op jit(solution)/shard_map/ppermute | solution.py:329
  14.1 54.0 %collective-permute-start.1 = (bf16[1792,512]{1,0:T(8,128)(2,1)S(1)}, bf16[1792,512]{1,0:T(8,128)(2,1)}, u32[]{:S(2)}, u32[]{:S(2)}) collective-permute-start(bf16[1792,512]{1,0:T(8,128)(2,1)S(1)} %constant_dynamic-slice_fusion.1.refs_4_), channel_id=1, source_target_pairs={{0,8},{8,16},{16,24},{24,28},{28,20},{20,12},{12,4},{4,0},{1,9},{9... | collective-permute-start | bytes 5505032 | tf_op jit(solution)/shard_map/ppermute | solution.py:329
  18.9 76.3 %collective-permute-start.11 = (bf16[1792,512]{1,0:T(8,128)(2,1)}, bf16[1792,512]{1,0:T(8,128)(2,1)}, u32[]{:S(2)}, u32[]{:S(2)}) collective-permute-start(bf16[1792,512]{1,0:T(8,128)(2,1)} %constant_dynamic-slice_fusion.refs_7_), channel_id=1, source_target_pairs={{4,12},{12,20},{20,28},{28,24},{24,16},{16,8},{8,0},{0,4},{5,13},{... | collective-permute-start | bytes 5505032 | tf_op jit(solution)/shard_map/ppermute | solution.py:329
  19.0 82.6 %collective-permute-start.10 = (bf16[1792,512]{1,0:T(8,128)(2,1)}, bf16[1792,512]{1,0:T(8,128)(2,1)}, u32[]{:S(2)}, u32[]{:S(2)}) collective-permute-start(bf16[1792,512]{1,0:T(8,128)(2,1)} %constant_dynamic-slice_fusion.refs_7_), channel_id=1, source_target_pairs={{0,8},{8,16},{16,24},{24,28},{28,20},{20,12},{12,4},{4,0},{1,9},{9... | collective-permute-start | bytes 5505032 | tf_op jit(solution)/shard_map/ppermute | solution.py:329
  66.6 67.8 %collective-permute-start.5 = (bf16[1792,512]{1,0:T(8,128)(2,1)}, bf16[1792,512]{1,0:T(8,128)(2,1)S(1)}, u32[]{:S(2)}, u32[]{:S(2)}) collective-permute-start(bf16[1792,512]{1,0:T(8,128)(2,1)} %step.14), channel_id=1, source_target_pairs={{4,12},{12,20},{20,28},{28,24},{24,16},{16,8},{8,0},{0,4},{5,13},{... | collective-permute-start | bytes 5505032 | tf_op jit(solution)/shard_map/ppermute | solution.py:329
  74.8 67.3 %collective-permute-start.7 = (bf16[1792,512]{1,0:T(8,128)(2,1)}, bf16[1792,512]{1,0:T(8,128)(2,1)S(1)}, u32[]{:S(2)}, u32[]{:S(2)}) collective-permute-start(bf16[1792,512]{1,0:T(8,128)(2,1)} %step.16), channel_id=1, source_target_pairs={{0,8},{8,16},{16,24},{24,28},{28,20},{20,12},{12,4},{4,0},{1,9},{9... | collective-permute-start | bytes 5505032 | tf_op jit(solution)/shard_map/ppermute | solution.py:329
  74.8 154.3 %collective-permute-start = (bf16[1024,2048]{1,0:T(8,128)(2,1)}, bf16[1024,2048]{1,0:T(8,128)(2,1)}, u32[]{:S(2)}, u32[]{:S(2)}) collective-permute-start(bf16[1024,2048]{1,0:T(8,128)(2,1)} %bitcast.2.grad_ref.refs_0_.refs_1_), channel_id=1, source_target_pairs={{0,4},{4,0},{8,12},{12,8},{16,20},{20,16},{24,28},{28,24},{1,5},{5... | collective-permute-start | bytes 12582920 | tf_op jit(solution)/shard_map/ppermute | solution.py:326
  100.5 73.3 %collective-permute-start.12 = (bf16[1792,512]{1,0:T(8,128)(2,1)}, bf16[1792,512]{1,0:T(8,128)(2,1)}, u32[]{:S(2)}, u32[]{:S(2)}) collective-permute-start(bf16[1792,512]{1,0:T(8,128)(2,1)} %step.18), channel_id=1, source_target_pairs={{4,12},{12,20},{20,28},{28,24},{24,16},{16,8},{8,0},{0,4},{5,13},{... | collective-permute-start | bytes 5505032 | tf_op jit(solution)/shard_map/ppermute | solution.py:329
  108.2 71.9 %collective-permute-start.14 = (bf16[1792,512]{1,0:T(8,128)(2,1)}, bf16[1792,512]{1,0:T(8,128)(2,1)}, u32[]{:S(2)}, u32[]{:S(2)}) collective-permute-start(bf16[1792,512]{1,0:T(8,128)(2,1)} %step.20), channel_id=1, source_target_pairs={{0,8},{8,16},{16,24},{24,28},{28,20},{20,12},{12,4},{4,0},{1,9},{9... | collective-permute-start | bytes 5505032 | tf_op jit(solution)/shard_map/ppermute | solution.py:329
  134.4 1.2 copy-start.2
  140.9 72.2 %collective-permute-start.6 = (bf16[1792,512]{1,0:T(8,128)(2,1)}, bf16[1792,512]{1,0:T(8,128)(2,1)}, u32[]{:S(2)}, u32[]{:S(2)}) collective-permute-start(bf16[1792,512]{1,0:T(8,128)(2,1)} %step.15), channel_id=1, source_target_pairs={{4,12},{12,20},{20,28},{28,24},{24,16},{16,8},{8,0},{0,4},{5,13},{... | collective-permute-start | bytes 5505032 | tf_op jit(solution)/shard_map/ppermute | solution.py:329
  142.1 1.2 copy-start.3
  150.0 69.5 %collective-permute-start.8 = (bf16[1792,512]{1,0:T(8,128)(2,1)}, bf16[1792,512]{1,0:T(8,128)(2,1)}, u32[]{:S(2)}, u32[]{:S(2)}) collective-permute-start(bf16[1792,512]{1,0:T(8,128)(2,1)} %step.17), channel_id=1, source_target_pairs={{0,8},{8,16},{16,24},{24,28},{28,20},{20,12},{12,4},{4,0},{1,9},{9... | collective-permute-start | bytes 5505032 | tf_op jit(solution)/shard_map/ppermute | solution.py:329
  179.1 73.2 %collective-permute-start.13 = (bf16[1792,512]{1,0:T(8,128)(2,1)}, bf16[1792,512]{1,0:T(8,128)(2,1)S(1)}, u32[]{:S(2)}, u32[]{:S(2)}) collective-permute-start(bf16[1792,512]{1,0:T(8,128)(2,1)} %step.19), channel_id=1, source_target_pairs={{4,12},{12,20},{20,28},{28,24},{24,16},{16,8},{8,0},{0,4},{5,13},{... | collective-permute-start | bytes 5505032 | tf_op jit(solution)/shard_map/ppermute | solution.py:329
  186.8 71.7 %collective-permute-start.15 = (bf16[1792,512]{1,0:T(8,128)(2,1)}, bf16[1792,512]{1,0:T(8,128)(2,1)S(1)}, u32[]{:S(2)}, u32[]{:S(2)}) collective-permute-start(bf16[1792,512]{1,0:T(8,128)(2,1)} %step.21), channel_id=1, source_target_pairs={{0,8},{8,16},{16,24},{24,28},{28,20},{20,12},{12,4},{4,0},{1,9},{9... | collective-permute-start | bytes 5505032 | tf_op jit(solution)/shard_map/ppermute | solution.py:329
  218.5 82.1 %collective-permute-start.18 = (bf16[1792,512]{1,0:T(8,128)(2,1)}, bf16[1792,512]{1,0:T(8,128)(2,1)}, u32[]{:S(2)}, u32[]{:S(2)}) collective-permute-start(bf16[1792,512]{1,0:T(8,128)(2,1)} %step.24.refs_15_), channel_id=1, source_target_pairs={{4,12},{12,20},{20,28},{28,24},{24,16},{16,8},{8,0},{0,4},{5,13},{... | collective-permute-start | bytes 5505032 | tf_op jit(solution)/shard_map/ppermute | solution.py:329
  226.2 77.1 %collective-permute-start.17 = (bf16[1792,512]{1,0:T(8,128)(2,1)}, bf16[1792,512]{1,0:T(8,128)(2,1)}, u32[]{:S(2)}, u32[]{:S(2)}) collective-permute-start(bf16[1792,512]{1,0:T(8,128)(2,1)} %step.22.refs_13_), channel_id=1, source_target_pairs={{0,8},{8,16},{16,24},{24,28},{28,20},{20,12},{12,4},{4,0},{1,9},{9... | collective-permute-start | bytes 5505032 | tf_op jit(solution)/shard_map/ppermute | solution.py:329
  252.4 1.3 copy-start
  258.6 1.2 copy-start.1
  265.7 11.6 %copy-start.5 = (bf16[1344,512]{1,0:T(8,128)(2,1)S(1)}, bf16[1344,512]{1,0:T(8,128)(2,1)}, u32[]{:S(2)}) copy-start(bf16[1344,512]{1,0:T(8,128)(2,1)} %step.25.refs_16_) | copy-start | bytes 4128772
  265.7 12.1 %copy-start.6 = (bf16[1344,512]{1,0:T(8,128)(2,1)S(1)}, bf16[1344,512]{1,0:T(8,128)(2,1)}, u32[]{:S(2)}) copy-start(bf16[1344,512]{1,0:T(8,128)(2,1)} %step.23.refs_14_) | copy-start | bytes 4128772
  277.2 31.2 %collective-permute-start.16 = (bf16[512,1792]{1,0:T(8,128)(2,1)}, bf16[512,1792]{1,0:T(8,128)(2,1)}, u32[]{:S(2)}, u32[]{:S(2)}) collective-permute-start(bf16[512,1792]{1,0:T(8,128)(2,1)} %get-tuple-element.20), channel_id=1, source_target_pairs={{0,4},{4,0},{8,12},{12,8},{16,20},{20,16},{24,28},{28,24},{1,5},{5... | collective-permute-start | bytes 5505032 | tf_op jit(solution)/shard_map/ppermute | solution.py:326
  277.3 43.9 %collective-permute-start.20 = (bf16[1344,512]{1,0:T(8,128)(2,1)S(1)}, bf16[1344,512]{1,0:T(8,128)(2,1)}, u32[]{:S(2)}, u32[]{:S(2)}) collective-permute-start(bf16[1344,512]{1,0:T(8,128)(2,1)S(1)} %copy-done.5), channel_id=1, source_target_pairs={{4,12},{12,20},{20,28},{28,24},{24,16},{16,8},{8,0},{0,4},{5,13},{... | collective-permute-start | bytes 4128776 | tf_op jit(solution)/shard_map/ppermute | solution.py:329
  277.8 44.0 %collective-permute-start.19 = (bf16[1344,512]{1,0:T(8,128)(2,1)S(1)}, bf16[1344,512]{1,0:T(8,128)(2,1)}, u32[]{:S(2)}, u32[]{:S(2)}) collective-permute-start(bf16[1344,512]{1,0:T(8,128)(2,1)S(1)} %copy-done.6), channel_id=1, source_target_pairs={{0,8},{8,16},{16,24},{24,28},{28,20},{20,12},{12,4},{4,0},{1,9},{9... | collective-permute-start | bytes 4128776 | tf_op jit(solution)/shard_map/ppermute | solution.py:329
  300.7 30.6 %collective-permute-start.21 = (bf16[448,512]{1,0:T(8,128)(2,1)}, bf16[448,512]{1,0:T(8,128)(2,1)S(1)}, u32[]{:S(2)}, u32[]{:S(2)}) collective-permute-start(bf16[448,512]{1,0:T(8,128)(2,1)} %step.26), channel_id=1, source_target_pairs={{0,8},{8,16},{16,24},{24,28},{28,20},{20,12},{12,4},{4,0},{1,9},{9... | collective-permute-start | bytes 1376264 | tf_op jit(solution)/shard_map/ppermute | solution.py:329
  303.3 28.0 %collective-permute-start.22 = (bf16[448,512]{1,0:T(8,128)(2,1)}, bf16[448,512]{1,0:T(8,128)(2,1)}, u32[]{:S(2)}, u32[]{:S(2)}) collective-permute-start(bf16[448,512]{1,0:T(8,128)(2,1)} %step.27), channel_id=1, source_target_pairs={{4,12},{12,20},{20,28},{28,24},{24,16},{16,8},{8,0},{0,4},{5,13},{... | collective-permute-start | bytes 1376264 | tf_op jit(solution)/shard_map/ppermute | solution.py:329

commit v4 on v3

--- a/solution.py
+++ b/solution.py
@@ -9,7 +9,7 @@
 from jax.sharding import PartitionSpec as P
 
 VMEM = 60 * 1024 * 1024
-STEP_FLOPS = 2e9
+STEP_FLOPS, ARRIVED_FLOPS = 2e9, 7e9
 F32, BF16 = jnp.float32, jnp.bfloat16
 ANY = pl.BlockSpec(memory_space=pl.ANY)
 
@@ -41,26 +41,50 @@
     return lax.dot_general(a, b, (contract, ((), ())), preferred_element_type=F32)
 
 
-def spread_kernel(place, even_ref, odd_ref, out_ref):
-    peers = out_ref.shape[0] // 2
-    for core, ref in enumerate((even_ref, odd_ref)):
-        for peer in range(peers):
-            out_ref[core * peers + peer] = ref[...]
-
-
-def spread_call(place, out_grad, peers, line, block):
-    rows = out_grad.shape[0]
-    return call(
-        spread_kernel,
-        (line,),
-        [
-            pl.BlockSpec((rows, block), lambda b, s: (0, 2 * b)),
-            pl.BlockSpec((rows, block), lambda b, s: (0, 2 * b + 1)),
+def spread_kernel(line, grad_ref, out_ref, held, load_sem, store_sem):
+    peers = out_ref.shape[0]
+    block = held.shape[1] // (2 * line)
+
+    def load(b):
+        here = pl.ds(b * block, block)
+        return pltpu.make_async_copy(grad_ref.at[:, here], held.at[:, here], load_sem.at[b])
+
+    def store(b, peer):
+        here = pl.ds(b // 2 * block, block)
+        return pltpu.make_async_copy(
+            held.at[:, pl.ds(b * block, block)], out_ref.at[peer, :, here], store_sem.at[b, peer]
+        )
+
+    places = [
+        (b, b % 2 * (peers // 2) + peer) for b in range(2 * line) for peer in range(peers // 2)
+    ]
+    for b in range(2 * line):
+        load(b).start()
+    for b in range(2 * line):
+        load(b).wait()
+        for place in places:
+            if place[0] == b:
+                store(*place).start()
+    for place in places:
+        store(*place).wait()
+
+
+def spread_call(out_grad, peers, line):
+    rows, width = out_grad.shape
+    return pl.pallas_call(
+        functools.partial(spread_kernel, line),
+        in_specs=[ANY],
+        out_specs=ANY,
+        out_shape=jax.ShapeDtypeStruct((peers, rows, width // 2), BF16),
+        scratch_shapes=[
+            pltpu.VMEM((rows, width), BF16),
+            pltpu.SemaphoreType.DMA((2 * line,)),
+            pltpu.SemaphoreType.DMA((2 * line, peers)),
         ],
-        pl.BlockSpec((peers, rows, block), lambda b, s: (0, 0, b)),
-        jax.ShapeDtypeStruct((peers, rows, line * block), BF16),
-        "spread",
-    )(place, out_grad, out_grad)
+        compiler_params=pltpu.CompilerParams(vmem_limit_bytes=VMEM),
+        cost_estimate=pl.CostEstimate(flops=0, bytes_accessed=0, transcendentals=0),
+        name="spread",
+    )(out_grad)
 
 
 def hidden_kernel(place, gate_own, up_own, gate_sib, up_sib, out_ref):
@@ -99,6 +123,22 @@
         pl.BlockSpec((tile, tokens), lambda i, s: (first + i, 0)),
         pl.BlockSpec((tokens, block), column),
     ]
+
+
+def arrived_kernel(place, *refs):
+    refs[-1][...] = jnp.zeros_like(refs[-1])
+
+
+def arrived_call(place, arrays):
+    return call(
+        arrived_kernel,
+        (1,),
+        [ANY] * len(arrays),
+        pl.BlockSpec((8, 128), lambda i, s: (0, 0)),
+        jax.ShapeDtypeStruct((8, 128), F32),
+        "arrived",
+        flops=ARRIVED_FLOPS,
+    )(place, *arrays)
 
 
 def step_kernel(flow, j, line, place, got_ref, hidden_ref, grad_ref, *rest):
@@ -339,7 +379,7 @@
     groups = [
         [(2 * z + c) * n_mp + m for c in range(2) for m in range(n_mp)] for z in range(line)
     ]
-    spread = spread_call(place, out_grad, 2 * n_mp, line, block)
+    spread = spread_call(out_grad, 2 * n_mp, line)
     out_grads = lax.all_to_all(
         spread, ("dp", "mp"), split_axis=0, concat_axis=0, tiled=True, axis_index_groups=groups
     ).reshape(2 * tokens, line * block)
@@ -352,8 +392,10 @@
         j = line + 1 - slot
         return step_call(place, before, hidden, out_grads, k, quarters, j, flow, line, after)
 
+    arrived = arrived_call(place, [got[flow][0][0] for flow in range(2)])
     for slot in range(2, line):
-        sent = [[step(slot, flow, k, (0, 4)) for k in range(2)] for flow in range(2)]
+        after = [(arrived,) if slot == 2 else (), ()]
+        sent = [[step(slot, flow, k, (0, 4), after[k]) for k in range(2)] for flow in range(2)]
         for flow in range(2):
             got[flow].append([send(x, flow) for x in sent[flow]])
 

time: 336 us -> 334 us (level)
  starting transfers between devices: 28.7 us -> 25.3 us
    ppermute x18, waiting for transfers between devices: 117 us -> 123 us  [send(): return lax.ppermute(x, 'dp', rings[flow])]
    all_to_all x1, waiting for transfers between devices: 5.46 us -> 0.01 us  [shards(): lax.all_to_all(spread, ('dp', 'mp'), split_axis=0, concat_axis=0, tiled=T...]
  transfers between devices with their start and end apart: 24 -> 24, of which waited for: 10 -> 14; matrix products, arithmetic and copies ran while one was open for 2% -> 2% of each run, Pallas kernels for 51% -> 51%
where the time goes in v4:
time: 334 us; the launch traced here: 332 us
  Pallas kernels  169 us (51%)
  waiting for transfers between devices  123 us (37%)
  starting transfers between devices  25.3 us (8%)
  local copies, waits for them, and re-layouts  10.7 us (3%)
    ppermute x18, waiting for transfers between devices, send(): return lax.ppermute(x, 'dp', rings[flow])  123 us
    pallas_call x14, Pallas kernels, step_call(): call(functools.partial(step_kernel, flow, j, line), (high - low,), [pl.Bl...  77.9 us
    pallas_call x4, Pallas kernels, product_call(): call(functools.partial(product_kernel, line, slots, counts), (steps,), ro...  46 us
    ppermute x18, starting transfers between devices, send(): return lax.ppermute(x, 'dp', rings[flow])  19.3 us
    pallas_call x1, Pallas kernels, hidden_call(): call(hidden_kernel, (units // tile,), [pl.BlockSpec((tokens, tile), lambd...  14.6 us
    pallas_call x1, Pallas kernels, own_call(): call(own_kernel, (steps,), term_specs(tile, tokens, block, 0, lambda s: 0...  10.5 us
    pallas_call x2, Pallas kernels, final_call(): call(functools.partial(final_kernel, scale, line), (rows // tile,), [got,...  9.9 us
  transfers between devices with their start and end apart: 24, of which 14 were waited for; matrix products, arithmetic and copies ran while one was open for 2% of the time, Pallas kernels for 51%

profile of v4, /device:TPU:0, one launch (start us, length us, event | category | flops | bytes accessed | tf_op | source)
XLA Modules:
  0.0 331.6 jit_solution(16017253540754297590)
XLA Ops:
  0.6 0.5 collective-permute-start.9
  1.1 0.1 collective-permute-start.3
  1.2 0.4 collective-permute-start.4
  1.7 3.6 %spread.1 = bf16[8,128,2048]{2,1,0:T(8,128)(2,1)} custom-call(bf16[128,4096]{1,0:T(8,128)(2,1)} %grad_ref.1), custom_call_target="tpu_custom_call" | custom-call | tf_op jit(solution)/shard_map/spread/pallas_call | solution.py:74
  5.2 4.9 %all-to-all-start = ((bf16[8,128,2048]{2,1,0:T(8,128)(2,1)}), bf16[8,128,2048]{2,1,0:T(8,128)(2,1)}, u32[]{:S(2)}, u32[]{:S(2)}) async-start(bf16[8,128,2048]{2,1,0:T(8,128)(2,1)} %spread.1), calls=%async_computation | async-start | bytes 8388608 | tf_op jit(solution)/shard_map/all_to_all | solution.py:383
  10.1 1.6 constant_dynamic-slice_fusion.1.refs_4_
  11.7 2.4 collective-permute-start.1
  14.2 2.8 constant_dynamic-slice_fusion.refs_7_
  17.0 0.1 collective-permute-start.11
  17.1 37.4 %collective-permute-done.1.refs_0_.got_ref.refs_4_ = bf16[1792,512]{1,0:T(8,128)(2,1)S(1)} collective-permute-done((bf16[1792,512]{1,0:T(8,128)(2,1)S(1)}, bf16[1792,512]{1,0:T(8,128)(2,1)S(1)}, u32[]{:S(2)}, u32[]{:S(2)}) %collective-permute-start.1) | collective-permute-done | bytes 1835040 | tf_op jit(solution)/shard_map/ppermute | solution.py:369
  54.5 1.3 copy-done.5
  55.8 2.5 collective-permute-start.10
  58.3 0.6 pad_add_fusion.place
  58.9 1.3 arrived.1.rest_0_
  60.2 14.6 %hidden.1.hidden_ref = bf16[3584,1024]{1,0:T(8,128)(2,1)} custom-call(s32[2]{0:T(128)} %pad_add_fusion.place, bf16[512,3584]{1,0:T(8,128)(2,1)} %gate_ref.1, bf16[512,3584]{1,0:T(8,128)(2,1)} %up_ref.1, bf16[512,3584]{1,0:T(8,128)(2,1)} %collective-permute-done.3.gate_sib, bf16[512,3584]{1,0:T(8,128)(2,1)} %collective-permute-done.4.up_sib), custom_call_target="tpu_custom_call" | custom-call | tf_op jit(solution)/shard_map/hidden/pallas_call | solution.py:104
  74.7 5.3 %step.14 = bf16[1792,512]{1,0:T(8,128)(2,1)} custom-call(s32[2]{0:T(128)} %pad_add_fusion.place, bf16[1792,512]{1,0:T(8,128)(2,1)} %collective-permute-done.2.refs_1_.got_ref.refs_7_, bf16[3584,1024]{1,0:T(8,128)(2,1)} %hidden.1.hidden_ref, bf16[1024,2048]{1,0:T(8,128)(2,1)} %bitcast.2.grad_ref.refs_0_.refs_1_, f32[8,128]{1,0:T(8,128)} %arrived.1.rest_0_), custom_call_target="tpu_custom_call" | custom-call | flops 2000000000 | tf_op jit(solution)/shard_map/step/pallas_call | solution.py:169
  80.1 6.7 %step.16 = bf16[1792,512]{1,0:T(8,128)(2,1)} custom-call(s32[2]{0:T(128)} %pad_add_fusion.place, bf16[1792,512]{1,0:T(8,128)(2,1)} %copy-done.5, bf16[3584,1024]{1,0:T(8,128)(2,1)} %hidden.1.hidden_ref, bf16[1024,2048]{1,0:T(8,128)(2,1)} %bitcast.2.grad_ref.refs_0_.refs_1_, f32[8,128]{1,0:T(8,128)} %arrived.1.rest_0_), custom_call_target="tpu_custom_call" | custom-call | flops 2000000000 | tf_op jit(solution)/shard_map/step/pallas_call | solution.py:169
  86.7 0.7 collective-permute-start.7
  87.4 4.6 %collective-permute-done.11.got_ref.refs_11_ = bf16[1792,512]{1,0:T(8,128)(2,1)} collective-permute-done((bf16[1792,512]{1,0:T(8,128)(2,1)}, bf16[1792,512]{1,0:T(8,128)(2,1)}, u32[]{:S(2)}, u32[]{:S(2)}) %collective-permute-start.11) | collective-permute-done | bytes 1835040 | tf_op jit(solution)/shard_map/ppermute | solution.py:369
  92.0 5.3 %step.18 = bf16[1792,512]{1,0:T(8,128)(2,1)} custom-call(s32[2]{0:T(128)} %pad_add_fusion.place, bf16[1792,512]{1,0:T(8,128)(2,1)} %collective-permute-done.11.got_ref.refs_11_, bf16[3584,1024]{1,0:T(8,128)(2,1)} %hidden.1.hidden_ref, bf16[1024,2048]{1,0:T(8,128)(2,1)} %bitcast.2.grad_ref.refs_0_.refs_1_), custom_call_target="tpu_custom_call" | custom-call | flops 2000000000 | tf_op jit(solution)/shard_map/step/pallas_call | solution.py:169
  97.4 1.7 collective-permute-done.10.got_ref.refs_8_
  99.0 6.7 %step.20 = bf16[1792,512]{1,0:T(8,128)(2,1)} custom-call(s32[2]{0:T(128)} %pad_add_fusion.place, bf16[1792,512]{1,0:T(8,128)(2,1)} %collective-permute-done.10.got_ref.refs_8_, bf16[3584,1024]{1,0:T(8,128)(2,1)} %hidden.1.hidden_ref, bf16[1024,2048]{1,0:T(8,128)(2,1)} %bitcast.2.grad_ref.refs_0_.refs_1_), custom_call_target="tpu_custom_call" | custom-call | flops 2000000000 | tf_op jit(solution)/shard_map/step/pallas_call | solution.py:169
  105.7 1.2 collective-permute-start.14
  106.9 24.4 %collective-permute-done.5.got_ref.refs_6_ = bf16[1792,512]{1,0:T(8,128)(2,1)S(1)} collective-permute-done((bf16[1792,512]{1,0:T(8,128)(2,1)}, bf16[1792,512]{1,0:T(8,128)(2,1)S(1)}, u32[]{:S(2)}, u32[]{:S(2)}) %collective-permute-start.5) | collective-permute-done | bytes 1835040 | tf_op jit(solution)/shard_map/ppermute | solution.py:369
  131.3 1.2 copy-done.2
  132.5 5.3 %step.15 = bf16[1792,512]{1,0:T(8,128)(2,1)} custom-call(s32[2]{0:T(128)} %pad_add_fusion.place, bf16[1792,512]{1,0:T(8,128)(2,1)} %copy-done.2, bf16[3584,1024]{1,0:T(8,128)(2,1)} %hidden.1.hidden_ref, bf16[1024,2048]{1,0:T(8,128)(2,1)} %bitcast.2.grad_ref.refs_0_.refs_1_), custom_call_target="tpu_custom_call" | custom-call | flops 2000000000 | tf_op jit(solution)/shard_map/step/pallas_call | solution.py:169
  137.8 0.6 collective-permute-done.7.got_ref.refs_5_
  138.4 1.2 copy-done.3
  139.6 6.7 %step.17 = bf16[1792,512]{1,0:T(8,128)(2,1)} custom-call(s32[2]{0:T(128)} %pad_add_fusion.place, bf16[1792,512]{1,0:T(8,128)(2,1)} %copy-done.3, bf16[3584,1024]{1,0:T(8,128)(2,1)} %hidden.1.hidden_ref, bf16[1024,2048]{1,0:T(8,128)(2,1)} %bitcast.2.grad_ref.refs_0_.refs_1_), custom_call_target="tpu_custom_call" | custom-call | flops 2000000000 | tf_op jit(solution)/shard_map/step/pallas_call | solution.py:169
  146.3 2.4 collective-permute-start.8
  148.7 22.0 %collective-permute-done.12.got_ref.refs_9_ = bf16[1792,512]{1,0:T(8,128)(2,1)} collective-permute-done((bf16[1792,512]{1,0:T(8,128)(2,1)}, bf16[1792,512]{1,0:T(8,128)(2,1)}, u32[]{:S(2)}, u32[]{:S(2)}) %collective-permute-start.12) | collective-permute-done | bytes 1835040 | tf_op jit(solution)/shard_map/ppermute | solution.py:369
  170.7 5.3 %step.19 = bf16[1792,512]{1,0:T(8,128)(2,1)} custom-call(s32[2]{0:T(128)} %pad_add_fusion.place, bf16[1792,512]{1,0:T(8,128)(2,1)} %collective-permute-done.12.got_ref.refs_9_, bf16[3584,1024]{1,0:T(8,128)(2,1)} %hidden.1.hidden_ref, bf16[1024,2048]{1,0:T(8,128)(2,1)} %bitcast.2.grad_ref.refs_0_.refs_1_), custom_call_target="tpu_custom_call" | custom-call | flops 2000000000 | tf_op jit(solution)/shard_map/step/pallas_call | solution.py:169
  176.0 1.7 collective-permute-done.14.got_ref.refs_8_
  177.7 6.7 %step.21 = bf16[1792,512]{1,0:T(8,128)(2,1)} custom-call(s32[2]{0:T(128)} %pad_add_fusion.place, bf16[1792,512]{1,0:T(8,128)(2,1)} %collective-permute-done.14.got_ref.refs_8_, bf16[3584,1024]{1,0:T(8,128)(2,1)} %hidden.1.hidden_ref, bf16[1024,2048]{1,0:T(8,128)(2,1)} %bitcast.2.grad_ref.refs_0_.refs_1_), custom_call_target="tpu_custom_call" | custom-call | flops 2000000000 | tf_op jit(solution)/shard_map/step/pallas_call | solution.py:169
  184.4 2.5 collective-permute-start.15
  186.9 10.5 %own.1.rest_0_.own_ref = bf16[3584,512]{1,0:T(8,128)(2,1)} custom-call(s32[2]{0:T(128)} %pad_add_fusion.place, bf16[3584,1024]{1,0:T(8,128)(2,1)} %hidden.1.hidden_ref, bf16[1024,2048]{1,0:T(8,128)(2,1)} %bitcast.2.grad_ref.refs_0_.refs_1_), custom_call_target="tpu_custom_call" | custom-call | tf_op jit(solution)/shard_map/own/pallas_call | solution.py:190
  197.3 12.7 %collective-permute-done.6.got_ref.refs_5_ = bf16[1792,512]{1,0:T(8,128)(2,1)} collective-permute-done((bf16[1792,512]{1,0:T(8,128)(2,1)}, bf16[1792,512]{1,0:T(8,128)(2,1)}, u32[]{:S(2)}, u32[]{:S(2)}) %collective-permute-start.6) | collective-permute-done | bytes 1835040 | tf_op jit(solution)/shard_map/ppermute | solution.py:369
  210.0 5.4 %step.24.refs_15_ = bf16[1792,512]{1,0:T(8,128)(2,1)} custom-call(s32[2]{0:T(128)} %pad_add_fusion.place, bf16[1792,512]{1,0:T(8,128)(2,1)} %collective-permute-done.6.got_ref.refs_5_, bf16[3584,1024]{1,0:T(8,128)(2,1)} %hidden.1.hidden_ref, bf16[1024,2048]{1,0:T(8,128)(2,1)} %bitcast.2.grad_ref.refs_0_.refs_1_, bf16[3584,512]{1,0:T(8,128)(2,1)} %own.1.rest_0_.own_ref), custom_call_target="tpu_custom_call" | custom-call | flops 2000000000 | tf_op jit(solution)/shard_map/step/pallas_call | solution.py:169
  215.4 1.6 collective-permute-done.8.got_ref.refs_6_
  217.0 6.7 %step.22.refs_13_ = bf16[1792,512]{1,0:T(8,128)(2,1)} custom-call(s32[2]{0:T(128)} %pad_add_fusion.place, bf16[1792,512]{1,0:T(8,128)(2,1)} %collective-permute-done.8.got_ref.refs_6_, bf16[3584,1024]{1,0:T(8,128)(2,1)} %hidden.1.hidden_ref, bf16[1024,2048]{1,0:T(8,128)(2,1)} %bitcast.2.grad_ref.refs_0_.refs_1_, bf16[3584,512]{1,0:T(8,128)(2,1)} %own.1.rest_0_.own_ref), custom_call_target="tpu_custom_call" | custom-call | flops 2000000000 | tf_op jit(solution)/shard_map/step/pallas_call | solution.py:169
  223.7 2.5 collective-permute-start.17
  226.2 10.9 %early.3 = (f32[512,1792]{1,0:T(8,128)}, f32[8,128]{1,0:T(8,128)}) custom-call(s32[2]{0:T(128)} %pad_add_fusion.place, bf16[1024,2048]{1,0:T(8,128)(2,1)} %bitcast.2.grad_ref.refs_0_.refs_1_, bf16[1024,2048]{1,0:T(8,128)(2,1)} %bitcast.2.grad_ref.refs_0_.refs_1_, bf16[1024,2048]{1,0:T(8,128)(2,1)} %collective-permute-done.refs_2_.refs_3_, ...), custom_call_target="tpu_custom_call" | custom-call | tf_op jit(solution)/shard_map/early/pallas_call | solution.py:312
  237.1 10.9 %early.2 = (f32[512,1792]{1,0:T(8,128)}, f32[8,128]{1,0:T(8,128)}) custom-call(s32[2]{0:T(128)} %pad_add_fusion.place, bf16[1024,2048]{1,0:T(8,128)(2,1)} %bitcast.2.grad_ref.refs_0_.refs_1_, bf16[1024,2048]{1,0:T(8,128)(2,1)} %bitcast.2.grad_ref.refs_0_.refs_1_, bf16[1024,2048]{1,0:T(8,128)(2,1)} %collective-permute-done.refs_2_.refs_3_, ...), custom_call_target="tpu_custom_call" | custom-call | tf_op jit(solution)/shard_map/early/pallas_call | solution.py:312
  248.0 1.2 collective-permute-done.13.got_ref.refs_9_
  249.2 1.3 copy-done
  250.5 4.9 %step.25.refs_16_ = bf16[1344,512]{1,0:T(8,128)(2,1)} custom-call(s32[2]{0:T(128)} %pad_add_fusion.place, bf16[1792,512]{1,0:T(8,128)(2,1)} %copy-done, bf16[3584,1024]{1,0:T(8,128)(2,1)} %hidden.1.hidden_ref, bf16[1024,2048]{1,0:T(8,128)(2,1)} %bitcast.2.grad_ref.refs_0_.refs_1_, f32[8,128]{1,0:T(8,128)} %get-tuple-element.18.rest_0_, ...), custom_call_target="tpu_custom_call" | custom-call | flops 1500000000 | tf_op jit(solution)/shard_map/step/pallas_call | solution.py:169
  255.4 0.9 collective-permute-done.15.got_ref.refs_10_
  256.3 1.2 copy-done.1
  257.6 5.9 %step.23.refs_14_ = bf16[1344,512]{1,0:T(8,128)(2,1)} custom-call(s32[2]{0:T(128)} %pad_add_fusion.place, bf16[1792,512]{1,0:T(8,128)(2,1)} %copy-done.1, bf16[3584,1024]{1,0:T(8,128)(2,1)} %hidden.1.hidden_ref, bf16[1024,2048]{1,0:T(8,128)(2,1)} %bitcast.2.grad_ref.refs_0_.refs_1_, f32[8,128]{1,0:T(8,128)} %get-tuple-element.18.rest_0_, ...), custom_call_target="tpu_custom_call" | custom-call | flops 1500000000 | tf_op jit(solution)/shard_map/step/pallas_call | solution.py:169
  263.5 11.5 %product.1 = (bf16[512,1792]{1,0:T(8,128)(2,1)}, f32[8,128]{1,0:T(8,128)}) custom-call(s32[2]{0:T(128)} %pad_add_fusion.place, bf16[1024,2048]{1,0:T(8,128)(2,1)} %bitcast.2.grad_ref.refs_0_.refs_1_, bf16[1024,2048]{1,0:T(8,128)(2,1)} %bitcast.2.grad_ref.refs_0_.refs_1_, bf16[1024,2048]{1,0:T(8,128)(2,1)} %collective-permute-done.refs_2_.refs_3_, ...), custom_call_target="tpu_custom_call" | custom-call | tf_op jit(solution)/shard_map/product/pallas_call | solution.py:312
  275.0 0.1 collective-permute-start.16
  275.1 0.5 collective-permute-start.20
  275.6 1.9 collective-permute-start.19
  277.5 12.7 %grads.1 = (bf16[512,3584]{1,0:T(8,128)(2,1)}, bf16[512,3584]{1,0:T(8,128)(2,1)}, f32[8,128]{1,0:T(8,128)}) custom-call(s32[2]{0:T(128)} %pad_add_fusion.place, bf16[1024,2048]{1,0:T(8,128)(2,1)} %bitcast.2.grad_ref.refs_0_.refs_1_, bf16[1024,2048]{1,0:T(8,128)(2,1)} %bitcast.2.grad_ref.refs_0_.refs_1_, ...), custom_call_target="tpu_custom_call" | custom-call | tf_op jit(solution)/shard_map/grads/pallas_call | solution.py:312
  290.2 3.7 %step.26 = bf16[448,512]{1,0:T(8,128)(2,1)} custom-call(s32[2]{0:T(128)} %pad_add_fusion.place, bf16[1792,512]{1,0:T(8,128)(2,1)} %copy-done.1, bf16[3584,1024]{1,0:T(8,128)(2,1)} %hidden.1.hidden_ref, bf16[1024,2048]{1,0:T(8,128)(2,1)} %bitcast.2.grad_ref.refs_0_.refs_1_, f32[8,128]{1,0:T(8,128)} %get-tuple-element.25.rest_0_), custom_call_target="tpu_custom_call" | custom-call | flops 500000000 | tf_op jit(solution)/shard_map/step/pallas_call | solution.py:169
  293.9 3.3 step.27
  297.2 2.6 collective-permute-start.21
  299.9 5.2 %final.2 = (bf16[3584,512]{1,0:T(8,128)(2,1)}, f32[8,128]{1,0:T(8,128)}) custom-call(s32[2]{0:T(128)} %pad_add_fusion.place, bf16[1792,512]{1,0:T(8,128)(2,1)} %collective-permute-done.17.one_ref, bf16[1792,512]{1,0:T(8,128)(2,1)} %collective-permute-done.18.two_ref, bf16[3584,512]{1,0:T(8,128)(2,1)} %own.1.rest_0_.own_ref, f32[8,128]{1,0:T(8,128)} %get-tuple-element.25.rest_0_), custom_call_target="tpu_custom_call" | custom-call | tf_op jit(solution)/shard_map/final/pallas_call | solution.py:232
  305.1 5.4 %join.1 = (bf16[512,3584]{1,0:T(8,128)(2,1)}, bf16[512,3584]{1,0:T(8,128)(2,1)}) custom-call(s32[2]{0:T(128)} %pad_add_fusion.place, bf16[512,1792]{1,0:T(8,128)(2,1)} %collective-permute-done.16.product_ref, bf16[512,3584]{1,0:T(8,128)(2,1)} %gate_ref.1, bf16[512,3584]{1,0:T(8,128)(2,1)} %up_ref.1, ...), custom_call_target="tpu_custom_call", output_to_operand_aliasing={{0}: (4, {}), {1}: (5, {})} | custom-call | tf_op jit(solution)/shard_map/join/pallas_call | solution.py:336
  310.4 7.7 %collective-permute-done.20.two_ref = bf16[1344,512]{1,0:T(8,128)(2,1)} collective-permute-done((bf16[1344,512]{1,0:T(8,128)(2,1)S(1)}, bf16[1344,512]{1,0:T(8,128)(2,1)}, u32[]{:S(2)}, u32[]{:S(2)}) %collective-permute-start.20) | collective-permute-done | bytes 1376288 | tf_op jit(solution)/shard_map/ppermute | solution.py:369
  318.2 6.2 %collective-permute-done.19.one_ref = bf16[1344,512]{1,0:T(8,128)(2,1)} collective-permute-done((bf16[1344,512]{1,0:T(8,128)(2,1)S(1)}, bf16[1344,512]{1,0:T(8,128)(2,1)}, u32[]{:S(2)}, u32[]{:S(2)}) %collective-permute-start.19) | collective-permute-done | bytes 1376288 | tf_op jit(solution)/shard_map/ppermute | solution.py:369
  324.4 4.7 %final.3 = (bf16[3584,512]{1,0:T(8,128)(2,1)}, f32[8,128]{1,0:T(8,128)}) custom-call(s32[2]{0:T(128)} %pad_add_fusion.place, bf16[1344,512]{1,0:T(8,128)(2,1)} %collective-permute-done.19.one_ref, bf16[1344,512]{1,0:T(8,128)(2,1)} %collective-permute-done.20.two_ref, bf16[3584,512]{1,0:T(8,128)(2,1)} %own.1.rest_0_.own_ref, ...), custom_call_target="tpu_custom_call", output_to_operand_aliasing={{0}: (4, {})} | custom-call | tf_op jit(solution)/shard_map/final/pallas_call | solution.py:232
  329.1 0.3 collective-permute-done.21
  329.4 2.2 fusion
  (29 shorter events, 0.1 us)
Async XLA Ops:
  0.6 13.6 %collective-permute-start.9 = (bf16[3584,512]{1,0:T(8,128)(2,1)}, bf16[3584,512]{1,0:T(8,128)(2,1)}, u32[]{:S(2)}, u32[]{:S(2)}) collective-permute-start(bf16[3584,512]{1,0:T(8,128)(2,1)} %param.7), channel_id=1, source_target_pairs={{0,4},{4,0},{8,12},{12,8},{16,20},{20,16},{24,28},{28,24},{1,5},{5... | collective-permute-start | bytes 11010056 | tf_op jit(solution)/shard_map/ppermute | solution.py:366
  1.1 59.0 %collective-permute-start.3 = (bf16[512,3584]{1,0:T(8,128)(2,1)}, bf16[512,3584]{1,0:T(8,128)(2,1)}, u32[]{:S(2)}, u32[]{:S(2)}) collective-permute-start(bf16[512,3584]{1,0:T(8,128)(2,1)} %gate_ref.1), channel_id=1, source_target_pairs={{0,4},{4,0},{8,12},{12,8},{16,20},{20,16},{24,28},{28,24},{1,5},{5... | collective-permute-start | bytes 11010056 | tf_op jit(solution)/shard_map/ppermute | solution.py:366
  1.2 58.9 %collective-permute-start.4 = (bf16[512,3584]{1,0:T(8,128)(2,1)}, bf16[512,3584]{1,0:T(8,128)(2,1)}, u32[]{:S(2)}, u32[]{:S(2)}) collective-permute-start(bf16[512,3584]{1,0:T(8,128)(2,1)} %up_ref.1), channel_id=1, source_target_pairs={{0,4},{4,0},{8,12},{12,8},{16,20},{20,16},{24,28},{28,24},{1,5},{5... | collective-permute-start | bytes 11010056 | tf_op jit(solution)/shard_map/ppermute | solution.py:366
  5.2 69.5 %all-to-all-start = ((bf16[8,128,2048]{2,1,0:T(8,128)(2,1)}), bf16[8,128,2048]{2,1,0:T(8,128)(2,1)}, u32[]{:S(2)}, u32[]{:S(2)}) async-start(bf16[8,128,2048]{2,1,0:T(8,128)(2,1)} %spread.1), calls=%async_computation | async-start | bytes 8388608 | tf_op jit(solution)/shard_map/all_to_all | solution.py:383
  11.7 5.3 %copy-start.4 = (bf16[1792,512]{1,0:T(8,128)(2,1)}, bf16[1792,512]{1,0:T(8,128)(2,1)S(1)}, u32[]{:S(2)}) copy-start(bf16[1792,512]{1,0:T(8,128)(2,1)S(1)} %constant_dynamic-slice_fusion.1.refs_4_) | copy-start | bytes 5505028
  11.7 42.8 %collective-permute-start.1 = (bf16[1792,512]{1,0:T(8,128)(2,1)S(1)}, bf16[1792,512]{1,0:T(8,128)(2,1)S(1)}, u32[]{:S(2)}, u32[]{:S(2)}) collective-permute-start(bf16[1792,512]{1,0:T(8,128)(2,1)S(1)} %constant_dynamic-slice_fusion.1.refs_4_), channel_id=1, source_target_pairs={{0,8},{8,16},{16,24},{24,28},{28,20},{20,12},{12,4},{4,0},{1,9},{9... | collective-permute-start | bytes 5505032 | tf_op jit(solution)/shard_map/ppermute | solution.py:369
  14.2 44.7 %collective-permute-start.2 = (bf16[1792,512]{1,0:T(8,128)(2,1)S(1)}, bf16[1792,512]{1,0:T(8,128)(2,1)}, u32[]{:S(2)}, u32[]{:S(2)}) collective-permute-start(bf16[1792,512]{1,0:T(8,128)(2,1)S(1)} %constant_dynamic-slice_fusion.1.refs_4_), channel_id=1, source_target_pairs={{4,12},{12,20},{20,28},{28,24},{24,16},{16,8},{8,0},{0,4},{5,13},{... | collective-permute-start | bytes 5505032 | tf_op jit(solution)/shard_map/ppermute | solution.py:369
  17.0 75.0 %collective-permute-start.11 = (bf16[1792,512]{1,0:T(8,128)(2,1)}, bf16[1792,512]{1,0:T(8,128)(2,1)}, u32[]{:S(2)}, u32[]{:S(2)}) collective-permute-start(bf16[1792,512]{1,0:T(8,128)(2,1)} %constant_dynamic-slice_fusion.refs_7_), channel_id=1, source_target_pairs={{4,12},{12,20},{20,28},{28,24},{24,16},{16,8},{8,0},{0,4},{5,13},{... | collective-permute-start | bytes 5505032 | tf_op jit(solution)/shard_map/ppermute | solution.py:369
  54.5 1.3 copy-start.5
  55.8 43.3 %collective-permute-start.10 = (bf16[1792,512]{1,0:T(8,128)(2,1)}, bf16[1792,512]{1,0:T(8,128)(2,1)}, u32[]{:S(2)}, u32[]{:S(2)}) collective-permute-start(bf16[1792,512]{1,0:T(8,128)(2,1)} %constant_dynamic-slice_fusion.refs_7_), channel_id=1, source_target_pairs={{0,8},{8,16},{16,24},{24,28},{28,20},{20,12},{12,4},{4,0},{1,9},{9... | collective-permute-start | bytes 5505032 | tf_op jit(solution)/shard_map/ppermute | solution.py:369
  80.1 51.2 %collective-permute-start.5 = (bf16[1792,512]{1,0:T(8,128)(2,1)}, bf16[1792,512]{1,0:T(8,128)(2,1)S(1)}, u32[]{:S(2)}, u32[]{:S(2)}) collective-permute-start(bf16[1792,512]{1,0:T(8,128)(2,1)} %step.14), channel_id=1, source_target_pairs={{4,12},{12,20},{20,28},{28,24},{24,16},{16,8},{8,0},{0,4},{5,13},{... | collective-permute-start | bytes 5505032 | tf_op jit(solution)/shard_map/ppermute | solution.py:369
  86.7 51.7 %collective-permute-start.7 = (bf16[1792,512]{1,0:T(8,128)(2,1)}, bf16[1792,512]{1,0:T(8,128)(2,1)S(1)}, u32[]{:S(2)}, u32[]{:S(2)}) collective-permute-start(bf16[1792,512]{1,0:T(8,128)(2,1)} %step.16), channel_id=1, source_target_pairs={{0,8},{8,16},{16,24},{24,28},{28,20},{20,12},{12,4},{4,0},{1,9},{9... | collective-permute-start | bytes 5505032 | tf_op jit(solution)/shard_map/ppermute | solution.py:369
  87.4 138.8 %collective-permute-start = (bf16[1024,2048]{1,0:T(8,128)(2,1)}, bf16[1024,2048]{1,0:T(8,128)(2,1)}, u32[]{:S(2)}, u32[]{:S(2)}) collective-permute-start(bf16[1024,2048]{1,0:T(8,128)(2,1)} %bitcast.2.grad_ref.refs_0_.refs_1_), channel_id=1, source_target_pairs={{0,4},{4,0},{8,12},{12,8},{16,20},{20,16},{24,28},{28,24},{1,5},{5... | collective-permute-start | bytes 12582920 | tf_op jit(solution)/shard_map/ppermute | solution.py:366
  97.4 73.3 %collective-permute-start.12 = (bf16[1792,512]{1,0:T(8,128)(2,1)}, bf16[1792,512]{1,0:T(8,128)(2,1)}, u32[]{:S(2)}, u32[]{:S(2)}) collective-permute-start(bf16[1792,512]{1,0:T(8,128)(2,1)} %step.18), channel_id=1, source_target_pairs={{4,12},{12,20},{20,28},{28,24},{24,16},{16,8},{8,0},{0,4},{5,13},{... | collective-permute-start | bytes 5505032 | tf_op jit(solution)/shard_map/ppermute | solution.py:369
  105.7 72.0 %collective-permute-start.14 = (bf16[1792,512]{1,0:T(8,128)(2,1)}, bf16[1792,512]{1,0:T(8,128)(2,1)}, u32[]{:S(2)}, u32[]{:S(2)}) collective-permute-start(bf16[1792,512]{1,0:T(8,128)(2,1)} %step.20), channel_id=1, source_target_pairs={{0,8},{8,16},{16,24},{24,28},{28,20},{20,12},{12,4},{4,0},{1,9},{9... | collective-permute-start | bytes 5505032 | tf_op jit(solution)/shard_map/ppermute | solution.py:369
  131.3 1.2 copy-start.2
  137.8 72.2 %collective-permute-start.6 = (bf16[1792,512]{1,0:T(8,128)(2,1)}, bf16[1792,512]{1,0:T(8,128)(2,1)}, u32[]{:S(2)}, u32[]{:S(2)}) collective-permute-start(bf16[1792,512]{1,0:T(8,128)(2,1)} %step.15), channel_id=1, source_target_pairs={{4,12},{12,20},{20,28},{28,24},{24,16},{16,8},{8,0},{0,4},{5,13},{... | collective-permute-start | bytes 5505032 | tf_op jit(solution)/shard_map/ppermute | solution.py:369
  138.4 1.2 copy-start.3
  146.3 70.7 %collective-permute-start.8 = (bf16[1792,512]{1,0:T(8,128)(2,1)}, bf16[1792,512]{1,0:T(8,128)(2,1)}, u32[]{:S(2)}, u32[]{:S(2)}) collective-permute-start(bf16[1792,512]{1,0:T(8,128)(2,1)} %step.17), channel_id=1, source_target_pairs={{0,8},{8,16},{16,24},{24,28},{28,20},{20,12},{12,4},{4,0},{1,9},{9... | collective-permute-start | bytes 5505032 | tf_op jit(solution)/shard_map/ppermute | solution.py:369
  176.0 73.2 %collective-permute-start.13 = (bf16[1792,512]{1,0:T(8,128)(2,1)}, bf16[1792,512]{1,0:T(8,128)(2,1)S(1)}, u32[]{:S(2)}, u32[]{:S(2)}) collective-permute-start(bf16[1792,512]{1,0:T(8,128)(2,1)} %step.19), channel_id=1, source_target_pairs={{4,12},{12,20},{20,28},{28,24},{24,16},{16,8},{8,0},{0,4},{5,13},{... | collective-permute-start | bytes 5505032 | tf_op jit(solution)/shard_map/ppermute | solution.py:369
  184.4 72.0 %collective-permute-start.15 = (bf16[1792,512]{1,0:T(8,128)(2,1)}, bf16[1792,512]{1,0:T(8,128)(2,1)S(1)}, u32[]{:S(2)}, u32[]{:S(2)}) collective-permute-start(bf16[1792,512]{1,0:T(8,128)(2,1)} %step.21), channel_id=1, source_target_pairs={{0,8},{8,16},{16,24},{24,28},{28,20},{20,12},{12,4},{4,0},{1,9},{9... | collective-permute-start | bytes 5505032 | tf_op jit(solution)/shard_map/ppermute | solution.py:369
  215.4 81.9 %collective-permute-start.18 = (bf16[1792,512]{1,0:T(8,128)(2,1)}, bf16[1792,512]{1,0:T(8,128)(2,1)}, u32[]{:S(2)}, u32[]{:S(2)}) collective-permute-start(bf16[1792,512]{1,0:T(8,128)(2,1)} %step.24.refs_15_), channel_id=1, source_target_pairs={{4,12},{12,20},{20,28},{28,24},{24,16},{16,8},{8,0},{0,4},{5,13},{... | collective-permute-start | bytes 5505032 | tf_op jit(solution)/shard_map/ppermute | solution.py:369
  223.7 76.2 %collective-permute-start.17 = (bf16[1792,512]{1,0:T(8,128)(2,1)}, bf16[1792,512]{1,0:T(8,128)(2,1)}, u32[]{:S(2)}, u32[]{:S(2)}) collective-permute-start(bf16[1792,512]{1,0:T(8,128)(2,1)} %step.22.refs_13_), channel_id=1, source_target_pairs={{0,8},{8,16},{16,24},{24,28},{28,20},{20,12},{12,4},{4,0},{1,9},{9... | collective-permute-start | bytes 5505032 | tf_op jit(solution)/shard_map/ppermute | solution.py:369
  249.2 1.3 copy-start
  256.3 1.2 copy-start.1
  263.5 11.6 %copy-start.6 = (bf16[1344,512]{1,0:T(8,128)(2,1)S(1)}, bf16[1344,512]{1,0:T(8,128)(2,1)}, u32[]{:S(2)}) copy-start(bf16[1344,512]{1,0:T(8,128)(2,1)} %step.25.refs_16_) | copy-start | bytes 4128772
  263.5 12.1 %copy-start.7 = (bf16[1344,512]{1,0:T(8,128)(2,1)S(1)}, bf16[1344,512]{1,0:T(8,128)(2,1)}, u32[]{:S(2)}) copy-start(bf16[1344,512]{1,0:T(8,128)(2,1)} %step.23.refs_14_) | copy-start | bytes 4128772
  275.0 30.1 %collective-permute-start.16 = (bf16[512,1792]{1,0:T(8,128)(2,1)}, bf16[512,1792]{1,0:T(8,128)(2,1)}, u32[]{:S(2)}, u32[]{:S(2)}) collective-permute-start(bf16[512,1792]{1,0:T(8,128)(2,1)} %get-tuple-element.20), channel_id=1, source_target_pairs={{0,4},{4,0},{8,12},{12,8},{16,20},{20,16},{24,28},{28,24},{1,5},{5... | collective-permute-start | bytes 5505032 | tf_op jit(solution)/shard_map/ppermute | solution.py:366
  275.1 43.1 %collective-permute-start.20 = (bf16[1344,512]{1,0:T(8,128)(2,1)S(1)}, bf16[1344,512]{1,0:T(8,128)(2,1)}, u32[]{:S(2)}, u32[]{:S(2)}) collective-permute-start(bf16[1344,512]{1,0:T(8,128)(2,1)S(1)} %copy-done.6), channel_id=1, source_target_pairs={{4,12},{12,20},{20,28},{28,24},{24,16},{16,8},{8,0},{0,4},{5,13},{... | collective-permute-start | bytes 4128776 | tf_op jit(solution)/shard_map/ppermute | solution.py:369
  275.6 48.8 %collective-permute-start.19 = (bf16[1344,512]{1,0:T(8,128)(2,1)S(1)}, bf16[1344,512]{1,0:T(8,128)(2,1)}, u32[]{:S(2)}, u32[]{:S(2)}) collective-permute-start(bf16[1344,512]{1,0:T(8,128)(2,1)S(1)} %copy-done.7), channel_id=1, source_target_pairs={{0,8},{8,16},{16,24},{24,28},{28,20},{20,12},{12,4},{4,0},{1,9},{9... | collective-permute-start | bytes 4128776 | tf_op jit(solution)/shard_map/ppermute | solution.py:369
  297.2 32.2 %collective-permute-start.21 = (bf16[448,512]{1,0:T(8,128)(2,1)}, bf16[448,512]{1,0:T(8,128)(2,1)S(1)}, u32[]{:S(2)}, u32[]{:S(2)}) collective-permute-start(bf16[448,512]{1,0:T(8,128)(2,1)} %step.26), channel_id=1, source_target_pairs={{0,8},{8,16},{16,24},{24,28},{28,20},{20,12},{12,4},{4,0},{1,9},{9... | collective-permute-start | bytes 1376264 | tf_op jit(solution)/shard_map/ppermute | solution.py:369
  299.9 29.5 %collective-permute-start.22 = (bf16[448,512]{1,0:T(8,128)(2,1)}, bf16[448,512]{1,0:T(8,128)(2,1)}, u32[]{:S(2)}, u32[]{:S(2)}) collective-permute-start(bf16[448,512]{1,0:T(8,128)(2,1)} %step.27), channel_id=1, source_target_pairs={{4,12},{12,20},{20,28},{28,24},{24,16},{16,8},{8,0},{0,4},{5,13},{... | collective-permute-start | bytes 1376264 | tf_op jit(solution)/shard_map/ppermute | solution.py:369

commit v5 on v4

--- a/solution.py
+++ b/solution.py
@@ -9,7 +9,7 @@
 from jax.sharding import PartitionSpec as P
 
 VMEM = 60 * 1024 * 1024
-STEP_FLOPS, ARRIVED_FLOPS = 2e9, 7e9
+STEP_FLOPS, ARRIVED_FLOPS = 2e9, 1.4e10
 F32, BF16 = jnp.float32, jnp.bfloat16
 ANY = pl.BlockSpec(memory_space=pl.ANY)
 

time: 334 us -> 334 us (level)
  transfers between devices with their start and end apart: 24 -> 24, of which waited for: 14 -> 9; matrix products, arithmetic and copies ran while one was open for 2% -> 2% of each run, Pallas kernels for 51% -> 51%
where the time goes in v5:
time: 334 us; the launch traced here: 332 us
  Pallas kernels  169 us (51%)
  waiting for transfers between devices  125 us (37%)
  starting transfers between devices  25 us (7%)
  local copies, waits for them, and re-layouts  9.43 us (3%)
    ppermute x18, waiting for transfers between devices, send(): return lax.ppermute(x, 'dp', rings[flow])  125 us
    pallas_call x14, Pallas kernels, step_call(): call(functools.partial(step_kernel, flow, j, line), (high - low,), [pl.Bl...  78 us
    pallas_call x4, Pallas kernels, product_call(): call(functools.partial(product_kernel, line, slots, counts), (steps,), ro...  46 us
    ppermute x18, starting transfers between devices, send(): return lax.ppermute(x, 'dp', rings[flow])  19 us
    pallas_call x1, Pallas kernels, hidden_call(): call(hidden_kernel, (units // tile,), [pl.BlockSpec((tokens, tile), lambd...  14.5 us
    pallas_call x1, Pallas kernels, own_call(): call(own_kernel, (steps,), term_specs(tile, tokens, block, 0, lambda s: 0...  10.5 us
    pallas_call x2, Pallas kernels, final_call(): call(functools.partial(final_kernel, scale, line), (rows // tile,), [got,...  9.9 us
  transfers between devices with their start and end apart: 24, of which 9 were waited for; matrix products, arithmetic and copies ran while one was open for 2% of the time, Pallas kernels for 51%

profile of v5, /device:TPU:0, one launch (start us, length us, event | category | flops | bytes accessed | tf_op | source)
XLA Modules:
  0.0 331.6 jit_solution(6454837293766931266)
XLA Ops:
  0.6 0.5 collective-permute-start.9
  1.1 0.1 collective-permute-start.3
  1.2 0.4 collective-permute-start.4
  1.7 3.5 %spread.1 = bf16[8,128,2048]{2,1,0:T(8,128)(2,1)} custom-call(bf16[128,4096]{1,0:T(8,128)(2,1)} %grad_ref.1), custom_call_target="tpu_custom_call" | custom-call | tf_op jit(solution)/shard_map/spread/pallas_call | solution.py:74
  5.2 4.9 %all-to-all-start = ((bf16[8,128,2048]{2,1,0:T(8,128)(2,1)}), bf16[8,128,2048]{2,1,0:T(8,128)(2,1)}, u32[]{:S(2)}, u32[]{:S(2)}) async-start(bf16[8,128,2048]{2,1,0:T(8,128)(2,1)} %spread.1), calls=%async_computation | async-start | bytes 8388608 | tf_op jit(solution)/shard_map/all_to_all | solution.py:383
  10.1 1.6 constant_dynamic-slice_fusion.1.refs_4_
  11.7 2.5 collective-permute-start.1
  14.1 0.0 collective-permute-start.2
  14.2 0.0 collective-permute-done.9
  14.2 2.8 constant_dynamic-slice_fusion.refs_7_
  17.0 0.1 collective-permute-start.11
  17.1 0.6 pad_add_fusion.place
  17.7 36.8 %collective-permute-done.1.refs_0_.got_ref.refs_4_ = bf16[1792,512]{1,0:T(8,128)(2,1)} collective-permute-done((bf16[1792,512]{1,0:T(8,128)(2,1)S(1)}, bf16[1792,512]{1,0:T(8,128)(2,1)}, u32[]{:S(2)}, u32[]{:S(2)}) %collective-permute-start.1) | collective-permute-done | bytes 1835040 | tf_op jit(solution)/shard_map/ppermute | solution.py:369
  54.5 2.6 collective-permute-start.10
  57.1 1.3 arrived.1.rest_0_
  58.3 0.0 collective-permute-done.3.gate_sib
  58.3 0.0 collective-permute-done.4.up_sib
  58.3 14.5 %hidden.1.hidden_ref = bf16[3584,1024]{1,0:T(8,128)(2,1)} custom-call(s32[2]{0:T(128)} %pad_add_fusion.place, bf16[512,3584]{1,0:T(8,128)(2,1)} %gate_ref.1, bf16[512,3584]{1,0:T(8,128)(2,1)} %up_ref.1, bf16[512,3584]{1,0:T(8,128)(2,1)} %collective-permute-done.3.gate_sib, bf16[512,3584]{1,0:T(8,128)(2,1)} %collective-permute-done.4.up_sib), custom_call_target="tpu_custom_call" | custom-call | tf_op jit(solution)/shard_map/hidden/pallas_call | solution.py:104
  72.9 0.0 all-to-all-done
  72.9 5.3 %step.14 = bf16[1792,512]{1,0:T(8,128)(2,1)} custom-call(s32[2]{0:T(128)} %pad_add_fusion.place, bf16[1792,512]{1,0:T(8,128)(2,1)} %collective-permute-done.2.refs_1_.got_ref.refs_7_, bf16[3584,1024]{1,0:T(8,128)(2,1)} %hidden.1.hidden_ref, bf16[1024,2048]{1,0:T(8,128)(2,1)} %bitcast.2.grad_ref.refs_0_.refs_1_, f32[8,128]{1,0:T(8,128)} %arrived.1.rest_0_), custom_call_target="tpu_custom_call" | custom-call | flops 2000000000 | tf_op jit(solution)/shard_map/step/pallas_call | solution.py:169
  78.2 6.7 %step.16 = bf16[1792,512]{1,0:T(8,128)(2,1)} custom-call(s32[2]{0:T(128)} %pad_add_fusion.place, bf16[1792,512]{1,0:T(8,128)(2,1)} %collective-permute-done.1.refs_0_.got_ref.refs_4_, bf16[3584,1024]{1,0:T(8,128)(2,1)} %hidden.1.hidden_ref, bf16[1024,2048]{1,0:T(8,128)(2,1)} %bitcast.2.grad_ref.refs_0_.refs_1_, f32[8,128]{1,0:T(8,128)} %arrived.1.rest_0_), custom_call_target="tpu_custom_call" | custom-call | flops 2000000000 | tf_op jit(solution)/shard_map/step/pallas_call | solution.py:169
  84.9 0.7 collective-permute-start.7
  85.6 7.7 %collective-permute-done.11.got_ref.refs_11_ = bf16[1792,512]{1,0:T(8,128)(2,1)} collective-permute-done((bf16[1792,512]{1,0:T(8,128)(2,1)}, bf16[1792,512]{1,0:T(8,128)(2,1)}, u32[]{:S(2)}, u32[]{:S(2)}) %collective-permute-start.11) | collective-permute-done | bytes 1835040 | tf_op jit(solution)/shard_map/ppermute | solution.py:369
  93.3 5.4 %step.18 = bf16[1792,512]{1,0:T(8,128)(2,1)} custom-call(s32[2]{0:T(128)} %pad_add_fusion.place, bf16[1792,512]{1,0:T(8,128)(2,1)} %collective-permute-done.11.got_ref.refs_11_, bf16[3584,1024]{1,0:T(8,128)(2,1)} %hidden.1.hidden_ref, bf16[1024,2048]{1,0:T(8,128)(2,1)} %bitcast.2.grad_ref.refs_0_.refs_1_), custom_call_target="tpu_custom_call" | custom-call | flops 2000000000 | tf_op jit(solution)/shard_map/step/pallas_call | solution.py:169
  98.6 6.7 %step.20 = bf16[1792,512]{1,0:T(8,128)(2,1)} custom-call(s32[2]{0:T(128)} %pad_add_fusion.place, bf16[1792,512]{1,0:T(8,128)(2,1)} %collective-permute-done.10.got_ref.refs_8_, bf16[3584,1024]{1,0:T(8,128)(2,1)} %hidden.1.hidden_ref, bf16[1024,2048]{1,0:T(8,128)(2,1)} %bitcast.2.grad_ref.refs_0_.refs_1_), custom_call_target="tpu_custom_call" | custom-call | flops 2000000000 | tf_op jit(solution)/shard_map/step/pallas_call | solution.py:169
  105.3 0.7 collective-permute-start.14
  106.0 26.5 %collective-permute-done.5.got_ref.refs_6_ = bf16[1792,512]{1,0:T(8,128)(2,1)S(1)} collective-permute-done((bf16[1792,512]{1,0:T(8,128)(2,1)}, bf16[1792,512]{1,0:T(8,128)(2,1)S(1)}, u32[]{:S(2)}, u32[]{:S(2)}) %collective-permute-start.5) | collective-permute-done | bytes 1835040 | tf_op jit(solution)/shard_map/ppermute | solution.py:369
  132.5 1.2 copy-done.2
  133.7 5.3 %step.15 = bf16[1792,512]{1,0:T(8,128)(2,1)} custom-call(s32[2]{0:T(128)} %pad_add_fusion.place, bf16[1792,512]{1,0:T(8,128)(2,1)} %copy-done.2, bf16[3584,1024]{1,0:T(8,128)(2,1)} %hidden.1.hidden_ref, bf16[1024,2048]{1,0:T(8,128)(2,1)} %bitcast.2.grad_ref.refs_0_.refs_1_), custom_call_target="tpu_custom_call" | custom-call | flops 2000000000 | tf_op jit(solution)/shard_map/step/pallas_call | solution.py:169
  139.1 0.0 copy-start.3
  139.1 1.2 copy-done.3
  140.3 6.7 %step.17 = bf16[1792,512]{1,0:T(8,128)(2,1)} custom-call(s32[2]{0:T(128)} %pad_add_fusion.place, bf16[1792,512]{1,0:T(8,128)(2,1)} %copy-done.3, bf16[3584,1024]{1,0:T(8,128)(2,1)} %hidden.1.hidden_ref, bf16[1024,2048]{1,0:T(8,128)(2,1)} %bitcast.2.grad_ref.refs_0_.refs_1_), custom_call_target="tpu_custom_call" | custom-call | flops 2000000000 | tf_op jit(solution)/shard_map/step/pallas_call | solution.py:169
  147.0 2.0 collective-permute-start.8
  149.0 22.9 %collective-permute-done.12.got_ref.refs_9_ = bf16[1792,512]{1,0:T(8,128)(2,1)} collective-permute-done((bf16[1792,512]{1,0:T(8,128)(2,1)}, bf16[1792,512]{1,0:T(8,128)(2,1)}, u32[]{:S(2)}, u32[]{:S(2)}) %collective-permute-start.12) | collective-permute-done | bytes 1835040 | tf_op jit(solution)/shard_map/ppermute | solution.py:369
  171.9 5.3 %step.19 = bf16[1792,512]{1,0:T(8,128)(2,1)} custom-call(s32[2]{0:T(128)} %pad_add_fusion.place, bf16[1792,512]{1,0:T(8,128)(2,1)} %collective-permute-done.12.got_ref.refs_9_, bf16[3584,1024]{1,0:T(8,128)(2,1)} %hidden.1.hidden_ref, bf16[1024,2048]{1,0:T(8,128)(2,1)} %bitcast.2.grad_ref.refs_0_.refs_1_), custom_call_target="tpu_custom_call" | custom-call | flops 2000000000 | tf_op jit(solution)/shard_map/step/pallas_call | solution.py:169
  177.3 6.7 %step.21 = bf16[1792,512]{1,0:T(8,128)(2,1)} custom-call(s32[2]{0:T(128)} %pad_add_fusion.place, bf16[1792,512]{1,0:T(8,128)(2,1)} %collective-permute-done.14.got_ref.refs_8_, bf16[3584,1024]{1,0:T(8,128)(2,1)} %hidden.1.hidden_ref, bf16[1024,2048]{1,0:T(8,128)(2,1)} %bitcast.2.grad_ref.refs_0_.refs_1_), custom_call_target="tpu_custom_call" | custom-call | flops 2000000000 | tf_op jit(solution)/shard_map/step/pallas_call | solution.py:169
  184.0 2.0 collective-permute-start.15
  186.0 10.5 %own.1.rest_0_.own_ref = bf16[3584,512]{1,0:T(8,128)(2,1)} custom-call(s32[2]{0:T(128)} %pad_add_fusion.place, bf16[3584,1024]{1,0:T(8,128)(2,1)} %hidden.1.hidden_ref, bf16[1024,2048]{1,0:T(8,128)(2,1)} %bitcast.2.grad_ref.refs_0_.refs_1_), custom_call_target="tpu_custom_call" | custom-call | tf_op jit(solution)/shard_map/own/pallas_call | solution.py:190
  196.4 14.8 %collective-permute-done.6.got_ref.refs_5_ = bf16[1792,512]{1,0:T(8,128)(2,1)} collective-permute-done((bf16[1792,512]{1,0:T(8,128)(2,1)}, bf16[1792,512]{1,0:T(8,128)(2,1)}, u32[]{:S(2)}, u32[]{:S(2)}) %collective-permute-start.6) | collective-permute-done | bytes 1835040 | tf_op jit(solution)/shard_map/ppermute | solution.py:369
  211.3 5.4 %step.24.refs_15_ = bf16[1792,512]{1,0:T(8,128)(2,1)} custom-call(s32[2]{0:T(128)} %pad_add_fusion.place, bf16[1792,512]{1,0:T(8,128)(2,1)} %collective-permute-done.6.got_ref.refs_5_, bf16[3584,1024]{1,0:T(8,128)(2,1)} %hidden.1.hidden_ref, bf16[1024,2048]{1,0:T(8,128)(2,1)} %bitcast.2.grad_ref.refs_0_.refs_1_, bf16[3584,512]{1,0:T(8,128)(2,1)} %own.1.rest_0_.own_ref), custom_call_target="tpu_custom_call" | custom-call | flops 2000000000 | tf_op jit(solution)/shard_map/step/pallas_call | solution.py:169
  216.6 6.7 %step.22.refs_13_ = bf16[1792,512]{1,0:T(8,128)(2,1)} custom-call(s32[2]{0:T(128)} %pad_add_fusion.place, bf16[1792,512]{1,0:T(8,128)(2,1)} %collective-permute-done.8.got_ref.refs_6_, bf16[3584,1024]{1,0:T(8,128)(2,1)} %hidden.1.hidden_ref, bf16[1024,2048]{1,0:T(8,128)(2,1)} %bitcast.2.grad_ref.refs_0_.refs_1_, bf16[3584,512]{1,0:T(8,128)(2,1)} %own.1.rest_0_.own_ref), custom_call_target="tpu_custom_call" | custom-call | flops 2000000000 | tf_op jit(solution)/shard_map/step/pallas_call | solution.py:169
  223.3 3.1 collective-permute-start.17
  226.4 10.9 %early.3 = (f32[512,1792]{1,0:T(8,128)}, f32[8,128]{1,0:T(8,128)}) custom-call(s32[2]{0:T(128)} %pad_add_fusion.place, bf16[1024,2048]{1,0:T(8,128)(2,1)} %bitcast.2.grad_ref.refs_0_.refs_1_, bf16[1024,2048]{1,0:T(8,128)(2,1)} %bitcast.2.grad_ref.refs_0_.refs_1_, bf16[1024,2048]{1,0:T(8,128)(2,1)} %collective-permute-done.refs_2_.refs_3_, ...), custom_call_target="tpu_custom_call" | custom-call | tf_op jit(solution)/shard_map/early/pallas_call | solution.py:312
  237.3 10.9 %early.2 = (f32[512,1792]{1,0:T(8,128)}, f32[8,128]{1,0:T(8,128)}) custom-call(s32[2]{0:T(128)} %pad_add_fusion.place, bf16[1024,2048]{1,0:T(8,128)(2,1)} %bitcast.2.grad_ref.refs_0_.refs_1_, bf16[1024,2048]{1,0:T(8,128)(2,1)} %bitcast.2.grad_ref.refs_0_.refs_1_, bf16[1024,2048]{1,0:T(8,128)(2,1)} %collective-permute-done.refs_2_.refs_3_, ...), custom_call_target="tpu_custom_call" | custom-call | tf_op jit(solution)/shard_map/early/pallas_call | solution.py:312
  248.1 2.4 collective-permute-done.13.got_ref.refs_9_
  250.5 1.3 copy-done
  251.8 4.9 %step.25.refs_16_ = bf16[1344,512]{1,0:T(8,128)(2,1)} custom-call(s32[2]{0:T(128)} %pad_add_fusion.place, bf16[1792,512]{1,0:T(8,128)(2,1)} %copy-done, bf16[3584,1024]{1,0:T(8,128)(2,1)} %hidden.1.hidden_ref, bf16[1024,2048]{1,0:T(8,128)(2,1)} %bitcast.2.grad_ref.refs_0_.refs_1_, f32[8,128]{1,0:T(8,128)} %get-tuple-element.18.rest_0_, ...), custom_call_target="tpu_custom_call" | custom-call | flops 1500000000 | tf_op jit(solution)/shard_map/step/pallas_call | solution.py:169
  256.7 1.2 copy-done.1
  257.9 5.9 %step.23.refs_14_ = bf16[1344,512]{1,0:T(8,128)(2,1)} custom-call(s32[2]{0:T(128)} %pad_add_fusion.place, bf16[1792,512]{1,0:T(8,128)(2,1)} %copy-done.1, bf16[3584,1024]{1,0:T(8,128)(2,1)} %hidden.1.hidden_ref, bf16[1024,2048]{1,0:T(8,128)(2,1)} %bitcast.2.grad_ref.refs_0_.refs_1_, f32[8,128]{1,0:T(8,128)} %get-tuple-element.18.rest_0_, ...), custom_call_target="tpu_custom_call" | custom-call | flops 1500000000 | tf_op jit(solution)/shard_map/step/pallas_call | solution.py:169
  263.8 11.5 %product.1 = (bf16[512,1792]{1,0:T(8,128)(2,1)}, f32[8,128]{1,0:T(8,128)}) custom-call(s32[2]{0:T(128)} %pad_add_fusion.place, bf16[1024,2048]{1,0:T(8,128)(2,1)} %bitcast.2.grad_ref.refs_0_.refs_1_, bf16[1024,2048]{1,0:T(8,128)(2,1)} %bitcast.2.grad_ref.refs_0_.refs_1_, bf16[1024,2048]{1,0:T(8,128)(2,1)} %collective-permute-done.refs_2_.refs_3_, ...), custom_call_target="tpu_custom_call" | custom-call | tf_op jit(solution)/shard_map/product/pallas_call | solution.py:312
  275.3 0.1 collective-permute-start.16
  275.4 0.5 collective-permute-start.20
  275.9 2.3 collective-permute-start.19
  278.2 12.7 %grads.1 = (bf16[512,3584]{1,0:T(8,128)(2,1)}, bf16[512,3584]{1,0:T(8,128)(2,1)}, f32[8,128]{1,0:T(8,128)}) custom-call(s32[2]{0:T(128)} %pad_add_fusion.place, bf16[1024,2048]{1,0:T(8,128)(2,1)} %bitcast.2.grad_ref.refs_0_.refs_1_, bf16[1024,2048]{1,0:T(8,128)(2,1)} %bitcast.2.grad_ref.refs_0_.refs_1_, ...), custom_call_target="tpu_custom_call" | custom-call | tf_op jit(solution)/shard_map/grads/pallas_call | solution.py:312
  290.9 3.7 %step.26 = bf16[448,512]{1,0:T(8,128)(2,1)} custom-call(s32[2]{0:T(128)} %pad_add_fusion.place, bf16[1792,512]{1,0:T(8,128)(2,1)} %copy-done.1, bf16[3584,1024]{1,0:T(8,128)(2,1)} %hidden.1.hidden_ref, bf16[1024,2048]{1,0:T(8,128)(2,1)} %bitcast.2.grad_ref.refs_0_.refs_1_, f32[8,128]{1,0:T(8,128)} %get-tuple-element.25.rest_0_), custom_call_target="tpu_custom_call" | custom-call | flops 500000000 | tf_op jit(solution)/shard_map/step/pallas_call | solution.py:169
  294.6 3.3 %step.27 = bf16[448,512]{1,0:T(8,128)(2,1)} custom-call(s32[2]{0:T(128)} %pad_add_fusion.place, bf16[1792,512]{1,0:T(8,128)(2,1)} %copy-done, bf16[3584,1024]{1,0:T(8,128)(2,1)} %hidden.1.hidden_ref, bf16[1024,2048]{1,0:T(8,128)(2,1)} %bitcast.2.grad_ref.refs_0_.refs_1_, f32[8,128]{1,0:T(8,128)} %get-tuple-element.25.rest_0_), custom_call_target="tpu_custom_call" | custom-call | flops 500000000 | tf_op jit(solution)/shard_map/step/pallas_call | solution.py:169
  298.0 2.6 collective-permute-start.21
  300.6 5.2 %final.2 = (bf16[3584,512]{1,0:T(8,128)(2,1)}, f32[8,128]{1,0:T(8,128)}) custom-call(s32[2]{0:T(128)} %pad_add_fusion.place, bf16[1792,512]{1,0:T(8,128)(2,1)} %collective-permute-done.17.one_ref, bf16[1792,512]{1,0:T(8,128)(2,1)} %collective-permute-done.18.two_ref, bf16[3584,512]{1,0:T(8,128)(2,1)} %own.1.rest_0_.own_ref, f32[8,128]{1,0:T(8,128)} %get-tuple-element.25.rest_0_), custom_call_target="tpu_custom_call" | custom-call | tf_op jit(solution)/shard_map/final/pallas_call | solution.py:232
  305.8 5.4 %join.1 = (bf16[512,3584]{1,0:T(8,128)(2,1)}, bf16[512,3584]{1,0:T(8,128)(2,1)}) custom-call(s32[2]{0:T(128)} %pad_add_fusion.place, bf16[512,1792]{1,0:T(8,128)(2,1)} %collective-permute-done.16.product_ref, bf16[512,3584]{1,0:T(8,128)(2,1)} %gate_ref.1, bf16[512,3584]{1,0:T(8,128)(2,1)} %up_ref.1, ...), custom_call_target="tpu_custom_call", output_to_operand_aliasing={{0}: (4, {}), {1}: (5, {})} | custom-call | tf_op jit(solution)/shard_map/join/pallas_call | solution.py:336
  311.1 8.3 %collective-permute-done.20.two_ref = bf16[1344,512]{1,0:T(8,128)(2,1)} collective-permute-done((bf16[1344,512]{1,0:T(8,128)(2,1)S(1)}, bf16[1344,512]{1,0:T(8,128)(2,1)}, u32[]{:S(2)}, u32[]{:S(2)}) %collective-permute-start.20) | collective-permute-done | bytes 1376288 | tf_op jit(solution)/shard_map/ppermute | solution.py:369
  319.4 4.5 %collective-permute-done.19.one_ref = bf16[1344,512]{1,0:T(8,128)(2,1)} collective-permute-done((bf16[1344,512]{1,0:T(8,128)(2,1)S(1)}, bf16[1344,512]{1,0:T(8,128)(2,1)}, u32[]{:S(2)}, u32[]{:S(2)}) %collective-permute-start.19) | collective-permute-done | bytes 1376288 | tf_op jit(solution)/shard_map/ppermute | solution.py:369
  323.9 4.7 %final.3 = (bf16[3584,512]{1,0:T(8,128)(2,1)}, f32[8,128]{1,0:T(8,128)}) custom-call(s32[2]{0:T(128)} %pad_add_fusion.place, bf16[1344,512]{1,0:T(8,128)(2,1)} %collective-permute-done.19.one_ref, bf16[1344,512]{1,0:T(8,128)(2,1)} %collective-permute-done.20.two_ref, bf16[3584,512]{1,0:T(8,128)(2,1)} %own.1.rest_0_.own_ref, ...), custom_call_target="tpu_custom_call", output_to_operand_aliasing={{0}: (4, {})} | custom-call | tf_op jit(solution)/shard_map/final/pallas_call | solution.py:232
  328.6 0.8 collective-permute-done.21
  329.4 2.2 fusion
  (27 shorter events, 0.1 us)
Async XLA Ops:
  0.6 13.5 %collective-permute-start.9 = (bf16[3584,512]{1,0:T(8,128)(2,1)}, bf16[3584,512]{1,0:T(8,128)(2,1)}, u32[]{:S(2)}, u32[]{:S(2)}) collective-permute-start(bf16[3584,512]{1,0:T(8,128)(2,1)} %param.7), channel_id=1, source_target_pairs={{0,4},{4,0},{8,12},{12,8},{16,20},{20,16},{24,28},{28,24},{1,5},{5... | collective-permute-start | bytes 11010056 | tf_op jit(solution)/shard_map/ppermute | solution.py:366
  1.1 57.2 %collective-permute-start.3 = (bf16[512,3584]{1,0:T(8,128)(2,1)}, bf16[512,3584]{1,0:T(8,128)(2,1)}, u32[]{:S(2)}, u32[]{:S(2)}) collective-permute-start(bf16[512,3584]{1,0:T(8,128)(2,1)} %gate_ref.1), channel_id=1, source_target_pairs={{0,4},{4,0},{8,12},{12,8},{16,20},{20,16},{24,28},{28,24},{1,5},{5... | collective-permute-start | bytes 11010056 | tf_op jit(solution)/shard_map/ppermute | solution.py:366
  1.2 57.1 %collective-permute-start.4 = (bf16[512,3584]{1,0:T(8,128)(2,1)}, bf16[512,3584]{1,0:T(8,128)(2,1)}, u32[]{:S(2)}, u32[]{:S(2)}) collective-permute-start(bf16[512,3584]{1,0:T(8,128)(2,1)} %up_ref.1), channel_id=1, source_target_pairs={{0,4},{4,0},{8,12},{12,8},{16,20},{20,16},{24,28},{28,24},{1,5},{5... | collective-permute-start | bytes 11010056 | tf_op jit(solution)/shard_map/ppermute | solution.py:366
  5.2 67.7 %all-to-all-start = ((bf16[8,128,2048]{2,1,0:T(8,128)(2,1)}), bf16[8,128,2048]{2,1,0:T(8,128)(2,1)}, u32[]{:S(2)}, u32[]{:S(2)}) async-start(bf16[8,128,2048]{2,1,0:T(8,128)(2,1)} %spread.1), calls=%async_computation | async-start | bytes 8388608 | tf_op jit(solution)/shard_map/all_to_all | solution.py:383
  11.7 5.3 %copy-start.4 = (bf16[1792,512]{1,0:T(8,128)(2,1)}, bf16[1792,512]{1,0:T(8,128)(2,1)S(1)}, u32[]{:S(2)}) copy-start(bf16[1792,512]{1,0:T(8,128)(2,1)S(1)} %constant_dynamic-slice_fusion.1.refs_4_) | copy-start | bytes 5505028
  11.7 42.8 %collective-permute-start.1 = (bf16[1792,512]{1,0:T(8,128)(2,1)S(1)}, bf16[1792,512]{1,0:T(8,128)(2,1)}, u32[]{:S(2)}, u32[]{:S(2)}) collective-permute-start(bf16[1792,512]{1,0:T(8,128)(2,1)S(1)} %constant_dynamic-slice_fusion.1.refs_4_), channel_id=1, source_target_pairs={{0,8},{8,16},{16,24},{24,28},{28,20},{20,12},{12,4},{4,0},{1,9},{9... | collective-permute-start | bytes 5505032 | tf_op jit(solution)/shard_map/ppermute | solution.py:369
  14.1 42.9 %collective-permute-start.2 = (bf16[1792,512]{1,0:T(8,128)(2,1)S(1)}, bf16[1792,512]{1,0:T(8,128)(2,1)}, u32[]{:S(2)}, u32[]{:S(2)}) collective-permute-start(bf16[1792,512]{1,0:T(8,128)(2,1)S(1)} %constant_dynamic-slice_fusion.1.refs_4_), channel_id=1, source_target_pairs={{4,12},{12,20},{20,28},{28,24},{24,16},{16,8},{8,0},{0,4},{5,13},{... | collective-permute-start | bytes 5505032 | tf_op jit(solution)/shard_map/ppermute | solution.py:369
  17.0 76.3 %collective-permute-start.11 = (bf16[1792,512]{1,0:T(8,128)(2,1)}, bf16[1792,512]{1,0:T(8,128)(2,1)}, u32[]{:S(2)}, u32[]{:S(2)}) collective-permute-start(bf16[1792,512]{1,0:T(8,128)(2,1)} %constant_dynamic-slice_fusion.refs_7_), channel_id=1, source_target_pairs={{4,12},{12,20},{20,28},{28,24},{24,16},{16,8},{8,0},{0,4},{5,13},{... | collective-permute-start | bytes 5505032 | tf_op jit(solution)/shard_map/ppermute | solution.py:369
  54.5 44.2 %collective-permute-start.10 = (bf16[1792,512]{1,0:T(8,128)(2,1)}, bf16[1792,512]{1,0:T(8,128)(2,1)}, u32[]{:S(2)}, u32[]{:S(2)}) collective-permute-start(bf16[1792,512]{1,0:T(8,128)(2,1)} %constant_dynamic-slice_fusion.refs_7_), channel_id=1, source_target_pairs={{0,8},{8,16},{16,24},{24,28},{28,20},{20,12},{12,4},{4,0},{1,9},{9... | collective-permute-start | bytes 5505032 | tf_op jit(solution)/shard_map/ppermute | solution.py:369
  78.2 54.3 %collective-permute-start.5 = (bf16[1792,512]{1,0:T(8,128)(2,1)}, bf16[1792,512]{1,0:T(8,128)(2,1)S(1)}, u32[]{:S(2)}, u32[]{:S(2)}) collective-permute-start(bf16[1792,512]{1,0:T(8,128)(2,1)} %step.14), channel_id=1, source_target_pairs={{4,12},{12,20},{20,28},{28,24},{24,16},{16,8},{8,0},{0,4},{5,13},{... | collective-permute-start | bytes 5505032 | tf_op jit(solution)/shard_map/ppermute | solution.py:369
  84.9 54.2 %collective-permute-start.7 = (bf16[1792,512]{1,0:T(8,128)(2,1)}, bf16[1792,512]{1,0:T(8,128)(2,1)S(1)}, u32[]{:S(2)}, u32[]{:S(2)}) collective-permute-start(bf16[1792,512]{1,0:T(8,128)(2,1)} %step.16), channel_id=1, source_target_pairs={{0,8},{8,16},{16,24},{24,28},{28,20},{20,12},{12,4},{4,0},{1,9},{9... | collective-permute-start | bytes 5505032 | tf_op jit(solution)/shard_map/ppermute | solution.py:369
  85.6 140.8 %collective-permute-start = (bf16[1024,2048]{1,0:T(8,128)(2,1)}, bf16[1024,2048]{1,0:T(8,128)(2,1)}, u32[]{:S(2)}, u32[]{:S(2)}) collective-permute-start(bf16[1024,2048]{1,0:T(8,128)(2,1)} %bitcast.2.grad_ref.refs_0_.refs_1_), channel_id=1, source_target_pairs={{0,4},{4,0},{8,12},{12,8},{16,20},{20,16},{24,28},{28,24},{1,5},{5... | collective-permute-start | bytes 12582920 | tf_op jit(solution)/shard_map/ppermute | solution.py:366
  98.6 73.3 %collective-permute-start.12 = (bf16[1792,512]{1,0:T(8,128)(2,1)}, bf16[1792,512]{1,0:T(8,128)(2,1)}, u32[]{:S(2)}, u32[]{:S(2)}) collective-permute-start(bf16[1792,512]{1,0:T(8,128)(2,1)} %step.18), channel_id=1, source_target_pairs={{4,12},{12,20},{20,28},{28,24},{24,16},{16,8},{8,0},{0,4},{5,13},{... | collective-permute-start | bytes 5505032 | tf_op jit(solution)/shard_map/ppermute | solution.py:369
  105.3 71.9 %collective-permute-start.14 = (bf16[1792,512]{1,0:T(8,128)(2,1)}, bf16[1792,512]{1,0:T(8,128)(2,1)}, u32[]{:S(2)}, u32[]{:S(2)}) collective-permute-start(bf16[1792,512]{1,0:T(8,128)(2,1)} %step.20), channel_id=1, source_target_pairs={{0,8},{8,16},{16,24},{24,28},{28,20},{20,12},{12,4},{4,0},{1,9},{9... | collective-permute-start | bytes 5505032 | tf_op jit(solution)/shard_map/ppermute | solution.py:369
  132.5 1.2 copy-start.2
  139.1 72.2 %collective-permute-start.6 = (bf16[1792,512]{1,0:T(8,128)(2,1)}, bf16[1792,512]{1,0:T(8,128)(2,1)}, u32[]{:S(2)}, u32[]{:S(2)}) collective-permute-start(bf16[1792,512]{1,0:T(8,128)(2,1)} %step.15), channel_id=1, source_target_pairs={{4,12},{12,20},{20,28},{28,24},{24,16},{16,8},{8,0},{0,4},{5,13},{... | collective-permute-start | bytes 5505032 | tf_op jit(solution)/shard_map/ppermute | solution.py:369
  139.1 1.2 copy-start.3
  147.0 69.6 %collective-permute-start.8 = (bf16[1792,512]{1,0:T(8,128)(2,1)}, bf16[1792,512]{1,0:T(8,128)(2,1)}, u32[]{:S(2)}, u32[]{:S(2)}) collective-permute-start(bf16[1792,512]{1,0:T(8,128)(2,1)} %step.17), channel_id=1, source_target_pairs={{0,8},{8,16},{16,24},{24,28},{28,20},{20,12},{12,4},{4,0},{1,9},{9... | collective-permute-start | bytes 5505032 | tf_op jit(solution)/shard_map/ppermute | solution.py:369
  177.3 73.2 %collective-permute-start.13 = (bf16[1792,512]{1,0:T(8,128)(2,1)}, bf16[1792,512]{1,0:T(8,128)(2,1)S(1)}, u32[]{:S(2)}, u32[]{:S(2)}) collective-permute-start(bf16[1792,512]{1,0:T(8,128)(2,1)} %step.19), channel_id=1, source_target_pairs={{4,12},{12,20},{20,28},{28,24},{24,16},{16,8},{8,0},{0,4},{5,13},{... | collective-permute-start | bytes 5505032 | tf_op jit(solution)/shard_map/ppermute | solution.py:369
  184.0 72.7 %collective-permute-start.15 = (bf16[1792,512]{1,0:T(8,128)(2,1)}, bf16[1792,512]{1,0:T(8,128)(2,1)S(1)}, u32[]{:S(2)}, u32[]{:S(2)}) collective-permute-start(bf16[1792,512]{1,0:T(8,128)(2,1)} %step.21), channel_id=1, source_target_pairs={{0,8},{8,16},{16,24},{24,28},{28,20},{20,12},{12,4},{4,0},{1,9},{9... | collective-permute-start | bytes 5505032 | tf_op jit(solution)/shard_map/ppermute | solution.py:369
  216.6 81.3 %collective-permute-start.18 = (bf16[1792,512]{1,0:T(8,128)(2,1)}, bf16[1792,512]{1,0:T(8,128)(2,1)}, u32[]{:S(2)}, u32[]{:S(2)}) collective-permute-start(bf16[1792,512]{1,0:T(8,128)(2,1)} %step.24.refs_15_), channel_id=1, source_target_pairs={{4,12},{12,20},{20,28},{28,24},{24,16},{16,8},{8,0},{0,4},{5,13},{... | collective-permute-start | bytes 5505032 | tf_op jit(solution)/shard_map/ppermute | solution.py:369
  223.3 77.3 %collective-permute-start.17 = (bf16[1792,512]{1,0:T(8,128)(2,1)}, bf16[1792,512]{1,0:T(8,128)(2,1)}, u32[]{:S(2)}, u32[]{:S(2)}) collective-permute-start(bf16[1792,512]{1,0:T(8,128)(2,1)} %step.22.refs_13_), channel_id=1, source_target_pairs={{0,8},{8,16},{16,24},{24,28},{28,20},{20,12},{12,4},{4,0},{1,9},{9... | collective-permute-start | bytes 5505032 | tf_op jit(solution)/shard_map/ppermute | solution.py:369
  250.5 1.3 copy-start
  256.7 1.2 copy-start.1
  263.8 11.6 %copy-start.5 = (bf16[1344,512]{1,0:T(8,128)(2,1)S(1)}, bf16[1344,512]{1,0:T(8,128)(2,1)}, u32[]{:S(2)}) copy-start(bf16[1344,512]{1,0:T(8,128)(2,1)} %step.25.refs_16_) | copy-start | bytes 4128772
  263.8 12.1 %copy-start.6 = (bf16[1344,512]{1,0:T(8,128)(2,1)S(1)}, bf16[1344,512]{1,0:T(8,128)(2,1)}, u32[]{:S(2)}) copy-start(bf16[1344,512]{1,0:T(8,128)(2,1)} %step.23.refs_14_) | copy-start | bytes 4128772
  275.3 30.4 %collective-permute-start.16 = (bf16[512,1792]{1,0:T(8,128)(2,1)}, bf16[512,1792]{1,0:T(8,128)(2,1)}, u32[]{:S(2)}, u32[]{:S(2)}) collective-permute-start(bf16[512,1792]{1,0:T(8,128)(2,1)} %get-tuple-element.20), channel_id=1, source_target_pairs={{0,4},{4,0},{8,12},{12,8},{16,20},{20,16},{24,28},{28,24},{1,5},{5... | collective-permute-start | bytes 5505032 | tf_op jit(solution)/shard_map/ppermute | solution.py:366
  275.4 44.0 %collective-permute-start.20 = (bf16[1344,512]{1,0:T(8,128)(2,1)S(1)}, bf16[1344,512]{1,0:T(8,128)(2,1)}, u32[]{:S(2)}, u32[]{:S(2)}) collective-permute-start(bf16[1344,512]{1,0:T(8,128)(2,1)S(1)} %copy-done.5), channel_id=1, source_target_pairs={{4,12},{12,20},{20,28},{28,24},{24,16},{16,8},{8,0},{0,4},{5,13},{... | collective-permute-start | bytes 4128776 | tf_op jit(solution)/shard_map/ppermute | solution.py:369
  275.9 47.9 %collective-permute-start.19 = (bf16[1344,512]{1,0:T(8,128)(2,1)S(1)}, bf16[1344,512]{1,0:T(8,128)(2,1)}, u32[]{:S(2)}, u32[]{:S(2)}) collective-permute-start(bf16[1344,512]{1,0:T(8,128)(2,1)S(1)} %copy-done.6), channel_id=1, source_target_pairs={{0,8},{8,16},{16,24},{24,28},{28,20},{20,12},{12,4},{4,0},{1,9},{9... | collective-permute-start | bytes 4128776 | tf_op jit(solution)/shard_map/ppermute | solution.py:369
  298.0 31.4 %collective-permute-start.21 = (bf16[448,512]{1,0:T(8,128)(2,1)}, bf16[448,512]{1,0:T(8,128)(2,1)S(1)}, u32[]{:S(2)}, u32[]{:S(2)}) collective-permute-start(bf16[448,512]{1,0:T(8,128)(2,1)} %step.26), channel_id=1, source_target_pairs={{0,8},{8,16},{16,24},{24,28},{28,20},{20,12},{12,4},{4,0},{1,9},{9... | collective-permute-start | bytes 1376264 | tf_op jit(solution)/shard_map/ppermute | solution.py:369
  300.6 28.8 %collective-permute-start.22 = (bf16[448,512]{1,0:T(8,128)(2,1)}, bf16[448,512]{1,0:T(8,128)(2,1)}, u32[]{:S(2)}, u32[]{:S(2)}) collective-permute-start(bf16[448,512]{1,0:T(8,128)(2,1)} %step.27), channel_id=1, source_target_pairs={{4,12},{12,20},{20,28},{28,24},{24,16},{16,8},{8,0},{0,4},{5,13},{... | collective-permute-start | bytes 1376264 | tf_op jit(solution)/shard_map/ppermute | solution.py:369
